TPU v7x, 256 devices: a whole 4x4x8 slice. The times are simulated.
256 devices in a mesh: half: 2 (over x_lo), panel: 4 (over x_hi, core), dom: 32 (over z, y).
Axes of the slice: x: 4 (x_hi: 2, x_lo: 2; x = x_hi * 2 + x_lo), y: 4, z: 8, core: 2. Of those that a mesh axis runs over, the one named last changes fastest.
Arguments:
- images: bfloat16 [4096, 8192], P(('half', 'dom')), parts along dimension 0, may hold values from -128 to 128
- shift_index: int32 [4096, 9], P(('half', 'dom')), parts along dimension 0, may hold values from 0 to 48, as said below
- references: bfloat16 [1024, 8192], P(('half', 'panel', 'dom')), parts along dimension 0, may hold values from -0.6 to 0.6
- slot_blocks: int32 [1024, 8], P(('half', 'panel')), parts along dimension 0, may hold values from 0 to 255
Outputs:
- volume: float32 [512, 1024], P(('half', 'panel', 'dom')), parts along dimension 0
- log_evidence: float32 [4096], P(('half', 'dom')), parts along dimension 0
There are 2 independent parts, one for each index of `half`. A program takes and returns all parts, laid end to end along the dimension named above; each array names one. Nothing has to cross between parts.
Inputs may be any that keep to these rules, and one draw needn't show every extreme that they name: `shift_index`: each row names 9 different offsets.
All inputs are finite; a program needn't handle non-finite values.
Results may differ from a plain program's by a relative error of at most 0.0048.
Values may be sent and summed in bfloat16 or wider, within the bound.
No kernel may reach another device: no remote copies, remote signals or barrier semaphores. Data moves between devices by JAX's collectives and lax.ppermute only.
A program may use at most 128 MiB of HBM per device.

v0:
```python
import math

import jax
import jax.numpy as jnp
from jax import lax
from jax.sharding import PartitionSpec as P

PIX = 64
SHIFTS = 9
GRID = 7
VB_DEV = 2


offset_sigma = 2.0


def offsets(shift_index):
    shift_row = (shift_index // GRID - GRID // 2).astype(jnp.float32)
    shift_col = (shift_index % GRID - GRID // 2).astype(jnp.float32)
    return (shift_row, shift_col)


def penalty(shift_index):
    shift_row, shift_col = offsets(shift_index)
    return (shift_row * shift_row + shift_col * shift_col) * (0.5 / (offset_sigma * offset_sigma))


def phase_table():
    shift_row, shift_col = offsets(jnp.arange(GRID * GRID, dtype=jnp.int32))
    frequency = jnp.arange(PIX, dtype=jnp.float32) - PIX // 2
    phase_angle = (
        -2.0
        * math.pi
        / PIX
        * (
            shift_row[:, None, None] * frequency[None, :, None]
            + shift_col[:, None, None] * frequency[None, None, :]
        )
    )
    return (jnp.cos(phase_angle), jnp.sin(phase_angle))


def shift_images(images, shift_index, cos_table, sin_table):
    row_count = images.shape[0]
    cosine = cos_table[shift_index]
    sine_part = sin_table[shift_index]
    picture = images.astype(jnp.float32).reshape(row_count, 1, PIX, 2, PIX)
    real_part = picture[:, :, :, 0, :]
    imag_part = picture[:, :, :, 1, :]
    out_real = real_part * cosine - imag_part * sine_part
    out_imag = real_part * sine_part + imag_part * cosine
    return (
        jnp.stack([out_real, out_imag], axis=3)
        .reshape(row_count * SHIFTS, 2 * PIX * PIX)
        .astype(jnp.bfloat16)
    )


def score_rows(images, shift_index, gathered, block_size):
    cos_table, sin_table = phase_table()
    row_count = images.shape[0]
    block_count = row_count // block_size
    ref_norms = jnp.sum(jnp.square(gathered.astype(jnp.float32)), axis=1)
    image_blocks = images.reshape(block_count, block_size, images.shape[1])
    index_blocks = shift_index.reshape(block_count, block_size, SHIFTS)

    def one_block(blocks):
        image_block, index_block = blocks
        moved = shift_images(image_block, index_block, cos_table, sin_table)
        correlation = lax.dot_general(
            moved, gathered, (((1,), (1,)), ((), ())), preferred_element_type=jnp.float32
        )
        return (correlation - 0.5 * ref_norms[None, :] - penalty(index_block).reshape(-1, 1), moved)

    scores, moved_blocks = lax.map(one_block, (image_blocks, index_blocks))
    return (scores.reshape(row_count, SHIFTS * gathered.shape[0]), moved_blocks)


def back_project(moved_blocks, weights, slot_table, group_count, block_total):
    block_count = moved_blocks.shape[0]
    block_rows = moved_blocks.shape[1]
    row_width = moved_blocks.shape[2]
    orient_count = slot_table.shape[0]
    segments = slot_table.shape[1]
    block_len = row_width // segments
    group_rows = orient_count // group_count
    weight_blocks = weights.reshape(block_count, block_rows, orient_count)

    def one_group(group_index, volume):

        def add_block(running, inputs):
            moved, weight_block = inputs
            return (
                running
                + lax.dot_general(
                    weight_block,
                    moved,
                    (((0,), (0,)), ((), ())),
                    preferred_element_type=jnp.float32,
                ),
                None,
            )

        slab_sums, _ = lax.scan(
            add_block,
            jnp.zeros((group_rows, row_width), jnp.float32),
            (moved_blocks, weight_blocks),
        )
        return volume.at[slot_table.reshape(-1)].add(
            slab_sums.reshape(group_rows * segments, block_len)
        )

    return lax.fori_loop(
        0, group_count, one_group, jnp.zeros((block_total, block_len), jnp.float32)
    )


def shards(images, shift_index, references, slot_blocks):
    n_panel = lax.axis_size("panel")
    n_dom = lax.axis_size("dom")
    part_dev = images.shape[0]
    segments = slot_blocks.shape[1]
    block_total = VB_DEV * n_panel * n_dom
    volume_scale = (part_dev * n_dom * segments / block_total) ** (-0.5)
    gathered = lax.all_gather(references, "dom", axis=0, tiled=True)
    block_size = min(64, part_dev)
    scores, moved_blocks = score_rows(images, shift_index, gathered, block_size)
    row_top = lax.pmax(jnp.max(scores, axis=1), "panel")
    raised = jnp.exp(scores - row_top[:, None])
    row_total = lax.psum(jnp.sum(raised, axis=1), "panel")
    weights = (raised / row_total[:, None]).astype(jnp.bfloat16)
    log_evidence = row_top + jnp.log(row_total)
    partial_value = back_project(moved_blocks, weights, slot_blocks, 1, block_total)
    summed = lax.psum_scatter(partial_value, ("panel", "dom"), scatter_dimension=0, tiled=True)
    return (summed * volume_scale, log_evidence)


def solution(mesh):
    in_specs = (
        P(("half", "dom"), None),
        P(("half", "dom"), None),
        P(("half", "panel", "dom"), None),
        P(("half", "panel"), None),
    )
    out_specs = (P(("half", "panel", "dom"), None), P(("half", "dom")))
    return jax.shard_map(shards, mesh=mesh, in_specs=in_specs, out_specs=out_specs, check_vma=False)
```

profile of v0, /device:TPU:32, one launch (start us, length us, event | category | flops | bytes accessed | tf_op | source)
XLA Modules:
  0.0 1431.0 jit_solution(7021139271280164268)
XLA Ops:
  7.2 0.7 all-gather.3.cloned.1.call-update
  8.0 0.7 compare_select_fusion.1
  9.0 5.7 fusion
  14.7 7.9 gather_fusion
  22.6 7.7 gather_fusion.1
  30.3 4.4 reshape.214
  34.8 7.9 fusion.22
  42.6 17.8 %subtract_convert_fusion = (bf16[64,9,64,1,64]{4,2,3,1,0:T(8,128)(2,1)S(1)}, bf16[64,9,64,1,64]{4,2,3,1,0:T(8,128)(2,1)}) fusion(f32[64,9,64,1,64]{4,2,3,1,0:T(8,128)} %bitcast.15, f32[64,9,64,1,64]{4,2,3,1,0:T(8,128)} %bitcast.14, f32[64,64,64]{2,1,0:T(8,128)S(1)} %bitcast.17, f32[64,64,64]{2,1,0:T(8,128)S(1)} %bitcast.16), kind=kLoop, calls=%fused_computation.5 | loop fusion | flops 18874368 | bytes 30408704 | tf_op jit(solution)/shard_map/convert.1
  60.5 8.4 pad_maximum_fusion
  68.8 17.8 %copy.21 = bf16[64,9,64,2,64]{4,3,2,1,0:T(2,128)(2,1)} copy(bf16[64,9,64,2,64]{4,2,3,1,0:T(8,128)(2,1)S(1)} %pad_maximum_fusion) | data formatting | bytes 18874368 | tf_op jit(solution)/shard_map/while/body/eval_jaxpr/stack | solution.py:53
  86.6 25.0 %convert_element_type.56 = bf16[576,8192]{1,0:T(8,128)(2,1)} reshape(bf16[64,9,64,2,64]{4,3,2,1,0:T(2,128)(2,1)} %copy.21) | data formatting | bytes 18874368 | tf_op jit(solution)/shard_map/while/body/eval_jaxpr/convert_element_type | solution.py:55
  112.1 2.8 reshape.246
  114.8 0.5 multiply_reduce_fusion
  115.3 6.4 fusion.23
  122.0 9.9 pmax.7
  132.2 0.3 fusion.5
  132.7 7.4 psum.7
  140.3 7.7 fusion.6
  147.9 5.0 reshape.235
  152.9 11.3 scatter_custom_fusion
  164.3 0.6 dynamic-slice.3
  165.5 0.5 log_add_fusion
  166.0 1256.8 %all-reduce.3.cloned.1.call-done = f32[256,1024]{1,0:T(8,128)} async-done(((f32[256,1024]{1,0:T(8,128)}), f32[256,1024]{1,0:T(8,128)}) %all-reduce.3.cloned.1.call-update) | async-done | bytes 1048592
  1422.8 1.4 dynamic-slice_multiply_fusion
  (33 shorter events, 1.8 us)
Async XLA Ops:
  7.2 104.9 %all-gather.3.cloned.1.call-start = ((), (), s32[]{:S(2)}) async-start(), calls=%async_computation | async-start | bytes 2162688 | tf_op jit(solution)/shard_map/all_gather | solution.py:125
  7.9 1414.9 %all-reduce.3.cloned.1.call-start = ((), (), s32[]{:S(2)}) async-start(), calls=%async_computation.1 | async-start | bytes 2097152
  22.6 7.7 copy-start
  86.6 25.0 %copy-start.1 = (s32[64,9]{0,1:T(8,128)S(1)}, s32[64,9]{0,1:T(8,128)}, u32[]{:S(2)}) copy-start(s32[64,9]{0,1:T(8,128)} %param.5) | copy-start | bytes 6916
  86.6 25.2 %copy-start.2 = (s32[128,8]{0,1:T(8,128)S(1)}, s32[128,8]{0,1:T(8,128)}, u32[]{:S(2)}) copy-start(s32[128,8]{0,1:T(8,128)} %param.7) | copy-start | bytes 12292
  147.9 16.3 %copy-start.3 = (u32[256]{0:T(256)S(1)}, u32[256]{0:T(256)}, u32[]{:S(2)}) copy-start(u32[256]{0:T(256)} %constant.101) | copy-start | bytes 3076
Sparse Core Ops, SparseCore 0:
  10.6 79.7 all-gather.2
  164.4 1258.4 all-reduce.2
where the time goes:
time: 1440 us; the launch traced here: 1430 us
  waiting for transfers between devices  1260 us (88%)
  local copies, waits for them, and re-layouts  80.3 us (6%)
  other arithmetic  46.9 us (3%)
  blocking collectives  17.3 us (1%)
  between operations  14.8 us (1%)
    unnamed x3, waiting for transfers between devices  1260 us
  transfers between devices with their start and end apart: 2, of which 1 were waited for; matrix products, arithmetic and copies ran while one was open for 7% of the time, Pallas kernels for 0%

commit v1 on v0

v1 whole, which is shorter than its diff:
```python
import functools
import math

import jax
import jax.numpy as jnp
import numpy as np
from jax import lax
from jax.experimental import pallas as pl
from jax.experimental.pallas import tpu as pltpu
from jax.sharding import Mesh
from jax.sharding import PartitionSpec as P

PIX = 64
SHIFTS = 9
GRID = 7
OFFS = GRID * GRID
KPAD = 160
Z, Y = 8, 4
SEG = 8
BLK = 1024
VB = 256
OFFSET_SIGMA = 2.0
BF16 = jnp.bfloat16
F32 = jnp.float32


def dom_of(z, y):
    return (z % Z) * Y + y % Y


COSETS = [[dom_of((c - 2 * (j // 2)) % 4 + 4 * (j % 2), j // 2) for j in range(8)] for c in range(4)]


def receive_from(dz, dy):
    return [(dom_of(z + dz, y + dy), dom_of(z, y)) for z in range(Z) for y in range(Y)]


def phase_parts():
    offset = np.arange(OFFS)
    a, b = offset // GRID - GRID // 2, offset % GRID - GRID // 2
    f = np.arange(PIX) - PIX // 2
    turns = (f[:, None, None] * a[None, :, None] + f[None, None, :] * b[None, :, None]) % PIX
    angle = -2.0 * math.pi / PIX * turns
    cos, sin = np.cos(angle), np.sin(angle)
    table = np.concatenate([cos, cos, -sin, sin], axis=2).astype(np.float32)
    high = table.astype(BF16)
    rest = table - high.astype(np.float32)
    mid = rest.astype(BF16)
    low = (rest - mid.astype(np.float32)).astype(BF16)
    pad = np.zeros((PIX, KPAD - 3 * OFFS, 4 * PIX), BF16)
    return np.concatenate([high, mid, low, pad], axis=1)


def shift_kernel(index_ref, image_ref, table_ref, out_ref, pen_ref, hot_ref):
    rows = image_ref.shape[0]

    @pl.when(pl.program_id(0) == 0)
    def _():
        k = lax.broadcasted_iota(jnp.int32, (KPAD, rows), 0)
        offset = jnp.where(k < 3 * OFFS, k % OFFS, -1)
        hot_t = jnp.concatenate(
            [jnp.where(offset == index_ref[t : t + 1, :], 1.0, 0.0) for t in range(SHIFTS)], axis=1
        )
        hot_ref[...] = hot_t.T.astype(BF16)
        k = lax.broadcasted_iota(jnp.int32, (8, KPAD), 1)
        a, b = k // GRID - GRID // 2, k % GRID - GRID // 2
        cost = (a * a + b * b).astype(F32) * (0.5 / (OFFSET_SIGMA * OFFSET_SIGMA))
        pen_ref[...] = jnp.dot(
            jnp.where(k < OFFS, cost, 0.0).astype(BF16), hot_t.astype(BF16), preferred_element_type=F32
        )

    for u in range(table_ref.shape[0]):
        phase = jnp.dot(hot_ref[...], table_ref[u], preferred_element_type=F32)
        cols = slice(u * 2 * PIX, (u + 1) * 2 * PIX)
        x = image_ref[:, cols].astype(F32)
        swapped = pltpu.roll(x, PIX, 1)
        for t in range(SHIFTS):
            part = phase[t * rows : (t + 1) * rows]
            out_ref[t * rows : (t + 1) * rows, cols] = (
                x * part[:, : 2 * PIX] + swapped * part[:, 2 * PIX :]
            ).astype(BF16)


def shift_images(images, index_t, table):
    rows, width = images.shape
    steps = 8
    total = rows * SHIFTS
    return pl.pallas_call(
        shift_kernel,
        grid=(steps,),
        in_specs=[
            pl.BlockSpec((SHIFTS, rows), lambda s: (0, 0)),
            pl.BlockSpec((rows, width // steps), lambda s: (0, s)),
            pl.BlockSpec((PIX // steps, KPAD, 4 * PIX), lambda s: (s, 0, 0)),
        ],
        out_specs=[
            pl.BlockSpec((total, width // steps), lambda s: (0, s)),
            pl.BlockSpec((8, total), lambda s: (0, 0)),
        ],
        out_shape=[
            jax.ShapeDtypeStruct((total, width), BF16),
            jax.ShapeDtypeStruct((8, total), F32),
        ],
        scratch_shapes=[pltpu.VMEM((total, KPAD), BF16)],
        compiler_params=pltpu.CompilerParams(vmem_limit_bytes=24 << 20),
        cost_estimate=pl.CostEstimate(flops=5 * 10**9, bytes_accessed=16 << 20, transcendentals=0),
        name="shift",
    )(index_t, images, table)


def tile_shifts(x):
    return jnp.concatenate([x] * SHIFTS, axis=1)


def over_shifts(op, x, rows):
    return functools.reduce(op, [x[:, t * rows : (t + 1) * rows] for t in range(SHIFTS)])


def score_kernel(own, up, down, right, left, moved, pen, raised, stats, acc, norm):
    step = pl.program_id(0)
    refs = jnp.concatenate([own[...], up[...], down[...], right[...], left[...]], axis=0)
    part = lax.dot_general(refs, moved[...], (((1,), (1,)), ((), ())), preferred_element_type=F32)
    wide = refs.astype(F32)
    square = jnp.sum(wide * wide, axis=1, keepdims=True)

    @pl.when(step == 0)
    def _():
        acc[...] = part
        norm[...] = square

    @pl.when(step > 0)
    def _():
        acc[...] += part
        norm[...] += square

    @pl.when(step == pl.num_programs(0) - 1)
    def _():
        rows = acc.shape[1] // SHIFTS
        scores = acc[...] - 0.5 * norm[...] - pen[0:1, :]
        top = over_shifts(jnp.maximum, jnp.max(scores, axis=0, keepdims=True), rows)
        value = jnp.exp(scores - tile_shifts(top))
        raised[...] = value
        total = over_shifts(jnp.add, jnp.sum(value, axis=0, keepdims=True), rows)
        stats[...] = jnp.concatenate([top, total], axis=0)


def score(pieces, moved, pen):
    total, width = moved.shape
    steps = 8
    count = sum(p.shape[0] for p in pieces)
    return pl.pallas_call(
        score_kernel,
        grid=(steps,),
        in_specs=[pl.BlockSpec((p.shape[0], width // steps), lambda s: (0, s)) for p in pieces]
        + [
            pl.BlockSpec((total, width // steps), lambda s: (0, s)),
            pl.BlockSpec((8, total), lambda s: (0, 0)),
        ],
        out_specs=[
            pl.BlockSpec((count, total), lambda s: (0, 0)),
            pl.BlockSpec((2, total // SHIFTS), lambda s: (0, 0)),
        ],
        out_shape=[
            jax.ShapeDtypeStruct((count, total), F32),
            jax.ShapeDtypeStruct((2, total // SHIFTS), F32),
        ],
        scratch_shapes=[pltpu.VMEM((count, total), F32), pltpu.VMEM((count, 1), F32)],
        compiler_params=pltpu.CompilerParams(vmem_limit_bytes=24 << 20),
        cost_estimate=pl.CostEstimate(flops=2 * 10**9, bytes_accessed=12 << 20, transcendentals=1 << 17),
        name="score",
    )(*pieces, moved, pen)


def insert_kernel(scale, raised, s0, s1, s2, s3, slot_ref, moved, mine, other, evidence, acc, weight, slots):
    step = pl.program_id(0)
    count = raised.shape[0]

    @pl.when(step == 0)
    def _():
        tops = [s[0:1, :] for s in (s0, s1, s2, s3)]
        sums = [s[1:2, :] for s in (s0, s1, s2, s3)]
        top = functools.reduce(jnp.maximum, tops)
        total = functools.reduce(jnp.add, [b * jnp.exp(a - top) for a, b in zip(tops, sums)])
        evidence[...] = top + jnp.log(total)
        factor = jnp.exp(tops[0] - top) / total
        weight[...] = (raised[...] * tile_shifts(factor)).astype(BF16)
        dom = lax.axis_index("dom")
        coset = (dom // Y + 2 * (dom % Y)) % 4
        q = lax.broadcasted_iota(jnp.int32, (count, count), 1) // 4
        group = q // 8
        j = q % 8
        ahead = jnp.where(group == 1, 1, jnp.where(group == 2, 3, jnp.where(group == 3, 2, 0)))
        c = (coset + ahead) % 4
        y = j // 2
        z = (c + 4 - 2 * (y % 2)) % 4 + 4 * (j % 2)
        source = (z * Y + y) * 4 + lax.broadcasted_iota(jnp.int32, (count, count), 1) % 4
        order = jnp.where(lax.broadcasted_iota(jnp.int32, (count, count), 0) == source, 1.0, 0.0)
        slots[...] = jnp.dot(
            slot_ref[...].astype(F32).astype(BF16), order.astype(BF16), preferred_element_type=F32
        ).astype(jnp.int32)

    core = lax.axis_index("core")
    m = lax.broadcasted_iota(jnp.int32, (VB, count), 0)
    half = m % (VB // 2)
    owner = jnp.where(m < VB // 2, core, 1 - core)
    block = half // (VB // 4) * (VB // 2) + owner * (VB // 4) + half % (VB // 4)
    hot = jnp.where(block == slots[pl.ds(step, 1), :], 1.0, 0.0).astype(BF16)
    blocked = jnp.dot(hot, weight[...], preferred_element_type=F32).astype(BF16)
    part = jnp.dot(blocked, moved[...], preferred_element_type=F32)

    @pl.when(step == 0)
    def _():
        acc[...] = part

    @pl.when(step > 0)
    def _():
        acc[...] += part

    @pl.when(step == pl.num_programs(0) - 1)
    def _():
        mine[...] = acc[: VB // 2] * scale
        other[...] = (acc[VB // 2 :] * scale).astype(BF16)


def insert(raised, stats, slots_t, moved, scale):
    count, total = raised.shape
    rows = total // SHIFTS
    return pl.pallas_call(
        functools.partial(insert_kernel, scale),
        grid=(SEG,),
        in_specs=[pl.BlockSpec((count, total), lambda s: (0, 0))]
        + [pl.BlockSpec((2, rows), lambda s: (0, 0))] * 4
        + [
            pl.BlockSpec((SEG, count), lambda s: (0, 0)),
            pl.BlockSpec((total, BLK), lambda s: (0, s)),
        ],
        out_specs=[
            pl.BlockSpec((VB // 2, BLK), lambda s: (0, 0)),
            pl.BlockSpec((VB // 2, BLK), lambda s: (0, 0)),
            pl.BlockSpec((1, rows), lambda s: (0, 0)),
        ],
        out_shape=[
            jax.ShapeDtypeStruct((VB // 2, BLK), F32),
            jax.ShapeDtypeStruct((VB // 2, BLK), BF16),
            jax.ShapeDtypeStruct((1, rows), F32),
        ],
        scratch_shapes=[
            pltpu.VMEM((VB, BLK), F32),
            pltpu.VMEM((count, total), BF16),
            pltpu.VMEM((SEG, count), jnp.int32),
        ],
        compiler_params=pltpu.CompilerParams(vmem_limit_bytes=24 << 20),
        cost_estimate=pl.CostEstimate(flops=3 * 10**9, bytes_accessed=12 << 20, transcendentals=0),
        name="insert",
    )(raised, *stats, slots_t, moved)


def shards(images, shift_index, references, slot_blocks):
    rows = images.shape[0]
    scale = (rows * Z * Y * SEG / VB) ** (-0.5)
    copies = jnp.broadcast_to(references[None], (8, *references.shape))
    own = lax.all_to_all(copies, "dom", 0, 0, axis_index_groups=COSETS, tiled=True)
    own = own.reshape(8 * references.shape[0], references.shape[1])
    near = own.shape[0] // 2
    up = lax.ppermute(own, "dom", receive_from(1, 0))
    down = lax.ppermute(own, "dom", receive_from(-1, 0))
    right = lax.ppermute(own[:near], "dom", receive_from(0, 1))
    left = lax.ppermute(own[near:], "dom", receive_from(0, -1))
    moved, pen = shift_images(images, shift_index.T, jnp.asarray(phase_parts()))
    raised, stats = score((own, up, down, right, left), moved, pen)
    swap = [(0, 1), (1, 0)]
    everyone = [
        stats,
        lax.ppermute(stats, "core", swap),
        lax.ppermute(stats, "px", swap),
        lax.ppermute(stats, ("px", "core"), [(i, 3 - i) for i in range(4)]),
    ]
    mine, other, evidence = insert(raised, everyone, slot_blocks.T, moved, scale)
    paired = mine + lax.ppermute(other, "core", swap).astype(F32)
    sent = paired.astype(BF16).reshape(2 * Z * Y, VB // (4 * Z * Y), BLK)
    arrived = lax.all_to_all(sent, ("px", "dom"), 0, 0, tiled=True)
    return (jnp.sum(arrived.astype(F32), axis=0), evidence.reshape(rows))


def solution(mesh):
    split = Mesh(mesh.devices.reshape(2, 2, 2, Z * Y), ("half", "px", "core", "dom"))
    in_specs = (
        P(("half", "dom"), None),
        P(("half", "dom"), None),
        P(("half", "px", "core", "dom"), None),
        P(("half", "px", "core"), None),
    )
    out_specs = (P(("half", "px", "core", "dom"), None), P(("half", "dom")))
    return jax.shard_map(shards, mesh=split, in_specs=in_specs, out_specs=out_specs, check_vma=False)
```

time: 1440 us -> 93.6 us (0.07)
  waiting for transfers between devices: 1260 us -> 2.98 us
  local copies, waits for them, and re-layouts: 80.3 us -> 5.92 us
  other arithmetic: 46.9 us -> 0.89 us
  blocking collectives: 17.3 us -> 52.3 us
  Pallas kernels: 0 us -> 20.9 us
    unnamed x3 -> x0, waiting for transfers between devices: 1260 us -> none
    all_to_all x0 -> x2, blocking collectives: none -> 52.3 us  [the longest x1 28.8 us: shards(): lax.all_to_all(copies, 'dom', 0, 0, axis_index_groups=COSETS, tiled=True)]
    convert_element_type x2 -> x0, local copies, waits for them, and re-layouts: 29.4 us -> none  [the longest x1 25 us: shift_images(): return jnp.stack([out_real, out_imag], axis=3).reshape(row_count * SHIFTS...]
    another operation x2 -> x0, other arithmetic: 26.2 us -> none
    pallas_call x0 -> x3, Pallas kernels: none -> 20.9 us  [the longest x1 7.76 us: insert(): pl.pallas_call(functools.partial(insert_kernel, scale), grid=(SEG,), in_s...]
    another operation x1 -> x0, local copies, waits for them, and re-layouts: 17.8 us -> none  [shift_images(): jnp.stack([out_real, out_imag], axis=3)]
    gather x2 -> x0, local copies, waits for them, and re-layouts: 15.6 us -> none  [the longest x1 7.91 us: shift_images(): cosine = cos_table[shift_index]]
  transfers between devices with their start and end apart: 2 -> 8, of which waited for: 1 -> 3; matrix products, arithmetic and copies ran while one was open for 7% -> 0% of each run, Pallas kernels for 0% -> 8%
where the time goes in v1:
time: 93.6 us; the launch traced here: 93.2 us
  blocking collectives  52.3 us (56%)
  Pallas kernels  20.9 us (22%)
  starting transfers between devices  9.52 us (10%)
  local copies, waits for them, and re-layouts  5.92 us (6%)
  waiting for transfers between devices  2.98 us (3%)
    all_to_all x1, blocking collectives, shards(): lax.all_to_all(copies, 'dom', 0, 0, axis_index_groups=COSETS, tiled=True)  28.8 us
    all_to_all x1, blocking collectives, shards(): arrived = lax.all_to_all(sent, ('px', 'dom'), 0, 0, tiled=True)  23.5 us
    pallas_call x1, Pallas kernels, insert(): pl.pallas_call(functools.partial(insert_kernel, scale), grid=(SEG,), in_s...  7.76 us
    pallas_call x1, Pallas kernels, shift_images(): pl.pallas_call(shift_kernel, grid=(steps,), in_specs=[pl.BlockSpec((SHIFT...  7.25 us
    pallas_call x1, Pallas kernels, score(): pl.pallas_call(score_kernel, grid=(steps,), in_specs=[pl.BlockSpec((p.sha...  5.89 us
    unnamed x8, local copies, waits for them, and re-layouts  4.41 us
    ppermute x1, starting transfers between devices, shards(): lax.ppermute(stats, 'px', swap)  3.11 us
    ppermute x1, starting transfers between devices, shards(): paired = mine + lax.ppermute(other, 'core', swap).astype(F32)  1.89 us
  transfers between devices with their start and end apart: 8, of which 3 were waited for; matrix products, arithmetic and copies ran while one was open for 0% of the time, Pallas kernels for 8%

profile of v1, /device:TPU:32, one launch (start us, length us, event | category | flops | bytes accessed | tf_op | source)
XLA Modules:
  0.0 93.2 jit_solution(8832221611079453563)
XLA Ops:
  0.6 1.0 %broadcast_in_dim.2 = bf16[8,4,8192]{2,1,0:T(4,128)(2,1)S(1)} broadcast(bf16[4,8192]{1,0:T(4,128)(2,1)} %param.7), dimensions={1,2} | broadcast | bytes 589824 | tf_op jit(solution)/shard_map/broadcast_in_dim | solution.py:261
  1.6 28.8 %all_to_all.10 = bf16[8,4,8192]{2,1,0:T(4,128)(2,1)S(1)} all-to-all(bf16[8,4,8192]{2,1,0:T(4,128)(2,1)S(1)} %broadcast_in_dim.2), channel_id=1, replica_groups={{0,16,9,25,2,18,11,27},{4,20,13,29,6,22,15,31},{8,24,1,17,10,26,3,19},{..., dimensions={0} | all-to-all | bytes 1048576 | tf_op jit(solution)/shard_map/all_to_all | solution.py:262
  30.4 0.1 reshape.16.own
  30.5 1.2 %collective-permute-start.1 = (bf16[32,8192]{1,0:T(8,128)(2,1)S(1)}, bf16[32,8192]{1,0:T(8,128)(2,1)S(1)}, u32[]{:S(2)}, u32[]{:S(2)}) collective-permute-start(bf16[32,8192]{1,0:T(8,128)(2,1)S(1)} %reshape.16.own), channel_id=1, source_target_pairs={{28,0},{29,1},{30,2},{31,3},{0,4},{1,5},{2,6},{3,7},{4,8},{5,9},{6... | collective-permute-start | bytes 1572872 | tf_op jit(solution)/shard_map/ppermute | solution.py:266
  31.7 0.9 %collective-permute-start = (bf16[32,8192]{1,0:T(8,128)(2,1)S(1)}, bf16[32,8192]{1,0:T(8,128)(2,1)S(1)}, u32[]{:S(2)}, u32[]{:S(2)}) collective-permute-start(bf16[32,8192]{1,0:T(8,128)(2,1)S(1)} %reshape.16.own), channel_id=1, source_target_pairs={{4,0},{5,1},{6,2},{7,3},{8,4},{9,5},{10,6},{11,7},{12,8},{13,9},{1... | collective-permute-start | bytes 1572872 | tf_op jit(solution)/shard_map/ppermute | solution.py:265
  32.6 0.2 fusion
  33.0 0.4 collective-permute-start.2
  33.4 1.7 %collective-permute-start.3 = (bf16[16,8192]{1,0:T(8,128)(2,1)S(1)}, bf16[16,8192]{1,0:T(8,128)(2,1)S(1)}, u32[]{:S(2)}, u32[]{:S(2)}) collective-permute-start(bf16[16,8192]{1,0:T(8,128)(2,1)S(1)} %slice.15), channel_id=1, source_target_pairs={{3,0},{0,1},{1,2},{2,3},{7,4},{4,5},{5,6},{6,7},{11,8},{8,9},{9,10... | collective-permute-start | bytes 786440 | tf_op jit(solution)/shard_map/ppermute | solution.py:268
  35.1 1.2 %copy-done = bf16[64,8192]{1,0:T(8,128)(2,1)S(1)} copy-done((bf16[64,8192]{1,0:T(8,128)(2,1)S(1)}, bf16[64,8192]{1,0:T(8,128)(2,1)}, u32[]{:S(2)}) %copy-start) | copy-done | bytes 1048600
  36.3 0.7 copy-done.1
  37.0 2.5 %copy-done.3 = bf16[64,160,256]{2,1,0:T(8,128)(2,1)S(1)} copy-done((bf16[64,160,256]{2,1,0:T(8,128)(2,1)S(1)}, bf16[64,160,256]{2,1,0:T(8,128)(2,1)}, u32[]{:S(2)}) %copy-start.3) | copy-done | bytes 5242904
  39.5 7.3 %shift.1 = (bf16[576,8192]{1,0:T(8,128)(2,1)S(1)}, f32[8,576]{1,0:T(8,128)S(1)}) custom-call(s32[9,64]{1,0:T(8,128)S(1)} %bitcast.3, bf16[64,8192]{1,0:T(8,128)(2,1)S(1)} %copy-done, bf16[64,160,256]{2,1,0:T(8,128)(2,1)S(1)} %copy-done.3), custom_call_target="tpu_custom_call" | custom-call | flops 5000000000 | bytes 16777216 | tf_op jit(solution)/shard_map/shift/pallas_call | solution.py:88
  46.8 5.9 %score.1 = (f32[128,576]{1,0:T(8,128)S(1)}, f32[2,64]{1,0:T(2,128)S(1)}) custom-call(bf16[32,8192]{1,0:T(8,128)(2,1)S(1)} %reshape.16.own, bf16[32,8192]{1,0:T(8,128)(2,1)S(1)} %collective-permute-done.up, bf16[32,8192]{1,0:T(8,128)(2,1)S(1)} %collective-permute-done.1.down, bf16[16,8192]{1,0:T(8,128)(2,1)S(1)} %collective-permute-done.2.right, ...), custom_call_target="tpu_custom_call" | custom-call | flops 2000000000 | bytes 12582912 | tf_op jit(solution)/shard_map/score/pallas_call | solution.py:151
  52.7 0.1 collective-permute-start.6
  52.7 3.1 %collective-permute-start.5 = (f32[2,64]{1,0:T(2,128)S(1)}, f32[2,64]{1,0:T(2,128)S(1)}, u32[]{:S(2)}, u32[]{:S(2)}) collective-permute-start(f32[2,64]{1,0:T(2,128)S(1)} %get-tuple-element.12.s0), channel_id=1, source_target_pairs={{0,64},{64,0},{1,65},{65,1},{2,66},{66,2},{3,67},{67,3},{4,68},{68... | collective-permute-start | bytes 1544 | tf_op jit(solution)/shard_map/ppermute | solution.py:275
  55.9 0.2 collective-permute-start.4
  56.1 1.1 %collective-permute-done.6.s3 = f32[2,64]{1,0:T(2,128)S(1)} collective-permute-done((f32[2,64]{1,0:T(2,128)S(1)}, f32[2,64]{1,0:T(2,128)S(1)}, u32[]{:S(2)}, u32[]{:S(2)}) %collective-permute-start.6) | collective-permute-done | bytes 544 | tf_op jit(solution)/shard_map/ppermute | solution.py:276
  57.2 0.7 collective-permute-done.5.s2
  57.9 7.8 %insert.1 = (f32[128,1024]{1,0:T(8,128)S(1)}, bf16[128,1024]{1,0:T(8,128)(2,1)S(1)}, f32[1,64]{1,0:T(1,128)}) custom-call(f32[128,576]{1,0:T(8,128)S(1)} %get-tuple-element.11.raised, f32[2,64]{1,0:T(2,128)S(1)} %get-tuple-element.12.s0, f32[2,64]{1,0:T(2,128)S(1)} %collective-permute-done.4.s1, f32[2,64]{1,0:T(2,128)S(1)} %collective-permute-done.5.s2, ...), custom_call_target="tpu_custom_call" | custom-call | flops 3000000000 | bytes 12582912 | tf_op jit(solution)/shard_map/insert/pallas_call | solution.py:228
  65.7 1.9 %collective-permute-start.7 = (bf16[128,1024]{1,0:T(8,128)(2,1)S(1)}, bf16[128,1024]{1,0:T(8,128)(2,1)S(1)}, u32[]{:S(2)}, u32[]{:S(2)}) collective-permute-start(bf16[128,1024]{1,0:T(8,128)(2,1)S(1)} %get-tuple-element.14), channel_id=1, source_target_pairs={{0,32},{32,0},{1,33},{33,1},{2,34},{34,2},{3,35},{35,3},{4,36},{36... | collective-permute-start | bytes 786440 | tf_op jit(solution)/shard_map/ppermute | solution.py:279
  67.6 1.2 %collective-permute-done.7 = bf16[128,1024]{1,0:T(8,128)(2,1)S(1)} collective-permute-done((bf16[128,1024]{1,0:T(8,128)(2,1)S(1)}, bf16[128,1024]{1,0:T(8,128)(2,1)S(1)}, u32[]{:S(2)}, u32[]{:S(2)}) %collective-permute-start.7) | collective-permute-done | bytes 262176 | tf_op jit(solution)/shard_map/ppermute | solution.py:279
  68.8 0.1 reshape.17
  68.9 23.5 %all_to_all.11 = bf16[64,2,1024]{2,1,0:T(2,128)(2,1)S(1)} all-to-all(bf16[64,2,1024]{2,1,0:T(2,128)(2,1)S(1)} %reshape.17), channel_id=1, replica_groups=mesh['half'=2,'px'=2,'core'=2,'dom'=32] {'px','dom'}, dimensions={0} | all-to-all | bytes 524288 | tf_op jit(solution)/shard_map/all_to_all | solution.py:281
  92.4 0.8 convert_reduce_fusion
  (13 shorter events, 0.2 us)
Async XLA Ops:
  30.5 16.2 %collective-permute-start.1 = (bf16[32,8192]{1,0:T(8,128)(2,1)S(1)}, bf16[32,8192]{1,0:T(8,128)(2,1)S(1)}, u32[]{:S(2)}, u32[]{:S(2)}) collective-permute-start(bf16[32,8192]{1,0:T(8,128)(2,1)S(1)} %reshape.16.own), channel_id=1, source_target_pairs={{28,0},{29,1},{30,2},{31,3},{0,4},{1,5},{2,6},{3,7},{4,8},{5,9},{6... | collective-permute-start | bytes 1572872 | tf_op jit(solution)/shard_map/ppermute | solution.py:266
  31.7 15.1 %collective-permute-start = (bf16[32,8192]{1,0:T(8,128)(2,1)S(1)}, bf16[32,8192]{1,0:T(8,128)(2,1)S(1)}, u32[]{:S(2)}, u32[]{:S(2)}) collective-permute-start(bf16[32,8192]{1,0:T(8,128)(2,1)S(1)} %reshape.16.own), channel_id=1, source_target_pairs={{4,0},{5,1},{6,2},{7,3},{8,4},{9,5},{10,6},{11,7},{12,8},{13,9},{1... | collective-permute-start | bytes 1572872 | tf_op jit(solution)/shard_map/ppermute | solution.py:265
  33.0 13.8 %collective-permute-start.2 = (bf16[16,8192]{1,0:T(8,128)(2,1)S(1)}, bf16[16,8192]{1,0:T(8,128)(2,1)S(1)}, u32[]{:S(2)}, u32[]{:S(2)}) collective-permute-start(bf16[16,8192]{1,0:T(8,128)(2,1)S(1)} %slice.13), channel_id=1, source_target_pairs={{1,0},{2,1},{3,2},{0,3},{5,4},{6,5},{7,6},{4,7},{9,8},{10,9},{11,1... | collective-permute-start | bytes 786440 | tf_op jit(solution)/shard_map/ppermute | solution.py:267
  33.4 13.4 %collective-permute-start.3 = (bf16[16,8192]{1,0:T(8,128)(2,1)S(1)}, bf16[16,8192]{1,0:T(8,128)(2,1)S(1)}, u32[]{:S(2)}, u32[]{:S(2)}) collective-permute-start(bf16[16,8192]{1,0:T(8,128)(2,1)S(1)} %slice.15), channel_id=1, source_target_pairs={{3,0},{0,1},{1,2},{2,3},{7,4},{4,5},{5,6},{6,7},{11,8},{8,9},{9,10... | collective-permute-start | bytes 786440 | tf_op jit(solution)/shard_map/ppermute | solution.py:268
  35.1 1.2 %copy-start = (bf16[64,8192]{1,0:T(8,128)(2,1)S(1)}, bf16[64,8192]{1,0:T(8,128)(2,1)}, u32[]{:S(2)}) copy-start(bf16[64,8192]{1,0:T(8,128)(2,1)} %image_ref.1) | copy-start | bytes 3145732
  36.3 0.7 copy-start.1
  37.0 2.5 %copy-start.3 = (bf16[64,160,256]{2,1,0:T(8,128)(2,1)S(1)}, bf16[64,160,256]{2,1,0:T(8,128)(2,1)}, u32[]{:S(2)}) copy-start(bf16[64,160,256]{2,1,0:T(8,128)(2,1)} %constant.4.clone.table_ref) | copy-start | bytes 15728644
  46.7 11.2 %copy-start.2 = (s32[128,8]{0,1:T(8,128)S(1)}, s32[128,8]{0,1:T(8,128)}, u32[]{:S(2)}) copy-start(s32[128,8]{0,1:T(8,128)} %param.8) | copy-start | bytes 12292
  52.7 4.6 %collective-permute-start.6 = (f32[2,64]{1,0:T(2,128)S(1)}, f32[2,64]{1,0:T(2,128)S(1)}, u32[]{:S(2)}, u32[]{:S(2)}) collective-permute-start(f32[2,64]{1,0:T(2,128)S(1)} %get-tuple-element.12.s0), channel_id=1, source_target_pairs={{0,96},{32,64},{64,32},{96,0},{1,97},{33,65},{65,33},{97,1},{2,98}... | collective-permute-start | bytes 1544 | tf_op jit(solution)/shard_map/ppermute | solution.py:276
  52.7 5.2 %collective-permute-start.5 = (f32[2,64]{1,0:T(2,128)S(1)}, f32[2,64]{1,0:T(2,128)S(1)}, u32[]{:S(2)}, u32[]{:S(2)}) collective-permute-start(f32[2,64]{1,0:T(2,128)S(1)} %get-tuple-element.12.s0), channel_id=1, source_target_pairs={{0,64},{64,0},{1,65},{65,1},{2,66},{66,2},{3,67},{67,3},{4,68},{68... | collective-permute-start | bytes 1544 | tf_op jit(solution)/shard_map/ppermute | solution.py:275
  55.9 2.0 %collective-permute-start.4 = (f32[2,64]{1,0:T(2,128)S(1)}, f32[2,64]{1,0:T(2,128)S(1)}, u32[]{:S(2)}, u32[]{:S(2)}) collective-permute-start(f32[2,64]{1,0:T(2,128)S(1)} %get-tuple-element.12.s0), channel_id=1, source_target_pairs={{0,32},{32,0},{1,33},{33,1},{2,34},{34,2},{3,35},{35,3},{4,36},{36... | collective-permute-start | bytes 1544 | tf_op jit(solution)/shard_map/ppermute | solution.py:274
  65.7 3.1 %collective-permute-start.7 = (bf16[128,1024]{1,0:T(8,128)(2,1)S(1)}, bf16[128,1024]{1,0:T(8,128)(2,1)S(1)}, u32[]{:S(2)}, u32[]{:S(2)}) collective-permute-start(bf16[128,1024]{1,0:T(8,128)(2,1)S(1)} %get-tuple-element.14), channel_id=1, source_target_pairs={{0,32},{32,0},{1,33},{33,1},{2,34},{34,2},{3,35},{35,3},{4,36},{36... | collective-permute-start | bytes 786440 | tf_op jit(solution)/shard_map/ppermute | solution.py:279

commit v2 on v1

v2 whole, which is shorter than its diff:
```python
import functools
import math

import jax
import jax.numpy as jnp
import numpy as np
from jax import lax
from jax.experimental import pallas as pl
from jax.experimental.pallas import tpu as pltpu
from jax.sharding import Mesh
from jax.sharding import PartitionSpec as P

PIX = 64
SHIFTS = 9
GRID = 7
OFFS = GRID * GRID
KPAD = 112
Z, Y = 8, 4
SEG = 8
BLK = 1024
VB = 256
OFFSET_SIGMA = 2.0
BF16 = jnp.bfloat16
F32 = jnp.float32


def dom_of(z, y):
    return (z % Z) * Y + y % Y


FAR = ((0, 0), (4, 0), (2, 2), (-2, 2))
NEAR = ((0, 0), (1, 0), (-1, 0), (0, 1), (0, -1), (1, 1), (-1, 1), (0, 2))


def receive_from(dz, dy):
    return [(dom_of(z + dz, y + dy), dom_of(z, y)) for z in range(Z) for y in range(Y)]


def phase_parts():
    offset = np.arange(OFFS)
    a, b = offset // GRID - GRID // 2, offset % GRID - GRID // 2
    f = np.arange(PIX) - PIX // 2
    turns = (f[:, None, None] * a[None, :, None] + f[None, None, :] * b[None, :, None]) % PIX
    angle = -2.0 * math.pi / PIX * turns
    cos, sin = np.cos(angle), np.sin(angle)
    table = np.concatenate([cos, cos, -sin, sin], axis=2).astype(np.float32)
    high = table.astype(BF16)
    low = (table - high.astype(np.float32)).astype(BF16)
    pad = np.zeros((PIX, KPAD - 2 * OFFS, 4 * PIX), BF16)
    return np.concatenate([high, low, pad], axis=1)


def one_hot(index_ref):
    rows = index_ref.shape[1]
    k = lax.broadcasted_iota(jnp.int32, (KPAD, rows), 0)
    offset = jnp.where(k < 2 * OFFS, k % OFFS, -1)
    return jnp.concatenate(
        [jnp.where(offset == index_ref[t : t + 1, :], 1.0, 0.0) for t in range(SHIFTS)], axis=1
    )


def shift_kernel(start, index_ref, image_ref, table_ref, out_ref, hot_ref):
    rows = image_ref.shape[0]
    hot_ref[...] = one_hot(index_ref).T.astype(BF16)
    for u in range(table_ref.shape[0]):
        phase = jnp.dot(hot_ref[...], table_ref[u], preferred_element_type=F32)
        cols = slice(u * 2 * PIX, (u + 1) * 2 * PIX)
        source = slice((start + u) * 2 * PIX, (start + u + 1) * 2 * PIX)
        x = image_ref[:, source].astype(F32)
        swapped = pltpu.roll(x, PIX, 1)
        for t in range(SHIFTS):
            part = phase[t * rows : (t + 1) * rows]
            out_ref[t * rows : (t + 1) * rows, cols] = (
                x * part[:, : 2 * PIX] + swapped * part[:, 2 * PIX :]
            ).astype(BF16)


VMEM = pl.BlockSpec(memory_space=pltpu.VMEM)


def params():
    return pltpu.CompilerParams(vmem_limit_bytes=24 << 20)


def shift_images(images, index_t, table, start):
    total = images.shape[0] * SHIFTS
    count = table.shape[0]
    return pl.pallas_call(
        functools.partial(shift_kernel, start),
        in_specs=[VMEM] * 3,
        out_specs=VMEM,
        out_shape=jax.ShapeDtypeStruct((total, count * 2 * PIX), BF16),
        scratch_shapes=[pltpu.VMEM((total, KPAD), BF16)],
        compiler_params=params(),
        cost_estimate=pl.CostEstimate(flops=count * 10**8, bytes_accessed=count << 18, transcendentals=0),
        name="shift",
    )(index_t, images, jnp.asarray(table))


def choose(g, values):
    out = jnp.zeros_like(g)
    for i, v in enumerate(values):
        if v:
            out = jnp.where(g == i, v, out)
    return out


def slots_kernel(slot_ref, hot_ref):
    count = slot_ref.shape[1]
    dom = lax.axis_index("dom")
    q = lax.broadcasted_iota(jnp.int32, (count, count), 1)
    piece, j = q // 16, (q // 4) % 4
    z = (dom // Y + choose(piece, [d for d, _ in NEAR]) + choose(j, [d for d, _ in FAR]) + Z) % Z
    y = (dom % Y + choose(piece, [d for _, d in NEAR]) + choose(j, [d for _, d in FAR]) + Y) % Y
    source = (z * Y + y) * 4 + q % 4
    order = jnp.where(lax.broadcasted_iota(jnp.int32, (count, count), 0) == source, 1.0, 0.0)
    slots = jnp.dot(
        slot_ref[...].astype(F32).astype(BF16), order.astype(BF16), preferred_element_type=F32
    ).astype(jnp.int32)
    core = lax.axis_index("core")
    m = lax.broadcasted_iota(jnp.int32, (VB, count), 0)
    half = m % (VB // 2)
    owner = jnp.where(m < VB // 2, core, 1 - core)
    block = half // (VB // 4) * (VB // 2) + owner * (VB // 4) + half % (VB // 4)
    for s in range(SEG):
        hot_ref[s] = jnp.where(block == slots[s : s + 1, :], 1.0, 0.0).astype(BF16)


def place_slots(slots_t):
    return pl.pallas_call(
        slots_kernel,
        in_specs=[VMEM],
        out_specs=VMEM,
        out_shape=jax.ShapeDtypeStruct((SEG, VB, slots_t.shape[1]), BF16),
        compiler_params=params(),
        cost_estimate=pl.CostEstimate(flops=10**8, bytes_accessed=4 << 20, transcendentals=0),
        name="slots",
    )(slots_t)


def tile_shifts(x):
    return jnp.concatenate([x] * SHIFTS, axis=1)


def over_shifts(op, x, rows):
    return functools.reduce(op, [x[:, t * rows : (t + 1) * rows] for t in range(SHIFTS)])


def score_kernel(n_moved, *refs):
    index_ref, raised, stats, acc = refs[-4:]
    moved, pieces = refs[:n_moved], refs[n_moved:-4]
    count, total = acc.shape
    acc[...] = jnp.zeros_like(acc)
    norm = jnp.zeros((count, 1), F32)
    start = 0
    for m in moved:
        for c in range(m.shape[1] // BLK):
            at = slice(start + c * BLK, start + (c + 1) * BLK)
            some = jnp.concatenate([p[:, at] for p in pieces], axis=0)
            acc[...] += lax.dot_general(
                some, m[:, c * BLK : (c + 1) * BLK], (((1,), (1,)), ((), ())), preferred_element_type=F32
            )
            wide = some.astype(F32)
            norm += jnp.sum(wide * wide, axis=1, keepdims=True)
        start += m.shape[1]
    k = lax.broadcasted_iota(jnp.int32, (8, KPAD), 1)
    a, b = k // GRID - GRID // 2, k % GRID - GRID // 2
    cost = (a * a + b * b).astype(F32) * (0.5 / (OFFSET_SIGMA * OFFSET_SIGMA))
    pen = jnp.dot(
        jnp.where(k < OFFS, cost, 0.0).astype(BF16), one_hot(index_ref).astype(BF16), preferred_element_type=F32
    )
    rows = total // SHIFTS
    scores = acc[...] - 0.5 * norm - pen[0:1, :]
    top = over_shifts(jnp.maximum, jnp.max(scores, axis=0, keepdims=True), rows)
    value = jnp.exp(scores - tile_shifts(top))
    raised[...] = value
    stats[0:1, :] = top
    stats[1:2, :] = over_shifts(jnp.add, jnp.sum(value, axis=0, keepdims=True), rows)


def score(pieces, moved, index_t):
    total = moved[0].shape[0]
    count = sum(p.shape[0] for p in pieces)
    return pl.pallas_call(
        functools.partial(score_kernel, len(moved)),
        in_specs=[VMEM] * (len(pieces) + len(moved) + 1),
        out_specs=[VMEM, VMEM],
        out_shape=[
            jax.ShapeDtypeStruct((count, total), F32),
            jax.ShapeDtypeStruct((2, total // SHIFTS), F32),
        ],
        scratch_shapes=[pltpu.VMEM((count, total), F32)],
        compiler_params=params(),
        cost_estimate=pl.CostEstimate(flops=2 * 10**9, bytes_accessed=12 << 20, transcendentals=1 << 17),
        name="score",
    )(*moved, *pieces, index_t)


def insert_kernel(scale, raised, s0, s1, s2, s3, hot, *rest):
    moved, (mine, other, evidence, acc, weight) = rest[:-5], rest[-5:]
    tops = [s[0:1, :] for s in (s0, s1, s2, s3)]
    sums = [s[1:2, :] for s in (s0, s1, s2, s3)]
    top = functools.reduce(jnp.maximum, tops)
    total = functools.reduce(jnp.add, [b * jnp.exp(a - top) for a, b in zip(tops, sums)])
    evidence[...] = top + jnp.log(total)
    factor = jnp.exp(tops[0] - top) / total
    weight[...] = (raised[...] * tile_shifts(factor)).astype(BF16)
    acc[...] = jnp.zeros_like(acc)

    start = 0
    for part in moved:
        for s in range(part.shape[1] // BLK):
            blocked = jnp.dot(hot[start + s], weight[...], preferred_element_type=F32).astype(BF16)
            acc[...] += jnp.dot(blocked, part[:, s * BLK : (s + 1) * BLK], preferred_element_type=F32)
        start += part.shape[1] // BLK
    mine[...] = acc[: VB // 2] * scale
    other[...] = (acc[VB // 2 :] * scale).astype(BF16)


def insert(raised, stats, hot, moved, scale):
    count, total = raised.shape
    rows = total // SHIFTS
    return pl.pallas_call(
        functools.partial(insert_kernel, scale),
        in_specs=[VMEM] * (6 + len(moved)),
        out_specs=[VMEM] * 3,
        out_shape=[
            jax.ShapeDtypeStruct((VB // 2, BLK), F32),
            jax.ShapeDtypeStruct((VB // 2, BLK), BF16),
            jax.ShapeDtypeStruct((1, rows), F32),
        ],
        scratch_shapes=[pltpu.VMEM((VB, BLK), F32), pltpu.VMEM((count, total), BF16)],
        compiler_params=params(),
        cost_estimate=pl.CostEstimate(flops=3 * 10**9, bytes_accessed=12 << 20, transcendentals=0),
        name="insert",
    )(raised, *stats, hot, *moved)


def gather(references, work):
    far = [lax.ppermute(references, "dom", receive_from(*d)) for d in FAR[1:]]
    far, done = lax.optimization_barrier((far, work[0]()))
    results = [done]
    own = jnp.concatenate([references, *far], axis=0)
    first = [lax.ppermute(own, "dom", receive_from(*d)) for d in NEAR[1:5]]
    up, done = lax.optimization_barrier((first[2], work[1]()))
    results.append(done)
    second = [lax.ppermute(up, "dom", receive_from(*d)) for d in ((1, 0), (-1, 0), (0, 1))]
    results.append(work[2]())
    return [own, *first, *second], results


def shards(images, shift_index, references, slot_blocks):
    rows = images.shape[0]
    scale = (rows * Z * Y * SEG / VB) ** (-0.5)
    index_t, table = shift_index.T, phase_parts()
    cuts = (0, 24, 40, 64)
    pieces, moved = gather(
        references,
        [functools.partial(shift_images, images, index_t, table[a:b], a) for a, b in zip(cuts, cuts[1:])],
    )
    hot = place_slots(slot_blocks.T)
    raised, stats = score(pieces, moved, index_t)
    swap = [(0, 1), (1, 0)]
    everyone = [
        stats,
        lax.ppermute(stats, "core", swap),
        lax.ppermute(stats, "px", swap),
        lax.ppermute(stats, ("px", "core"), [(i, 3 - i) for i in range(4)]),
    ]
    mine, other, evidence = insert(raised, everyone, hot, moved, scale)
    paired = mine + lax.ppermute(other, "core", swap).astype(F32)
    sent = paired.astype(BF16).reshape(2 * Z * Y, VB // (4 * Z * Y), BLK)
    arrived = lax.all_to_all(sent, ("px", "dom"), 0, 0, tiled=True)
    return (jnp.sum(arrived.astype(F32), axis=0), evidence.reshape(rows))


def solution(mesh):
    split = Mesh(mesh.devices.reshape(2, 2, 2, Z * Y), ("half", "px", "core", "dom"))
    in_specs = (
        P(("half", "dom"), None),
        P(("half", "dom"), None),
        P(("half", "px", "core", "dom"), None),
        P(("half", "px", "core"), None),
    )
    out_specs = (P(("half", "px", "core", "dom"), None), P(("half", "dom")))
    return jax.shard_map(shards, mesh=split, in_specs=in_specs, out_specs=out_specs, check_vma=False)
```

time: 93.6 us -> 80.2 us (0.86)
  blocking collectives: 52.3 us -> 24.1 us
  starting transfers between devices: 9.52 us -> 23.3 us
  waiting for transfers between devices: 2.98 us -> 12 us
  Pallas kernels: 20.9 us -> 15 us
  local copies, waits for them, and re-layouts: 5.92 us -> 3.38 us
    all_to_all x1 -> x0, blocking collectives: 28.8 us -> none  [shards(): lax.all_to_all(copies, 'dom', 0, 0, axis_index_groups=COSETS, tiled=True)]
    ppermute x4 -> x10, starting transfers between devices: 4.21 us -> 19.7 us  [the longest x3 11.7 us: gather(): far = [lax.ppermute(references, 'dom', receive_from(*d)) for d in FAR[1:]]]
    ppermute x4 -> x10, waiting for transfers between devices: 0.01 us -> 6.6 us  [the longest x4 2.83 us: gather(): first = [lax.ppermute(own, 'dom', receive_from(*d)) for d in NEAR[1:5]]]
    pallas_call x3 -> x6, Pallas kernels: 20.9 us -> 15 us  [the longest x3 5.91 us: shift_images(): pl.pallas_call(functools.partial(shift_kernel, start), in_specs=[VMEM] *...]
    ppermute x1, starting transfers between devices: 1.89 us -> 0.14 us  [shards(): paired = mine + lax.ppermute(other, 'core', swap).astype(F32)]
    ppermute x1, waiting for transfers between devices: 1.13 us -> 2.44 us  [shards(): lax.ppermute(stats, ('px', 'core'), [(i, 3 - i) for i in range(4)])]
    unnamed x8 -> x14, local copies, waits for them, and re-layouts: 4.41 us -> 3.28 us
    broadcast_in_dim x1 -> x0, local copies, waits for them, and re-layouts: 0.98 us -> none  [shards(): copies = jnp.broadcast_to(references[None], (8, *references.shape))]
  transfers between devices with their start and end apart: 8 -> 14, of which waited for: 3 -> 9; matrix products, arithmetic and copies ran while one was open for 0% -> 0% of each run, Pallas kernels for 8% -> 8%
where the time goes in v2:
time: 80.2 us; the launch traced here: 79.5 us
  blocking collectives  24.1 us (30%)
  starting transfers between devices  23.3 us (29%)
  Pallas kernels  15 us (19%)
  waiting for transfers between devices  12 us (15%)
  local copies, waits for them, and re-layouts  3.38 us (4%)
  other arithmetic  1.06 us (1%)
    all_to_all x1, blocking collectives, shards(): arrived = lax.all_to_all(sent, ('px', 'dom'), 0, 0, tiled=True)  24.1 us
    ppermute x3, starting transfers between devices, gather(): far = [lax.ppermute(references, 'dom', receive_from(*d)) for d in FAR[1:]]  11.7 us
    pallas_call x3, Pallas kernels, shift_images(): pl.pallas_call(functools.partial(shift_kernel, start), in_specs=[VMEM] *...  5.91 us
    pallas_call x1, Pallas kernels, insert(): pl.pallas_call(functools.partial(insert_kernel, scale), in_specs=[VMEM] *...  5 us
    ppermute x4, starting transfers between devices, gather(): first = [lax.ppermute(own, 'dom', receive_from(*d)) for d in NEAR[1:5]]  4.2 us
    pallas_call x1, Pallas kernels, score(): pl.pallas_call(functools.partial(score_kernel, len(moved)), in_specs=[VME...  3.8 us
    ppermute x3, starting transfers between devices, gather(): lax.ppermute(up, 'dom', receive_from(*d))  3.8 us
    unnamed x14, local copies, waits for them, and re-layouts  3.28 us
  transfers between devices with their start and end apart: 14, of which 9 were waited for; matrix products, arithmetic and copies ran while one was open for 0% of the time, Pallas kernels for 8%

profile of v2, /device:TPU:32, one launch (start us, length us, event | category | flops | bytes accessed | tf_op | source)
XLA Modules:
  0.0 79.5 jit_solution(14801394338098130088)
XLA Ops:
  0.6 6.4 %collective-permute-start = (bf16[4,8192]{1,0:T(4,128)(2,1)}, bf16[4,8192]{1,0:T(4,128)(2,1)S(1)}, u32[]{:S(2)}, u32[]{:S(2)}) collective-permute-start(bf16[4,8192]{1,0:T(4,128)(2,1)} %param.9), channel_id=1, source_target_pairs={{16,0},{17,1},{18,2},{19,3},{20,4},{21,5},{22,6},{23,7},{24,8},{25... | collective-permute-start | bytes 196616 | tf_op jit(solution)/shard_map/ppermute | solution.py:240
  7.0 3.2 %collective-permute-start.1 = (bf16[4,8192]{1,0:T(4,128)(2,1)}, bf16[4,8192]{1,0:T(4,128)(2,1)S(1)}, u32[]{:S(2)}, u32[]{:S(2)}) collective-permute-start(bf16[4,8192]{1,0:T(4,128)(2,1)} %param.9), channel_id=1, source_target_pairs={{10,0},{11,1},{8,2},{9,3},{14,4},{15,5},{12,6},{13,7},{18,8},{19,9... | collective-permute-start | bytes 196616 | tf_op jit(solution)/shard_map/ppermute | solution.py:240
  10.2 2.1 %collective-permute-start.2 = (bf16[4,8192]{1,0:T(4,128)(2,1)}, bf16[4,8192]{1,0:T(4,128)(2,1)S(1)}, u32[]{:S(2)}, u32[]{:S(2)}) collective-permute-start(bf16[4,8192]{1,0:T(4,128)(2,1)} %param.9), channel_id=1, source_target_pairs={{26,0},{27,1},{24,2},{25,3},{30,4},{31,5},{28,6},{29,7},{2,8},{3,9... | collective-permute-start | bytes 196616 | tf_op jit(solution)/shard_map/ppermute | solution.py:240
  13.0 1.2 %copy-done.2 = bf16[64,8192]{1,0:T(8,128)(2,1)S(1)} copy-done((bf16[64,8192]{1,0:T(8,128)(2,1)S(1)}, bf16[64,8192]{1,0:T(8,128)(2,1)}, u32[]{:S(2)}) %copy-start.2) | copy-done | bytes 1048600
  14.3 1.3 %copy-done.4 = bf16[24,112,256]{2,1,0:T(8,128)(2,1)S(1)} copy-done((bf16[24,112,256]{2,1,0:T(8,128)(2,1)S(1)}, bf16[24,112,256]{2,1,0:T(8,128)(2,1)}, u32[]{:S(2)}) %copy-start.4) | copy-done | bytes 1376280
  15.6 2.2 %shift.3.refs_0_.rest_0_ = bf16[576,3072]{1,0:T(8,128)(2,1)S(1)} custom-call(s32[9,64]{1,0:T(8,128)S(1)} %bitcast.3, bf16[64,8192]{1,0:T(8,128)(2,1)S(1)} %copy-done.2, bf16[24,112,256]{2,1,0:T(8,128)(2,1)S(1)} %copy-done.4), custom_call_target="tpu_custom_call" | custom-call | flops 2400000000 | bytes 6291456 | tf_op jit(solution)/shard_map/shift/pallas_call | solution.py:88
  17.8 1.4 %collective-permute-done.2 = bf16[4,8192]{1,0:T(4,128)(2,1)S(1)} collective-permute-done((bf16[4,8192]{1,0:T(4,128)(2,1)}, bf16[4,8192]{1,0:T(4,128)(2,1)S(1)}, u32[]{:S(2)}, u32[]{:S(2)}) %collective-permute-start.2) | collective-permute-done | bytes 65568 | tf_op jit(solution)/shard_map/ppermute | solution.py:240
  19.4 1.7 %collective-permute-start.3 = (bf16[16,8192]{1,0:T(8,128)(2,1)S(1)}, bf16[16,8192]{1,0:T(8,128)(2,1)S(1)}, u32[]{:S(2)}, u32[]{:S(2)}) collective-permute-start(bf16[16,8192]{1,0:T(8,128)(2,1)S(1)} %pad_maximum_fusion.refs_3_), channel_id=1, source_target_pairs={{1,0},{2,1},{3,2},{0,3},{5,4},{6,5},{7,6},{4,7},{9,8},{10,9},{11,1... | collective-permute-start | bytes 786440 | tf_op jit(solution)/shard_map/ppermute | solution.py:244
  21.1 1.0 %collective-permute-start.4 = (bf16[16,8192]{1,0:T(8,128)(2,1)S(1)}, bf16[16,8192]{1,0:T(8,128)(2,1)S(1)}, u32[]{:S(2)}, u32[]{:S(2)}) collective-permute-start(bf16[16,8192]{1,0:T(8,128)(2,1)S(1)} %pad_maximum_fusion.refs_3_), channel_id=1, source_target_pairs={{4,0},{5,1},{6,2},{7,3},{8,4},{9,5},{10,6},{11,7},{12,8},{13,9},{1... | collective-permute-start | bytes 786440 | tf_op jit(solution)/shard_map/ppermute | solution.py:244
  22.1 1.6 %shift.4.refs_1_.rest_1_ = bf16[576,2048]{1,0:T(8,128)(2,1)S(1)} custom-call(s32[9,64]{1,0:T(8,128)S(1)} %bitcast.4, bf16[64,8192]{1,0:T(8,128)(2,1)S(1)} %copy-done.2, bf16[16,112,256]{2,1,0:T(8,128)(2,1)S(1)} %copy-done.5), custom_call_target="tpu_custom_call" | custom-call | flops 1600000000 | bytes 4194304 | tf_op jit(solution)/shard_map/shift/pallas_call | solution.py:88
  23.7 1.3 %collective-permute-start.5 = (bf16[16,8192]{1,0:T(8,128)(2,1)S(1)}, bf16[16,8192]{1,0:T(8,128)(2,1)S(1)}, u32[]{:S(2)}, u32[]{:S(2)}) collective-permute-start(bf16[16,8192]{1,0:T(8,128)(2,1)S(1)} %pad_maximum_fusion.refs_3_), channel_id=1, source_target_pairs={{28,0},{29,1},{30,2},{31,3},{0,4},{1,5},{2,6},{3,7},{4,8},{5,9},{6... | collective-permute-start | bytes 786440 | tf_op jit(solution)/shard_map/ppermute | solution.py:244
  26.0 1.0 %collective-permute-start.7 = (bf16[16,8192]{1,0:T(8,128)(2,1)S(1)}, bf16[16,8192]{1,0:T(8,128)(2,1)S(1)}, u32[]{:S(2)}, u32[]{:S(2)}) collective-permute-start(bf16[16,8192]{1,0:T(8,128)(2,1)S(1)} %collective-permute-done.3.refs_6_), channel_id=1, source_target_pairs={{4,0},{5,1},{6,2},{7,3},{8,4},{9,5},{10,6},{11,7},{12,8},{13,9},{1... | collective-permute-start | bytes 786440 | tf_op jit(solution)/shard_map/ppermute | solution.py:247
  27.1 1.0 %collective-permute-start.8 = (bf16[16,8192]{1,0:T(8,128)(2,1)S(1)}, bf16[16,8192]{1,0:T(8,128)(2,1)S(1)}, u32[]{:S(2)}, u32[]{:S(2)}) collective-permute-start(bf16[16,8192]{1,0:T(8,128)(2,1)S(1)} %collective-permute-done.3.refs_6_), channel_id=1, source_target_pairs={{28,0},{29,1},{30,2},{31,3},{0,4},{1,5},{2,6},{3,7},{4,8},{5,9},{6... | collective-permute-start | bytes 786440 | tf_op jit(solution)/shard_map/ppermute | solution.py:247
  28.1 1.9 %collective-permute-done.4.refs_4_ = bf16[16,8192]{1,0:T(8,128)(2,1)S(1)} collective-permute-done((bf16[16,8192]{1,0:T(8,128)(2,1)S(1)}, bf16[16,8192]{1,0:T(8,128)(2,1)S(1)}, u32[]{:S(2)}, u32[]{:S(2)}) %collective-permute-start.4) | collective-permute-done | bytes 262176 | tf_op jit(solution)/shard_map/ppermute | solution.py:244
  30.0 1.8 %collective-permute-start.9 = (bf16[16,8192]{1,0:T(8,128)(2,1)S(1)}, bf16[16,8192]{1,0:T(8,128)(2,1)S(1)}, u32[]{:S(2)}, u32[]{:S(2)}) collective-permute-start(bf16[16,8192]{1,0:T(8,128)(2,1)S(1)} %collective-permute-done.3.refs_6_), channel_id=1, source_target_pairs={{1,0},{2,1},{3,2},{0,3},{5,4},{6,5},{7,6},{4,7},{9,8},{10,9},{11,1... | collective-permute-start | bytes 786440 | tf_op jit(solution)/shard_map/ppermute | solution.py:247
  31.8 2.2 %shift.5.refs_2_.rest_2_ = bf16[576,3072]{1,0:T(8,128)(2,1)S(1)} custom-call(s32[9,64]{1,0:T(8,128)S(1)} %bitcast.5, bf16[64,8192]{1,0:T(8,128)(2,1)S(1)} %copy-done.2, bf16[24,112,256]{2,1,0:T(8,128)(2,1)S(1)} %copy-done.3), custom_call_target="tpu_custom_call" | custom-call | flops 2400000000 | bytes 6291456 | tf_op jit(solution)/shard_map/shift/pallas_call | solution.py:88
  34.1 1.9 %collective-permute-done.8.refs_9_ = bf16[16,8192]{1,0:T(8,128)(2,1)S(1)} collective-permute-done((bf16[16,8192]{1,0:T(8,128)(2,1)S(1)}, bf16[16,8192]{1,0:T(8,128)(2,1)S(1)}, u32[]{:S(2)}, u32[]{:S(2)}) %collective-permute-start.8) | collective-permute-done | bytes 262176 | tf_op jit(solution)/shard_map/ppermute | solution.py:247
  36.4 3.8 %score.1 = (f32[128,576]{1,0:T(8,128)S(1)}, f32[2,64]{1,0:T(2,128)S(1)}) custom-call(bf16[576,3072]{1,0:T(8,128)(2,1)S(1)} %shift.3.refs_0_.rest_0_, bf16[576,2048]{1,0:T(8,128)(2,1)S(1)} %shift.4.refs_1_.rest_1_, bf16[576,3072]{1,0:T(8,128)(2,1)S(1)} %shift.5.refs_2_.rest_2_, bf16[16,8192]{1,0:T(8,128)(2,1)S(1)} %pad_maximum_fusion.refs_3_, ...), custom_call_target="tpu_custom_call" | custom-call | flops 2000000000 | bytes 12582912 | tf_op jit(solution)/shard_map/score/pallas_call | solution.py:184
  40.2 3.1 %collective-permute-start.11 = (f32[2,64]{1,0:T(2,128)S(1)}, f32[2,64]{1,0:T(2,128)S(1)}, u32[]{:S(2)}, u32[]{:S(2)}) collective-permute-start(f32[2,64]{1,0:T(2,128)S(1)} %get-tuple-element.20.s0), channel_id=1, source_target_pairs={{0,64},{64,0},{1,65},{65,1},{2,66},{66,2},{3,67},{67,3},{4,68},{68... | collective-permute-start | bytes 1544 | tf_op jit(solution)/shard_map/ppermute | solution.py:267
  43.8 1.5 %collective-permute-done.11.s2 = f32[2,64]{1,0:T(2,128)S(1)} collective-permute-done((f32[2,64]{1,0:T(2,128)S(1)}, f32[2,64]{1,0:T(2,128)S(1)}, u32[]{:S(2)}, u32[]{:S(2)}) %collective-permute-start.11) | collective-permute-done | bytes 544 | tf_op jit(solution)/shard_map/ppermute | solution.py:267
  45.4 2.4 %collective-permute-done.12.s3 = f32[2,64]{1,0:T(2,128)S(1)} collective-permute-done((f32[2,64]{1,0:T(2,128)S(1)}, f32[2,64]{1,0:T(2,128)S(1)}, u32[]{:S(2)}, u32[]{:S(2)}) %collective-permute-start.12) | collective-permute-done | bytes 544 | tf_op jit(solution)/shard_map/ppermute | solution.py:268
  47.8 5.0 %insert.1 = (f32[128,1024]{1,0:T(8,128)S(1)}, bf16[128,1024]{1,0:T(8,128)(2,1)S(1)}, f32[1,64]{1,0:T(1,128)}) custom-call(f32[128,576]{1,0:T(8,128)S(1)} %get-tuple-element.19.raised, f32[2,64]{1,0:T(2,128)S(1)} %get-tuple-element.20.s0, f32[2,64]{1,0:T(2,128)S(1)} %collective-permute-done.10.s1, f32[2,64]{1,0:T(2,128)S(1)} %collective-permute-done.11.s2, ...), custom_call_target="tpu_custom_call" | custom-call | flops 3000000000 | bytes 12582912 | tf_op jit(solution)/shard_map/insert/pallas_call | solution.py:223
  53.0 1.4 %collective-permute-done.13 = bf16[128,1024]{1,0:T(8,128)(2,1)S(1)} collective-permute-done((bf16[128,1024]{1,0:T(8,128)(2,1)S(1)}, bf16[128,1024]{1,0:T(8,128)(2,1)S(1)}, u32[]{:S(2)}, u32[]{:S(2)}) %collective-permute-start.13) | collective-permute-done | bytes 262176 | tf_op jit(solution)/shard_map/ppermute | solution.py:271
  54.5 24.1 %all_to_all.5 = bf16[64,2,1024]{2,1,0:T(2,128)(2,1)S(1)} all-to-all(bf16[64,2,1024]{2,1,0:T(2,128)(2,1)S(1)} %reshape.10), channel_id=1, replica_groups=mesh['half'=2,'px'=2,'core'=2,'dom'=32] {'px','dom'}, dimensions={0} | all-to-all | bytes 524288 | tf_op jit(solution)/shard_map/all_to_all | solution.py:273
  (29 shorter events, 4.2 us)
Async XLA Ops:
  0.6 17.1 %collective-permute-start = (bf16[4,8192]{1,0:T(4,128)(2,1)}, bf16[4,8192]{1,0:T(4,128)(2,1)S(1)}, u32[]{:S(2)}, u32[]{:S(2)}) collective-permute-start(bf16[4,8192]{1,0:T(4,128)(2,1)} %param.9), channel_id=1, source_target_pairs={{16,0},{17,1},{18,2},{19,3},{20,4},{21,5},{22,6},{23,7},{24,8},{25... | collective-permute-start | bytes 196616 | tf_op jit(solution)/shard_map/ppermute | solution.py:240
  7.0 10.8 %collective-permute-start.1 = (bf16[4,8192]{1,0:T(4,128)(2,1)}, bf16[4,8192]{1,0:T(4,128)(2,1)S(1)}, u32[]{:S(2)}, u32[]{:S(2)}) collective-permute-start(bf16[4,8192]{1,0:T(4,128)(2,1)} %param.9), channel_id=1, source_target_pairs={{10,0},{11,1},{8,2},{9,3},{14,4},{15,5},{12,6},{13,7},{18,8},{19,9... | collective-permute-start | bytes 196616 | tf_op jit(solution)/shard_map/ppermute | solution.py:240
  10.2 9.0 %collective-permute-start.2 = (bf16[4,8192]{1,0:T(4,128)(2,1)}, bf16[4,8192]{1,0:T(4,128)(2,1)S(1)}, u32[]{:S(2)}, u32[]{:S(2)}) collective-permute-start(bf16[4,8192]{1,0:T(4,128)(2,1)} %param.9), channel_id=1, source_target_pairs={{26,0},{27,1},{24,2},{25,3},{30,4},{31,5},{28,6},{29,7},{2,8},{3,9... | collective-permute-start | bytes 196616 | tf_op jit(solution)/shard_map/ppermute | solution.py:240
  12.3 0.7 copy-start
  13.0 1.2 %copy-start.2 = (bf16[64,8192]{1,0:T(8,128)(2,1)S(1)}, bf16[64,8192]{1,0:T(8,128)(2,1)}, u32[]{:S(2)}) copy-start(bf16[64,8192]{1,0:T(8,128)(2,1)} %image_ref.5) | copy-start | bytes 3145732
  14.3 1.3 %copy-start.4 = (bf16[24,112,256]{2,1,0:T(8,128)(2,1)S(1)}, bf16[24,112,256]{2,1,0:T(8,128)(2,1)}, u32[]{:S(2)}) copy-start(bf16[24,112,256]{2,1,0:T(8,128)(2,1)} %constant.8.clone.table_ref) | copy-start | bytes 4128772
  15.6 3.6 %copy-start.6 = (bf16[4,8192]{1,0:T(4,128)(2,1)S(1)}, bf16[4,8192]{1,0:T(4,128)(2,1)}, u32[]{:S(2)}) copy-start(bf16[4,8192]{1,0:T(4,128)(2,1)} %param.9) | copy-start | bytes 196612
  15.6 6.5 %copy-start.5 = (bf16[16,112,256]{2,1,0:T(8,128)(2,1)S(1)}, bf16[16,112,256]{2,1,0:T(8,128)(2,1)}, u32[]{:S(2)}) copy-start(bf16[16,112,256]{2,1,0:T(8,128)(2,1)} %constant.9.clone.table_ref) | copy-start | bytes 2752516
  19.3 12.4 %copy-start.3 = (bf16[24,112,256]{2,1,0:T(8,128)(2,1)S(1)}, bf16[24,112,256]{2,1,0:T(8,128)(2,1)}, u32[]{:S(2)}) copy-start(bf16[24,112,256]{2,1,0:T(8,128)(2,1)} %constant.10.clone.table_ref) | copy-start | bytes 4128772
  19.4 6.7 %collective-permute-start.3 = (bf16[16,8192]{1,0:T(8,128)(2,1)S(1)}, bf16[16,8192]{1,0:T(8,128)(2,1)S(1)}, u32[]{:S(2)}, u32[]{:S(2)}) collective-permute-start(bf16[16,8192]{1,0:T(8,128)(2,1)S(1)} %pad_maximum_fusion.refs_3_), channel_id=1, source_target_pairs={{1,0},{2,1},{3,2},{0,3},{5,4},{6,5},{7,6},{4,7},{9,8},{10,9},{11,1... | collective-permute-start | bytes 786440 | tf_op jit(solution)/shard_map/ppermute | solution.py:244
  21.1 8.9 %collective-permute-start.4 = (bf16[16,8192]{1,0:T(8,128)(2,1)S(1)}, bf16[16,8192]{1,0:T(8,128)(2,1)S(1)}, u32[]{:S(2)}, u32[]{:S(2)}) collective-permute-start(bf16[16,8192]{1,0:T(8,128)(2,1)S(1)} %pad_maximum_fusion.refs_3_), channel_id=1, source_target_pairs={{4,0},{5,1},{6,2},{7,3},{8,4},{9,5},{10,6},{11,7},{12,8},{13,9},{1... | collective-permute-start | bytes 786440 | tf_op jit(solution)/shard_map/ppermute | solution.py:244
  23.7 10.3 %collective-permute-start.5 = (bf16[16,8192]{1,0:T(8,128)(2,1)S(1)}, bf16[16,8192]{1,0:T(8,128)(2,1)S(1)}, u32[]{:S(2)}, u32[]{:S(2)}) collective-permute-start(bf16[16,8192]{1,0:T(8,128)(2,1)S(1)} %pad_maximum_fusion.refs_3_), channel_id=1, source_target_pairs={{28,0},{29,1},{30,2},{31,3},{0,4},{1,5},{2,6},{3,7},{4,8},{5,9},{6... | collective-permute-start | bytes 786440 | tf_op jit(solution)/shard_map/ppermute | solution.py:244
  25.0 9.0 %collective-permute-start.6 = (bf16[16,8192]{1,0:T(8,128)(2,1)S(1)}, bf16[16,8192]{1,0:T(8,128)(2,1)S(1)}, u32[]{:S(2)}, u32[]{:S(2)}) collective-permute-start(bf16[16,8192]{1,0:T(8,128)(2,1)S(1)} %pad_maximum_fusion.refs_3_), channel_id=1, source_target_pairs={{3,0},{0,1},{1,2},{2,3},{7,4},{4,5},{5,6},{6,7},{11,8},{8,9},{9,10... | collective-permute-start | bytes 786440 | tf_op jit(solution)/shard_map/ppermute | solution.py:244
  26.0 8.1 %collective-permute-start.7 = (bf16[16,8192]{1,0:T(8,128)(2,1)S(1)}, bf16[16,8192]{1,0:T(8,128)(2,1)S(1)}, u32[]{:S(2)}, u32[]{:S(2)}) collective-permute-start(bf16[16,8192]{1,0:T(8,128)(2,1)S(1)} %collective-permute-done.3.refs_6_), channel_id=1, source_target_pairs={{4,0},{5,1},{6,2},{7,3},{8,4},{9,5},{10,6},{11,7},{12,8},{13,9},{1... | collective-permute-start | bytes 786440 | tf_op jit(solution)/shard_map/ppermute | solution.py:247
  27.1 8.9 %collective-permute-start.8 = (bf16[16,8192]{1,0:T(8,128)(2,1)S(1)}, bf16[16,8192]{1,0:T(8,128)(2,1)S(1)}, u32[]{:S(2)}, u32[]{:S(2)}) collective-permute-start(bf16[16,8192]{1,0:T(8,128)(2,1)S(1)} %collective-permute-done.3.refs_6_), channel_id=1, source_target_pairs={{28,0},{29,1},{30,2},{31,3},{0,4},{1,5},{2,6},{3,7},{4,8},{5,9},{6... | collective-permute-start | bytes 786440 | tf_op jit(solution)/shard_map/ppermute | solution.py:247
  30.0 6.4 %collective-permute-start.9 = (bf16[16,8192]{1,0:T(8,128)(2,1)S(1)}, bf16[16,8192]{1,0:T(8,128)(2,1)S(1)}, u32[]{:S(2)}, u32[]{:S(2)}) collective-permute-start(bf16[16,8192]{1,0:T(8,128)(2,1)S(1)} %collective-permute-done.3.refs_6_), channel_id=1, source_target_pairs={{1,0},{2,1},{3,2},{0,3},{5,4},{6,5},{7,6},{4,7},{9,8},{10,9},{11,1... | collective-permute-start | bytes 786440 | tf_op jit(solution)/shard_map/ppermute | solution.py:247
  33.9 9.6 %copy-start.1 = (s32[128,8]{0,1:T(8,128)S(1)}, s32[128,8]{0,1:T(8,128)}, u32[]{:S(2)}) copy-start(s32[128,8]{0,1:T(8,128)} %param.10) | copy-start | bytes 12292
  40.2 3.7 %collective-permute-start.10 = (f32[2,64]{1,0:T(2,128)S(1)}, f32[2,64]{1,0:T(2,128)S(1)}, u32[]{:S(2)}, u32[]{:S(2)}) collective-permute-start(f32[2,64]{1,0:T(2,128)S(1)} %get-tuple-element.20.s0), channel_id=1, source_target_pairs={{0,32},{32,0},{1,33},{33,1},{2,34},{34,2},{3,35},{35,3},{4,36},{36... | collective-permute-start | bytes 1544 | tf_op jit(solution)/shard_map/ppermute | solution.py:266
  40.2 5.2 %collective-permute-start.11 = (f32[2,64]{1,0:T(2,128)S(1)}, f32[2,64]{1,0:T(2,128)S(1)}, u32[]{:S(2)}, u32[]{:S(2)}) collective-permute-start(f32[2,64]{1,0:T(2,128)S(1)} %get-tuple-element.20.s0), channel_id=1, source_target_pairs={{0,64},{64,0},{1,65},{65,1},{2,66},{66,2},{3,67},{67,3},{4,68},{68... | collective-permute-start | bytes 1544 | tf_op jit(solution)/shard_map/ppermute | solution.py:267
  43.3 4.5 %collective-permute-start.12 = (f32[2,64]{1,0:T(2,128)S(1)}, f32[2,64]{1,0:T(2,128)S(1)}, u32[]{:S(2)}, u32[]{:S(2)}) collective-permute-start(f32[2,64]{1,0:T(2,128)S(1)} %get-tuple-element.20.s0), channel_id=1, source_target_pairs={{0,96},{32,64},{64,32},{96,0},{1,97},{33,65},{65,33},{97,1},{2,98}... | collective-permute-start | bytes 1544 | tf_op jit(solution)/shard_map/ppermute | solution.py:268
  52.8 1.5 %collective-permute-start.13 = (bf16[128,1024]{1,0:T(8,128)(2,1)S(1)}, bf16[128,1024]{1,0:T(8,128)(2,1)S(1)}, u32[]{:S(2)}, u32[]{:S(2)}) collective-permute-start(bf16[128,1024]{1,0:T(8,128)(2,1)S(1)} %get-tuple-element.22), channel_id=1, source_target_pairs={{0,32},{32,0},{1,33},{33,1},{2,34},{34,2},{3,35},{35,3},{4,36},{36... | collective-permute-start | bytes 786440 | tf_op jit(solution)/shard_map/ppermute | solution.py:271

commit v3 on v2

--- a/solution.py
+++ b/solution.py
@@ -15,6 +15,7 @@
 GRID = 7
 OFFS = GRID * GRID
 KPAD = 112
+CUT = 24
 Z, Y = 8, 4
 SEG = 8
 BLK = 1024
@@ -149,17 +150,17 @@
 def score_kernel(n_moved, *refs):
     index_ref, raised, stats, acc = refs[-4:]
     moved, pieces = refs[:n_moved], refs[n_moved:-4]
-    count, total = acc.shape
-    acc[...] = jnp.zeros_like(acc)
+    total, count = acc.shape
     norm = jnp.zeros((count, 1), F32)
     start = 0
     for m in moved:
         for c in range(m.shape[1] // BLK):
             at = slice(start + c * BLK, start + (c + 1) * BLK)
             some = jnp.concatenate([p[:, at] for p in pieces], axis=0)
-            acc[...] += lax.dot_general(
-                some, m[:, c * BLK : (c + 1) * BLK], (((1,), (1,)), ((), ())), preferred_element_type=F32
+            part = lax.dot_general(
+                m[:, c * BLK : (c + 1) * BLK], some, (((1,), (1,)), ((), ())), preferred_element_type=F32
             )
+            acc[...] = acc[...] + part if at.start else part
             wide = some.astype(F32)
             norm += jnp.sum(wide * wide, axis=1, keepdims=True)
         start += m.shape[1]
@@ -170,7 +171,7 @@
         jnp.where(k < OFFS, cost, 0.0).astype(BF16), one_hot(index_ref).astype(BF16), preferred_element_type=F32
     )
     rows = total // SHIFTS
-    scores = acc[...] - 0.5 * norm - pen[0:1, :]
+    scores = acc[...].T - 0.5 * norm - pen[0:1, :]
     top = over_shifts(jnp.maximum, jnp.max(scores, axis=0, keepdims=True), rows)
     value = jnp.exp(scores - tile_shifts(top))
     raised[...] = value
@@ -189,7 +190,7 @@
             jax.ShapeDtypeStruct((count, total), F32),
             jax.ShapeDtypeStruct((2, total // SHIFTS), F32),
         ],
-        scratch_shapes=[pltpu.VMEM((count, total), F32)],
+        scratch_shapes=[pltpu.VMEM((total, count), F32)],
         compiler_params=params(),
         cost_estimate=pl.CostEstimate(flops=2 * 10**9, bytes_accessed=12 << 20, transcendentals=1 << 17),
         name="score",
@@ -197,7 +198,7 @@
 
 
 def insert_kernel(scale, raised, s0, s1, s2, s3, hot, *rest):
-    moved, (mine, other, evidence, acc, weight) = rest[:-5], rest[-5:]
+    moved, (mine, other, evidence, weight) = rest[:-4], rest[-4:]
     tops = [s[0:1, :] for s in (s0, s1, s2, s3)]
     sums = [s[1:2, :] for s in (s0, s1, s2, s3)]
     top = functools.reduce(jnp.maximum, tops)
@@ -205,14 +206,11 @@
     evidence[...] = top + jnp.log(total)
     factor = jnp.exp(tops[0] - top) / total
     weight[...] = (raised[...] * tile_shifts(factor)).astype(BF16)
-    acc[...] = jnp.zeros_like(acc)
-
-    start = 0
-    for part in moved:
-        for s in range(part.shape[1] // BLK):
-            blocked = jnp.dot(hot[start + s], weight[...], preferred_element_type=F32).astype(BF16)
-            acc[...] += jnp.dot(blocked, part[:, s * BLK : (s + 1) * BLK], preferred_element_type=F32)
-        start += part.shape[1] // BLK
+    blocked = [jnp.dot(hot[s], weight[...], preferred_element_type=F32).astype(BF16) for s in range(SEG)]
+    parts = [m[:, s : s + BLK] for m in moved for s in range(0, m.shape[1], BLK)]
+    acc = jnp.dot(
+        jnp.concatenate(blocked, axis=1), jnp.concatenate(parts, axis=0), preferred_element_type=F32
+    )
     mine[...] = acc[: VB // 2] * scale
     other[...] = (acc[VB // 2 :] * scale).astype(BF16)
 
@@ -222,41 +220,38 @@
     rows = total // SHIFTS
     return pl.pallas_call(
         functools.partial(insert_kernel, scale),
-        in_specs=[VMEM] * (6 + len(moved)),
+        in_specs=[VMEM] * (2 + len(stats) + len(moved)),
         out_specs=[VMEM] * 3,
         out_shape=[
             jax.ShapeDtypeStruct((VB // 2, BLK), F32),
             jax.ShapeDtypeStruct((VB // 2, BLK), BF16),
             jax.ShapeDtypeStruct((1, rows), F32),
         ],
-        scratch_shapes=[pltpu.VMEM((VB, BLK), F32), pltpu.VMEM((count, total), BF16)],
+        scratch_shapes=[pltpu.VMEM((count, total), BF16)],
         compiler_params=params(),
         cost_estimate=pl.CostEstimate(flops=3 * 10**9, bytes_accessed=12 << 20, transcendentals=0),
         name="insert",
     )(raised, *stats, hot, *moved)
 
 
-def gather(references, work):
+def gather(references, early, late):
     far = [lax.ppermute(references, "dom", receive_from(*d)) for d in FAR[1:]]
-    far, done = lax.optimization_barrier((far, work[0]()))
-    results = [done]
+    far, early = lax.optimization_barrier((far, early()))
     own = jnp.concatenate([references, *far], axis=0)
     first = [lax.ppermute(own, "dom", receive_from(*d)) for d in NEAR[1:5]]
-    up, done = lax.optimization_barrier((first[2], work[1]()))
-    results.append(done)
+    up = first[2]
     second = [lax.ppermute(up, "dom", receive_from(*d)) for d in ((1, 0), (-1, 0), (0, 1))]
-    results.append(work[2]())
-    return [own, *first, *second], results
+    return [own, *first, *second], (early, late())
 
 
 def shards(images, shift_index, references, slot_blocks):
     rows = images.shape[0]
     scale = (rows * Z * Y * SEG / VB) ** (-0.5)
     index_t, table = shift_index.T, phase_parts()
-    cuts = (0, 24, 40, 64)
     pieces, moved = gather(
         references,
-        [functools.partial(shift_images, images, index_t, table[a:b], a) for a, b in zip(cuts, cuts[1:])],
+        lambda: shift_images(images, index_t, table[:CUT], 0),
+        lambda: shift_images(images, index_t, table[CUT:], CUT),
     )
     hot = place_slots(slot_blocks.T)
     raised, stats = score(pieces, moved, index_t)

time: 80.2 us -> 78.1 us (0.974)
  Pallas kernels: 15 us -> 12.6 us
    ppermute x4, waiting for transfers between devices: 2.83 us -> 4.47 us  [gather(): first = [lax.ppermute(own, 'dom', receive_from(*d)) for d in NEAR[1:5]]]
    pallas_call x1, Pallas kernels: 5 us -> 3.74 us  [insert(): pl.pallas_call(functools.partial(insert_kernel, scale), in_specs=[VMEM] *...]
    ppermute x3, waiting for transfers between devices: 2.38 us -> 1.14 us  [gather(): lax.ppermute(up, 'dom', receive_from(*d))]
    pallas_call x3 -> x2, Pallas kernels: 5.91 us -> 5.58 us  [shift_images(): pl.pallas_call(functools.partial(shift_kernel, start), in_specs=[VMEM] *...]
    unnamed x14 -> x12, local copies, waits for them, and re-layouts: 3.28 us -> 3.27 us
  transfers between devices with their start and end apart: 14 -> 14, of which waited for: 9 -> 7; matrix products, arithmetic and copies ran while one was open for 0% -> 0% of each run, Pallas kernels for 8% -> 8%
where the time goes in v3:
time: 78.1 us; the launch traced here: 77.4 us
  blocking collectives  24.1 us (31%)
  starting transfers between devices  23.2 us (30%)
  Pallas kernels  12.6 us (16%)
  waiting for transfers between devices  12.3 us (16%)
  local copies, waits for them, and re-layouts  3.37 us (4%)
  other arithmetic  1.05 us (1%)
    all_to_all x1, blocking collectives, shards(): arrived = lax.all_to_all(sent, ('px', 'dom'), 0, 0, tiled=True)  24.1 us
    ppermute x3, starting transfers between devices, gather(): far = [lax.ppermute(references, 'dom', receive_from(*d)) for d in FAR[1:]]  11.7 us
    pallas_call x2, Pallas kernels, shift_images(): pl.pallas_call(functools.partial(shift_kernel, start), in_specs=[VMEM] *...  5.58 us
    ppermute x4, waiting for transfers between devices, gather(): first = [lax.ppermute(own, 'dom', receive_from(*d)) for d in NEAR[1:5]]  4.47 us
    ppermute x4, starting transfers between devices, gather(): first = [lax.ppermute(own, 'dom', receive_from(*d)) for d in NEAR[1:5]]  4.13 us
    ppermute x3, starting transfers between devices, gather(): lax.ppermute(up, 'dom', receive_from(*d))  3.8 us
    pallas_call x1, Pallas kernels, insert(): pl.pallas_call(functools.partial(insert_kernel, scale), in_specs=[VMEM] *...  3.74 us
    unnamed x12, local copies, waits for them, and re-layouts  3.27 us
  transfers between devices with their start and end apart: 14, of which 7 were waited for; matrix products, arithmetic and copies ran while one was open for 0% of the time, Pallas kernels for 8%

profile of v3, /device:TPU:32, one launch (start us, length us, event | category | flops | bytes accessed | tf_op | source)
XLA Modules:
  0.0 77.4 jit_solution(1921118506530714538)
XLA Ops:
  0.6 6.4 %collective-permute-start = (bf16[4,8192]{1,0:T(4,128)(2,1)}, bf16[4,8192]{1,0:T(4,128)(2,1)S(1)}, u32[]{:S(2)}, u32[]{:S(2)}) collective-permute-start(bf16[4,8192]{1,0:T(4,128)(2,1)} %param.8), channel_id=1, source_target_pairs={{16,0},{17,1},{18,2},{19,3},{20,4},{21,5},{22,6},{23,7},{24,8},{25... | collective-permute-start | bytes 196616 | tf_op jit(solution)/shard_map/ppermute | solution.py:238
  7.0 3.2 %collective-permute-start.1 = (bf16[4,8192]{1,0:T(4,128)(2,1)}, bf16[4,8192]{1,0:T(4,128)(2,1)S(1)}, u32[]{:S(2)}, u32[]{:S(2)}) collective-permute-start(bf16[4,8192]{1,0:T(4,128)(2,1)} %param.8), channel_id=1, source_target_pairs={{10,0},{11,1},{8,2},{9,3},{14,4},{15,5},{12,6},{13,7},{18,8},{19,9... | collective-permute-start | bytes 196616 | tf_op jit(solution)/shard_map/ppermute | solution.py:238
  10.2 2.1 %collective-permute-start.2 = (bf16[4,8192]{1,0:T(4,128)(2,1)}, bf16[4,8192]{1,0:T(4,128)(2,1)S(1)}, u32[]{:S(2)}, u32[]{:S(2)}) collective-permute-start(bf16[4,8192]{1,0:T(4,128)(2,1)} %param.8), channel_id=1, source_target_pairs={{26,0},{27,1},{24,2},{25,3},{30,4},{31,5},{28,6},{29,7},{2,8},{3,9... | collective-permute-start | bytes 196616 | tf_op jit(solution)/shard_map/ppermute | solution.py:238
  13.0 1.2 %copy-done.2 = bf16[64,8192]{1,0:T(8,128)(2,1)S(1)} copy-done((bf16[64,8192]{1,0:T(8,128)(2,1)S(1)}, bf16[64,8192]{1,0:T(8,128)(2,1)}, u32[]{:S(2)}) %copy-start.2) | copy-done | bytes 1048600
  14.3 1.3 %copy-done.4 = bf16[24,112,256]{2,1,0:T(8,128)(2,1)S(1)} copy-done((bf16[24,112,256]{2,1,0:T(8,128)(2,1)S(1)}, bf16[24,112,256]{2,1,0:T(8,128)(2,1)}, u32[]{:S(2)}) %copy-start.4) | copy-done | bytes 1376280
  15.6 2.2 %shift.2.refs_0_.rest_0_ = bf16[576,3072]{1,0:T(8,128)(2,1)S(1)} custom-call(s32[9,64]{1,0:T(8,128)S(1)} %bitcast.3, bf16[64,8192]{1,0:T(8,128)(2,1)S(1)} %copy-done.2, bf16[24,112,256]{2,1,0:T(8,128)(2,1)S(1)} %copy-done.4), custom_call_target="tpu_custom_call" | custom-call | flops 2400000000 | bytes 6291456 | tf_op jit(solution)/shard_map/shift/pallas_call | solution.py:89
  17.8 1.4 %collective-permute-done.2 = bf16[4,8192]{1,0:T(4,128)(2,1)S(1)} collective-permute-done((bf16[4,8192]{1,0:T(4,128)(2,1)}, bf16[4,8192]{1,0:T(4,128)(2,1)S(1)}, u32[]{:S(2)}, u32[]{:S(2)}) %collective-permute-start.2) | collective-permute-done | bytes 65568 | tf_op jit(solution)/shard_map/ppermute | solution.py:238
  19.3 1.7 %collective-permute-start.5 = (bf16[16,8192]{1,0:T(8,128)(2,1)S(1)}, bf16[16,8192]{1,0:T(8,128)(2,1)S(1)}, u32[]{:S(2)}, u32[]{:S(2)}) collective-permute-start(bf16[16,8192]{1,0:T(8,128)(2,1)S(1)} %pad_maximum_fusion.refs_2_), channel_id=1, source_target_pairs={{1,0},{2,1},{3,2},{0,3},{5,4},{6,5},{7,6},{4,7},{9,8},{10,9},{11,1... | collective-permute-start | bytes 786440 | tf_op jit(solution)/shard_map/ppermute | solution.py:241
  21.1 1.0 %collective-permute-start.3 = (bf16[16,8192]{1,0:T(8,128)(2,1)S(1)}, bf16[16,8192]{1,0:T(8,128)(2,1)S(1)}, u32[]{:S(2)}, u32[]{:S(2)}) collective-permute-start(bf16[16,8192]{1,0:T(8,128)(2,1)S(1)} %pad_maximum_fusion.refs_2_), channel_id=1, source_target_pairs={{4,0},{5,1},{6,2},{7,3},{8,4},{9,5},{10,6},{11,7},{12,8},{13,9},{1... | collective-permute-start | bytes 786440 | tf_op jit(solution)/shard_map/ppermute | solution.py:241
  22.1 1.2 %collective-permute-start.4 = (bf16[16,8192]{1,0:T(8,128)(2,1)S(1)}, bf16[16,8192]{1,0:T(8,128)(2,1)S(1)}, u32[]{:S(2)}, u32[]{:S(2)}) collective-permute-start(bf16[16,8192]{1,0:T(8,128)(2,1)S(1)} %pad_maximum_fusion.refs_2_), channel_id=1, source_target_pairs={{28,0},{29,1},{30,2},{31,3},{0,4},{1,5},{2,6},{3,7},{4,8},{5,9},{6... | collective-permute-start | bytes 786440 | tf_op jit(solution)/shard_map/ppermute | solution.py:241
  23.5 2.5 %collective-permute-done.5.refs_5_ = bf16[16,8192]{1,0:T(8,128)(2,1)S(1)} collective-permute-done((bf16[16,8192]{1,0:T(8,128)(2,1)S(1)}, bf16[16,8192]{1,0:T(8,128)(2,1)S(1)}, u32[]{:S(2)}, u32[]{:S(2)}) %collective-permute-start.5) | collective-permute-done | bytes 262176 | tf_op jit(solution)/shard_map/ppermute | solution.py:241
  26.0 1.0 %collective-permute-start.7 = (bf16[16,8192]{1,0:T(8,128)(2,1)S(1)}, bf16[16,8192]{1,0:T(8,128)(2,1)S(1)}, u32[]{:S(2)}, u32[]{:S(2)}) collective-permute-start(bf16[16,8192]{1,0:T(8,128)(2,1)S(1)} %collective-permute-done.5.refs_5_), channel_id=1, source_target_pairs={{4,0},{5,1},{6,2},{7,3},{8,4},{9,5},{10,6},{11,7},{12,8},{13,9},{1... | collective-permute-start | bytes 786440 | tf_op jit(solution)/shard_map/ppermute | solution.py:243
  27.1 1.0 %collective-permute-start.8 = (bf16[16,8192]{1,0:T(8,128)(2,1)S(1)}, bf16[16,8192]{1,0:T(8,128)(2,1)S(1)}, u32[]{:S(2)}, u32[]{:S(2)}) collective-permute-start(bf16[16,8192]{1,0:T(8,128)(2,1)S(1)} %collective-permute-done.5.refs_5_), channel_id=1, source_target_pairs={{28,0},{29,1},{30,2},{31,3},{0,4},{1,5},{2,6},{3,7},{4,8},{5,9},{6... | collective-permute-start | bytes 786440 | tf_op jit(solution)/shard_map/ppermute | solution.py:243
  28.0 1.9 %collective-permute-done.3.refs_3_ = bf16[16,8192]{1,0:T(8,128)(2,1)S(1)} collective-permute-done((bf16[16,8192]{1,0:T(8,128)(2,1)S(1)}, bf16[16,8192]{1,0:T(8,128)(2,1)S(1)}, u32[]{:S(2)}, u32[]{:S(2)}) %collective-permute-start.3) | collective-permute-done | bytes 262176 | tf_op jit(solution)/shard_map/ppermute | solution.py:241
  30.0 1.8 %collective-permute-start.9 = (bf16[16,8192]{1,0:T(8,128)(2,1)S(1)}, bf16[16,8192]{1,0:T(8,128)(2,1)S(1)}, u32[]{:S(2)}, u32[]{:S(2)}) collective-permute-start(bf16[16,8192]{1,0:T(8,128)(2,1)S(1)} %collective-permute-done.5.refs_5_), channel_id=1, source_target_pairs={{1,0},{2,1},{3,2},{0,3},{5,4},{6,5},{7,6},{4,7},{9,8},{10,9},{11,1... | collective-permute-start | bytes 786440 | tf_op jit(solution)/shard_map/ppermute | solution.py:243
  31.7 3.4 %shift.3.refs_1_.rest_1_ = bf16[576,5120]{1,0:T(8,128)(2,1)S(1)} custom-call(s32[9,64]{1,0:T(8,128)S(1)} %bitcast.4, bf16[64,8192]{1,0:T(8,128)(2,1)S(1)} %copy-done.2, bf16[40,112,256]{2,1,0:T(8,128)(2,1)S(1)} %copy-done.3), custom_call_target="tpu_custom_call" | custom-call | flops 4000000000 | bytes 10485760 | tf_op jit(solution)/shard_map/shift/pallas_call | solution.py:89
  35.2 1.1 %collective-permute-done.9.refs_9_ = bf16[16,8192]{1,0:T(8,128)(2,1)S(1)} collective-permute-done((bf16[16,8192]{1,0:T(8,128)(2,1)S(1)}, bf16[16,8192]{1,0:T(8,128)(2,1)S(1)}, u32[]{:S(2)}, u32[]{:S(2)}) %collective-permute-start.9) | collective-permute-done | bytes 262176 | tf_op jit(solution)/shard_map/ppermute | solution.py:243
  36.3 3.0 %score.1 = (f32[128,576]{1,0:T(8,128)S(1)}, f32[2,64]{1,0:T(2,128)S(1)}) custom-call(bf16[576,3072]{1,0:T(8,128)(2,1)S(1)} %shift.2.refs_0_.rest_0_, bf16[576,5120]{1,0:T(8,128)(2,1)S(1)} %shift.3.refs_1_.rest_1_, bf16[16,8192]{1,0:T(8,128)(2,1)S(1)} %pad_maximum_fusion.refs_2_, bf16[16,8192]{1,0:T(8,128)(2,1)S(1)} %collective-permute-done.3.refs_3_, ...), custom_call_target="tpu_custom_call" | custom-call | flops 2000000000 | bytes 12582912 | tf_op jit(solution)/shard_map/score/pallas_call | solution.py:185
  39.4 3.1 %collective-permute-start.11 = (f32[2,64]{1,0:T(2,128)S(1)}, f32[2,64]{1,0:T(2,128)S(1)}, u32[]{:S(2)}, u32[]{:S(2)}) collective-permute-start(f32[2,64]{1,0:T(2,128)S(1)} %get-tuple-element.16.s0), channel_id=1, source_target_pairs={{0,64},{64,0},{1,65},{65,1},{2,66},{66,2},{3,67},{67,3},{4,68},{68... | collective-permute-start | bytes 1544 | tf_op jit(solution)/shard_map/ppermute | solution.py:262
  43.1 1.5 %collective-permute-done.11.s2 = f32[2,64]{1,0:T(2,128)S(1)} collective-permute-done((f32[2,64]{1,0:T(2,128)S(1)}, f32[2,64]{1,0:T(2,128)S(1)}, u32[]{:S(2)}, u32[]{:S(2)}) %collective-permute-start.11) | collective-permute-done | bytes 544 | tf_op jit(solution)/shard_map/ppermute | solution.py:262
  44.6 2.4 %collective-permute-done.12.s3 = f32[2,64]{1,0:T(2,128)S(1)} collective-permute-done((f32[2,64]{1,0:T(2,128)S(1)}, f32[2,64]{1,0:T(2,128)S(1)}, u32[]{:S(2)}, u32[]{:S(2)}) %collective-permute-start.12) | collective-permute-done | bytes 544 | tf_op jit(solution)/shard_map/ppermute | solution.py:263
  47.0 3.7 %insert.1 = (f32[128,1024]{1,0:T(8,128)S(1)}, bf16[128,1024]{1,0:T(8,128)(2,1)S(1)}, f32[1,64]{1,0:T(1,128)}) custom-call(f32[128,576]{1,0:T(8,128)S(1)} %get-tuple-element.15.raised, f32[2,64]{1,0:T(2,128)S(1)} %get-tuple-element.16.s0, f32[2,64]{1,0:T(2,128)S(1)} %collective-permute-done.10.s1, f32[2,64]{1,0:T(2,128)S(1)} %collective-permute-done.11.s2, ...), custom_call_target="tpu_custom_call" | custom-call | flops 3000000000 | bytes 12582912 | tf_op jit(solution)/shard_map/insert/pallas_call | solution.py:221
  50.9 1.4 %collective-permute-done.13 = bf16[128,1024]{1,0:T(8,128)(2,1)S(1)} collective-permute-done((bf16[128,1024]{1,0:T(8,128)(2,1)S(1)}, bf16[128,1024]{1,0:T(8,128)(2,1)S(1)}, u32[]{:S(2)}, u32[]{:S(2)}) %collective-permute-start.13) | collective-permute-done | bytes 262176 | tf_op jit(solution)/shard_map/ppermute | solution.py:266
  52.5 24.1 %all_to_all.5 = bf16[64,2,1024]{2,1,0:T(2,128)(2,1)S(1)} all-to-all(bf16[64,2,1024]{2,1,0:T(2,128)(2,1)S(1)} %reshape.10), channel_id=1, replica_groups=mesh['half'=2,'px'=2,'core'=2,'dom'=32] {'px','dom'}, dimensions={0} | all-to-all | bytes 524288 | tf_op jit(solution)/shard_map/all_to_all | solution.py:268
  (26 shorter events, 2.7 us)
Async XLA Ops:
  0.6 17.1 %collective-permute-start = (bf16[4,8192]{1,0:T(4,128)(2,1)}, bf16[4,8192]{1,0:T(4,128)(2,1)S(1)}, u32[]{:S(2)}, u32[]{:S(2)}) collective-permute-start(bf16[4,8192]{1,0:T(4,128)(2,1)} %param.8), channel_id=1, source_target_pairs={{16,0},{17,1},{18,2},{19,3},{20,4},{21,5},{22,6},{23,7},{24,8},{25... | collective-permute-start | bytes 196616 | tf_op jit(solution)/shard_map/ppermute | solution.py:238
  7.0 10.8 %collective-permute-start.1 = (bf16[4,8192]{1,0:T(4,128)(2,1)}, bf16[4,8192]{1,0:T(4,128)(2,1)S(1)}, u32[]{:S(2)}, u32[]{:S(2)}) collective-permute-start(bf16[4,8192]{1,0:T(4,128)(2,1)} %param.8), channel_id=1, source_target_pairs={{10,0},{11,1},{8,2},{9,3},{14,4},{15,5},{12,6},{13,7},{18,8},{19,9... | collective-permute-start | bytes 196616 | tf_op jit(solution)/shard_map/ppermute | solution.py:238
  10.2 9.0 %collective-permute-start.2 = (bf16[4,8192]{1,0:T(4,128)(2,1)}, bf16[4,8192]{1,0:T(4,128)(2,1)S(1)}, u32[]{:S(2)}, u32[]{:S(2)}) collective-permute-start(bf16[4,8192]{1,0:T(4,128)(2,1)} %param.8), channel_id=1, source_target_pairs={{26,0},{27,1},{24,2},{25,3},{30,4},{31,5},{28,6},{29,7},{2,8},{3,9... | collective-permute-start | bytes 196616 | tf_op jit(solution)/shard_map/ppermute | solution.py:238
  12.3 0.7 copy-start
  13.0 1.2 %copy-start.2 = (bf16[64,8192]{1,0:T(8,128)(2,1)S(1)}, bf16[64,8192]{1,0:T(8,128)(2,1)}, u32[]{:S(2)}) copy-start(bf16[64,8192]{1,0:T(8,128)(2,1)} %image_ref.3) | copy-start | bytes 3145732
  14.3 1.3 %copy-start.4 = (bf16[24,112,256]{2,1,0:T(8,128)(2,1)S(1)}, bf16[24,112,256]{2,1,0:T(8,128)(2,1)}, u32[]{:S(2)}) copy-start(bf16[24,112,256]{2,1,0:T(8,128)(2,1)} %constant.6.clone.table_ref) | copy-start | bytes 4128772
  15.6 3.6 %copy-start.5 = (bf16[4,8192]{1,0:T(4,128)(2,1)S(1)}, bf16[4,8192]{1,0:T(4,128)(2,1)}, u32[]{:S(2)}) copy-start(bf16[4,8192]{1,0:T(4,128)(2,1)} %param.8) | copy-start | bytes 196612
  15.6 16.1 %copy-start.3 = (bf16[40,112,256]{2,1,0:T(8,128)(2,1)S(1)}, bf16[40,112,256]{2,1,0:T(8,128)(2,1)}, u32[]{:S(2)}) copy-start(bf16[40,112,256]{2,1,0:T(8,128)(2,1)} %constant.7.clone.table_ref) | copy-start | bytes 6881284
  19.3 6.7 %collective-permute-start.5 = (bf16[16,8192]{1,0:T(8,128)(2,1)S(1)}, bf16[16,8192]{1,0:T(8,128)(2,1)S(1)}, u32[]{:S(2)}, u32[]{:S(2)}) collective-permute-start(bf16[16,8192]{1,0:T(8,128)(2,1)S(1)} %pad_maximum_fusion.refs_2_), channel_id=1, source_target_pairs={{1,0},{2,1},{3,2},{0,3},{5,4},{6,5},{7,6},{4,7},{9,8},{10,9},{11,1... | collective-permute-start | bytes 786440 | tf_op jit(solution)/shard_map/ppermute | solution.py:241
  21.1 8.9 %collective-permute-start.3 = (bf16[16,8192]{1,0:T(8,128)(2,1)S(1)}, bf16[16,8192]{1,0:T(8,128)(2,1)S(1)}, u32[]{:S(2)}, u32[]{:S(2)}) collective-permute-start(bf16[16,8192]{1,0:T(8,128)(2,1)S(1)} %pad_maximum_fusion.refs_2_), channel_id=1, source_target_pairs={{4,0},{5,1},{6,2},{7,3},{8,4},{9,5},{10,6},{11,7},{12,8},{13,9},{1... | collective-permute-start | bytes 786440 | tf_op jit(solution)/shard_map/ppermute | solution.py:241
  22.1 13.1 %collective-permute-start.4 = (bf16[16,8192]{1,0:T(8,128)(2,1)S(1)}, bf16[16,8192]{1,0:T(8,128)(2,1)S(1)}, u32[]{:S(2)}, u32[]{:S(2)}) collective-permute-start(bf16[16,8192]{1,0:T(8,128)(2,1)S(1)} %pad_maximum_fusion.refs_2_), channel_id=1, source_target_pairs={{28,0},{29,1},{30,2},{31,3},{0,4},{1,5},{2,6},{3,7},{4,8},{5,9},{6... | collective-permute-start | bytes 786440 | tf_op jit(solution)/shard_map/ppermute | solution.py:241
  23.3 11.9 %collective-permute-start.6 = (bf16[16,8192]{1,0:T(8,128)(2,1)S(1)}, bf16[16,8192]{1,0:T(8,128)(2,1)S(1)}, u32[]{:S(2)}, u32[]{:S(2)}) collective-permute-start(bf16[16,8192]{1,0:T(8,128)(2,1)S(1)} %pad_maximum_fusion.refs_2_), channel_id=1, source_target_pairs={{3,0},{0,1},{1,2},{2,3},{7,4},{4,5},{5,6},{6,7},{11,8},{8,9},{9,10... | collective-permute-start | bytes 786440 | tf_op jit(solution)/shard_map/ppermute | solution.py:241
  26.0 9.2 %collective-permute-start.7 = (bf16[16,8192]{1,0:T(8,128)(2,1)S(1)}, bf16[16,8192]{1,0:T(8,128)(2,1)S(1)}, u32[]{:S(2)}, u32[]{:S(2)}) collective-permute-start(bf16[16,8192]{1,0:T(8,128)(2,1)S(1)} %collective-permute-done.5.refs_5_), channel_id=1, source_target_pairs={{4,0},{5,1},{6,2},{7,3},{8,4},{9,5},{10,6},{11,7},{12,8},{13,9},{1... | collective-permute-start | bytes 786440 | tf_op jit(solution)/shard_map/ppermute | solution.py:243
  27.1 8.1 %collective-permute-start.8 = (bf16[16,8192]{1,0:T(8,128)(2,1)S(1)}, bf16[16,8192]{1,0:T(8,128)(2,1)S(1)}, u32[]{:S(2)}, u32[]{:S(2)}) collective-permute-start(bf16[16,8192]{1,0:T(8,128)(2,1)S(1)} %collective-permute-done.5.refs_5_), channel_id=1, source_target_pairs={{28,0},{29,1},{30,2},{31,3},{0,4},{1,5},{2,6},{3,7},{4,8},{5,9},{6... | collective-permute-start | bytes 786440 | tf_op jit(solution)/shard_map/ppermute | solution.py:243
  30.0 6.4 %collective-permute-start.9 = (bf16[16,8192]{1,0:T(8,128)(2,1)S(1)}, bf16[16,8192]{1,0:T(8,128)(2,1)S(1)}, u32[]{:S(2)}, u32[]{:S(2)}) collective-permute-start(bf16[16,8192]{1,0:T(8,128)(2,1)S(1)} %collective-permute-done.5.refs_5_), channel_id=1, source_target_pairs={{1,0},{2,1},{3,2},{0,3},{5,4},{6,5},{7,6},{4,7},{9,8},{10,9},{11,1... | collective-permute-start | bytes 786440 | tf_op jit(solution)/shard_map/ppermute | solution.py:243
  35.1 7.6 %copy-start.1 = (s32[128,8]{0,1:T(8,128)S(1)}, s32[128,8]{0,1:T(8,128)}, u32[]{:S(2)}) copy-start(s32[128,8]{0,1:T(8,128)} %param.9) | copy-start | bytes 12292
  39.4 3.7 %collective-permute-start.10 = (f32[2,64]{1,0:T(2,128)S(1)}, f32[2,64]{1,0:T(2,128)S(1)}, u32[]{:S(2)}, u32[]{:S(2)}) collective-permute-start(f32[2,64]{1,0:T(2,128)S(1)} %get-tuple-element.16.s0), channel_id=1, source_target_pairs={{0,32},{32,0},{1,33},{33,1},{2,34},{34,2},{3,35},{35,3},{4,36},{36... | collective-permute-start | bytes 1544 | tf_op jit(solution)/shard_map/ppermute | solution.py:261
  39.4 5.2 %collective-permute-start.11 = (f32[2,64]{1,0:T(2,128)S(1)}, f32[2,64]{1,0:T(2,128)S(1)}, u32[]{:S(2)}, u32[]{:S(2)}) collective-permute-start(f32[2,64]{1,0:T(2,128)S(1)} %get-tuple-element.16.s0), channel_id=1, source_target_pairs={{0,64},{64,0},{1,65},{65,1},{2,66},{66,2},{3,67},{67,3},{4,68},{68... | collective-permute-start | bytes 1544 | tf_op jit(solution)/shard_map/ppermute | solution.py:262
  42.5 4.5 %collective-permute-start.12 = (f32[2,64]{1,0:T(2,128)S(1)}, f32[2,64]{1,0:T(2,128)S(1)}, u32[]{:S(2)}, u32[]{:S(2)}) collective-permute-start(f32[2,64]{1,0:T(2,128)S(1)} %get-tuple-element.16.s0), channel_id=1, source_target_pairs={{0,96},{32,64},{64,32},{96,0},{1,97},{33,65},{65,33},{97,1},{2,98}... | collective-permute-start | bytes 1544 | tf_op jit(solution)/shard_map/ppermute | solution.py:263
  50.8 1.5 %collective-permute-start.13 = (bf16[128,1024]{1,0:T(8,128)(2,1)S(1)}, bf16[128,1024]{1,0:T(8,128)(2,1)S(1)}, u32[]{:S(2)}, u32[]{:S(2)}) collective-permute-start(bf16[128,1024]{1,0:T(8,128)(2,1)S(1)} %get-tuple-element.18), channel_id=1, source_target_pairs={{0,32},{32,0},{1,33},{33,1},{2,34},{34,2},{3,35},{35,3},{4,36},{36... | collective-permute-start | bytes 786440 | tf_op jit(solution)/shard_map/ppermute | solution.py:266

commit v4 on v3

--- a/solution.py
+++ b/solution.py
@@ -15,7 +15,7 @@
 GRID = 7
 OFFS = GRID * GRID
 KPAD = 112
-CUT = 24
+CUT = 16
 Z, Y = 8, 4
 SEG = 8
 BLK = 1024
@@ -122,7 +122,7 @@
     m = lax.broadcasted_iota(jnp.int32, (VB, count), 0)
     half = m % (VB // 2)
     owner = jnp.where(m < VB // 2, core, 1 - core)
-    block = half // (VB // 4) * (VB // 2) + owner * (VB // 4) + half % (VB // 4)
+    block = (half // 2) % 2 * (VB // 2) + owner * (VB // 4) + half // 4 * 2 + half % 2
     for s in range(SEG):
         hot_ref[s] = jnp.where(block == slots[s : s + 1, :], 1.0, 0.0).astype(BF16)
 
@@ -258,14 +258,14 @@
     swap = [(0, 1), (1, 0)]
     everyone = [
         stats,
+        lax.ppermute(stats, ("px", "core"), [(i, 3 - i) for i in range(4)]),
+        lax.ppermute(stats, "px", swap),
         lax.ppermute(stats, "core", swap),
-        lax.ppermute(stats, "px", swap),
-        lax.ppermute(stats, ("px", "core"), [(i, 3 - i) for i in range(4)]),
     ]
     mine, other, evidence = insert(raised, everyone, hot, moved, scale)
     paired = mine + lax.ppermute(other, "core", swap).astype(F32)
     sent = paired.astype(BF16).reshape(2 * Z * Y, VB // (4 * Z * Y), BLK)
-    arrived = lax.all_to_all(sent, ("px", "dom"), 0, 0, tiled=True)
+    arrived = lax.all_to_all(sent, ("dom", "px"), 0, 0, tiled=True)
     return (jnp.sum(arrived.astype(F32), axis=0), evidence.reshape(rows))
 
 

time: 78.1 us -> 76.2 us (0.976)
  waiting for transfers between devices: 12.3 us -> 9.09 us
  starting transfers between devices: 23.2 us -> 24.9 us
    ppermute x1, starting transfers between devices: 0.15 us -> 1.88 us  [shards(): paired = mine + lax.ppermute(other, 'core', swap).astype(F32)]
    ppermute x1, waiting for transfers between devices: 2.45 us -> 0.87 us  [shards(): lax.ppermute(stats, ('px', 'core'), [(i, 3 - i) for i in range(4)])]
    ppermute x1, waiting for transfers between devices: 1.51 us -> 0.67 us  [shards(): lax.ppermute(stats, 'px', swap)]
where the time goes in v4:
time: 76.2 us; the launch traced here: 75.9 us
  starting transfers between devices  24.9 us (33%)
  blocking collectives  24.3 us (32%)
  Pallas kernels  12.7 us (17%)
  waiting for transfers between devices  9.09 us (12%)
  local copies, waits for them, and re-layouts  3.21 us (4%)
  other arithmetic  1.05 us (1%)
    all_to_all x1, blocking collectives, shards(): arrived = lax.all_to_all(sent, ('dom', 'px'), 0, 0, tiled=True)  24.3 us
    ppermute x3, starting transfers between devices, gather(): far = [lax.ppermute(references, 'dom', receive_from(*d)) for d in FAR[1:]]  11.7 us
    pallas_call x2, Pallas kernels, shift_images(): pl.pallas_call(functools.partial(shift_kernel, start), in_specs=[VMEM] *...  5.57 us
    ppermute x4, starting transfers between devices, gather(): first = [lax.ppermute(own, 'dom', receive_from(*d)) for d in NEAR[1:5]]  4.13 us
    ppermute x3, starting transfers between devices, gather(): lax.ppermute(up, 'dom', receive_from(*d))  3.8 us
    pallas_call x1, Pallas kernels, insert(): pl.pallas_call(functools.partial(insert_kernel, scale), in_specs=[VMEM] *...  3.79 us
    ppermute x4, waiting for transfers between devices, gather(): first = [lax.ppermute(own, 'dom', receive_from(*d)) for d in NEAR[1:5]]  3.69 us
    unnamed x12, local copies, waits for them, and re-layouts  3.11 us
  transfers between devices with their start and end apart: 14, of which 7 were waited for; matrix products, arithmetic and copies ran while one was open for 0% of the time, Pallas kernels for 8%

profile of v4, /device:TPU:32, one launch (start us, length us, event | category | flops | bytes accessed | tf_op | source)
XLA Modules:
  0.0 75.9 jit_solution(7209467386003024320)
XLA Ops:
  0.6 6.4 %collective-permute-start = (bf16[4,8192]{1,0:T(4,128)(2,1)}, bf16[4,8192]{1,0:T(4,128)(2,1)S(1)}, u32[]{:S(2)}, u32[]{:S(2)}) collective-permute-start(bf16[4,8192]{1,0:T(4,128)(2,1)} %param.8), channel_id=1, source_target_pairs={{16,0},{17,1},{18,2},{19,3},{20,4},{21,5},{22,6},{23,7},{24,8},{25... | collective-permute-start | bytes 196616 | tf_op jit(solution)/shard_map/ppermute | solution.py:238
  7.0 3.2 %collective-permute-start.1 = (bf16[4,8192]{1,0:T(4,128)(2,1)}, bf16[4,8192]{1,0:T(4,128)(2,1)S(1)}, u32[]{:S(2)}, u32[]{:S(2)}) collective-permute-start(bf16[4,8192]{1,0:T(4,128)(2,1)} %param.8), channel_id=1, source_target_pairs={{10,0},{11,1},{8,2},{9,3},{14,4},{15,5},{12,6},{13,7},{18,8},{19,9... | collective-permute-start | bytes 196616 | tf_op jit(solution)/shard_map/ppermute | solution.py:238
  10.2 2.1 %collective-permute-start.2 = (bf16[4,8192]{1,0:T(4,128)(2,1)}, bf16[4,8192]{1,0:T(4,128)(2,1)S(1)}, u32[]{:S(2)}, u32[]{:S(2)}) collective-permute-start(bf16[4,8192]{1,0:T(4,128)(2,1)} %param.8), channel_id=1, source_target_pairs={{26,0},{27,1},{24,2},{25,3},{30,4},{31,5},{28,6},{29,7},{2,8},{3,9... | collective-permute-start | bytes 196616 | tf_op jit(solution)/shard_map/ppermute | solution.py:238
  12.3 0.7 copy-done
  13.0 1.2 %copy-done.2 = bf16[64,8192]{1,0:T(8,128)(2,1)S(1)} copy-done((bf16[64,8192]{1,0:T(8,128)(2,1)S(1)}, bf16[64,8192]{1,0:T(8,128)(2,1)}, u32[]{:S(2)}) %copy-start.2) | copy-done | bytes 1048600
  14.3 1.2 %copy-done.4 = bf16[16,112,256]{2,1,0:T(8,128)(2,1)S(1)} copy-done((bf16[16,112,256]{2,1,0:T(8,128)(2,1)S(1)}, bf16[16,112,256]{2,1,0:T(8,128)(2,1)}, u32[]{:S(2)}) %copy-start.4) | copy-done | bytes 917528
  15.4 1.6 %shift.2.refs_0_.rest_0_ = bf16[576,2048]{1,0:T(8,128)(2,1)S(1)} custom-call(s32[9,64]{1,0:T(8,128)S(1)} %bitcast.3, bf16[64,8192]{1,0:T(8,128)(2,1)S(1)} %copy-done.2, bf16[16,112,256]{2,1,0:T(8,128)(2,1)S(1)} %copy-done.4), custom_call_target="tpu_custom_call" | custom-call | flops 1600000000 | bytes 4194304 | tf_op jit(solution)/shard_map/shift/pallas_call | solution.py:89
  17.0 2.2 %collective-permute-done.2 = bf16[4,8192]{1,0:T(4,128)(2,1)S(1)} collective-permute-done((bf16[4,8192]{1,0:T(4,128)(2,1)}, bf16[4,8192]{1,0:T(4,128)(2,1)S(1)}, u32[]{:S(2)}, u32[]{:S(2)}) %collective-permute-start.2) | collective-permute-done | bytes 65568 | tf_op jit(solution)/shard_map/ppermute | solution.py:238
  19.3 1.5 %collective-permute-start.5 = (bf16[16,8192]{1,0:T(8,128)(2,1)S(1)}, bf16[16,8192]{1,0:T(8,128)(2,1)S(1)}, u32[]{:S(2)}, u32[]{:S(2)}) collective-permute-start(bf16[16,8192]{1,0:T(8,128)(2,1)S(1)} %pad_maximum_fusion.refs_2_), channel_id=1, source_target_pairs={{1,0},{2,1},{3,2},{0,3},{5,4},{6,5},{7,6},{4,7},{9,8},{10,9},{11,1... | collective-permute-start | bytes 786440 | tf_op jit(solution)/shard_map/ppermute | solution.py:241
  21.3 1.5 %collective-permute-start.4 = (bf16[16,8192]{1,0:T(8,128)(2,1)S(1)}, bf16[16,8192]{1,0:T(8,128)(2,1)S(1)}, u32[]{:S(2)}, u32[]{:S(2)}) collective-permute-start(bf16[16,8192]{1,0:T(8,128)(2,1)S(1)} %pad_maximum_fusion.refs_2_), channel_id=1, source_target_pairs={{28,0},{29,1},{30,2},{31,3},{0,4},{1,5},{2,6},{3,7},{4,8},{5,9},{6... | collective-permute-start | bytes 786440 | tf_op jit(solution)/shard_map/ppermute | solution.py:241
  23.5 2.5 %collective-permute-done.5.refs_5_ = bf16[16,8192]{1,0:T(8,128)(2,1)S(1)} collective-permute-done((bf16[16,8192]{1,0:T(8,128)(2,1)S(1)}, bf16[16,8192]{1,0:T(8,128)(2,1)S(1)}, u32[]{:S(2)}, u32[]{:S(2)}) %collective-permute-start.5) | collective-permute-done | bytes 262176 | tf_op jit(solution)/shard_map/ppermute | solution.py:241
  26.0 1.0 %collective-permute-start.7 = (bf16[16,8192]{1,0:T(8,128)(2,1)S(1)}, bf16[16,8192]{1,0:T(8,128)(2,1)S(1)}, u32[]{:S(2)}, u32[]{:S(2)}) collective-permute-start(bf16[16,8192]{1,0:T(8,128)(2,1)S(1)} %collective-permute-done.5.refs_5_), channel_id=1, source_target_pairs={{4,0},{5,1},{6,2},{7,3},{8,4},{9,5},{10,6},{11,7},{12,8},{13,9},{1... | collective-permute-start | bytes 786440 | tf_op jit(solution)/shard_map/ppermute | solution.py:243
  27.1 1.0 %collective-permute-start.8 = (bf16[16,8192]{1,0:T(8,128)(2,1)S(1)}, bf16[16,8192]{1,0:T(8,128)(2,1)S(1)}, u32[]{:S(2)}, u32[]{:S(2)}) collective-permute-start(bf16[16,8192]{1,0:T(8,128)(2,1)S(1)} %collective-permute-done.5.refs_5_), channel_id=1, source_target_pairs={{28,0},{29,1},{30,2},{31,3},{0,4},{1,5},{2,6},{3,7},{4,8},{5,9},{6... | collective-permute-start | bytes 786440 | tf_op jit(solution)/shard_map/ppermute | solution.py:243
  28.0 1.1 %collective-permute-done.3.refs_3_ = bf16[16,8192]{1,0:T(8,128)(2,1)S(1)} collective-permute-done((bf16[16,8192]{1,0:T(8,128)(2,1)S(1)}, bf16[16,8192]{1,0:T(8,128)(2,1)S(1)}, u32[]{:S(2)}, u32[]{:S(2)}) %collective-permute-start.3) | collective-permute-done | bytes 262176 | tf_op jit(solution)/shard_map/ppermute | solution.py:241
  29.2 1.8 %collective-permute-start.9 = (bf16[16,8192]{1,0:T(8,128)(2,1)S(1)}, bf16[16,8192]{1,0:T(8,128)(2,1)S(1)}, u32[]{:S(2)}, u32[]{:S(2)}) collective-permute-start(bf16[16,8192]{1,0:T(8,128)(2,1)S(1)} %collective-permute-done.5.refs_5_), channel_id=1, source_target_pairs={{1,0},{2,1},{3,2},{0,3},{5,4},{6,5},{7,6},{4,7},{9,8},{10,9},{11,1... | collective-permute-start | bytes 786440 | tf_op jit(solution)/shard_map/ppermute | solution.py:243
  31.0 4.0 %shift.3.refs_1_.rest_1_ = bf16[576,6144]{1,0:T(8,128)(2,1)S(1)} custom-call(s32[9,64]{1,0:T(8,128)S(1)} %bitcast.4, bf16[64,8192]{1,0:T(8,128)(2,1)S(1)} %copy-done.2, bf16[48,112,256]{2,1,0:T(8,128)(2,1)S(1)} %copy-done.3), custom_call_target="tpu_custom_call" | custom-call | flops 4800000000 | bytes 12582912 | tf_op jit(solution)/shard_map/shift/pallas_call | solution.py:89
  35.6 3.0 %score.1 = (f32[128,576]{1,0:T(8,128)S(1)}, f32[2,64]{1,0:T(2,128)S(1)}) custom-call(bf16[576,2048]{1,0:T(8,128)(2,1)S(1)} %shift.2.refs_0_.rest_0_, bf16[576,6144]{1,0:T(8,128)(2,1)S(1)} %shift.3.refs_1_.rest_1_, bf16[16,8192]{1,0:T(8,128)(2,1)S(1)} %pad_maximum_fusion.refs_2_, bf16[16,8192]{1,0:T(8,128)(2,1)S(1)} %collective-permute-done.3.refs_3_, ...), custom_call_target="tpu_custom_call" | custom-call | flops 2000000000 | bytes 12582912 | tf_op jit(solution)/shard_map/score/pallas_call | solution.py:185
  38.7 3.1 %collective-permute-start.11 = (f32[2,64]{1,0:T(2,128)S(1)}, f32[2,64]{1,0:T(2,128)S(1)}, u32[]{:S(2)}, u32[]{:S(2)}) collective-permute-start(f32[2,64]{1,0:T(2,128)S(1)} %get-tuple-element.16.s0), channel_id=1, source_target_pairs={{0,64},{64,0},{1,65},{65,1},{2,66},{66,2},{3,67},{67,3},{4,68},{68... | collective-permute-start | bytes 1544 | tf_op jit(solution)/shard_map/ppermute | solution.py:262
  42.3 0.9 %collective-permute-done.10.s1 = f32[2,64]{1,0:T(2,128)S(1)} collective-permute-done((f32[2,64]{1,0:T(2,128)S(1)}, f32[2,64]{1,0:T(2,128)S(1)}, u32[]{:S(2)}, u32[]{:S(2)}) %collective-permute-start.10) | collective-permute-done | bytes 544 | tf_op jit(solution)/shard_map/ppermute | solution.py:261
  43.8 3.8 %insert.1 = (f32[128,1024]{1,0:T(8,128)S(1)}, bf16[128,1024]{1,0:T(8,128)(2,1)S(1)}, f32[1,64]{1,0:T(1,128)}) custom-call(f32[128,576]{1,0:T(8,128)S(1)} %get-tuple-element.15.raised, f32[2,64]{1,0:T(2,128)S(1)} %get-tuple-element.16.s0, f32[2,64]{1,0:T(2,128)S(1)} %collective-permute-done.10.s1, f32[2,64]{1,0:T(2,128)S(1)} %collective-permute-done.11.s2, ...), custom_call_target="tpu_custom_call" | custom-call | flops 3000000000 | bytes 12582912 | tf_op jit(solution)/shard_map/insert/pallas_call | solution.py:221
  47.6 1.9 %collective-permute-start.13 = (bf16[128,1024]{1,0:T(8,128)(2,1)S(1)}, bf16[128,1024]{1,0:T(8,128)(2,1)S(1)}, u32[]{:S(2)}, u32[]{:S(2)}) collective-permute-start(bf16[128,1024]{1,0:T(8,128)(2,1)S(1)} %get-tuple-element.18), channel_id=1, source_target_pairs={{0,32},{32,0},{1,33},{33,1},{2,34},{34,2},{3,35},{35,3},{4,36},{36... | collective-permute-start | bytes 786440 | tf_op jit(solution)/shard_map/ppermute | solution.py:266
  49.5 1.2 %collective-permute-done.13 = bf16[128,1024]{1,0:T(8,128)(2,1)S(1)} collective-permute-done((bf16[128,1024]{1,0:T(8,128)(2,1)S(1)}, bf16[128,1024]{1,0:T(8,128)(2,1)S(1)}, u32[]{:S(2)}, u32[]{:S(2)}) %collective-permute-start.13) | collective-permute-done | bytes 262176 | tf_op jit(solution)/shard_map/ppermute | solution.py:266
  50.8 24.3 %all_to_all.5 = bf16[64,2,1024]{2,1,0:T(2,128)(2,1)S(1)} all-to-all(bf16[64,2,1024]{2,1,0:T(2,128)(2,1)S(1)} %reshape.10), channel_id=1, replica_groups=mesh['half'=2,'px'=2,'core'=2,'dom'=32] {'dom','px'}, dimensions={0} | all-to-all | bytes 524288 | tf_op jit(solution)/shard_map/all_to_all | solution.py:268
  75.1 0.8 %convert_reduce_fusion = f32[2,1024]{1,0:T(2,128)} fusion(bf16[64,2,1024]{2,1,0:T(2,128)(2,1)S(1)} %all_to_all.5), kind=kLoop, calls=%fused_computation | loop fusion | flops 260096 | bytes 270336 | tf_op jit(solution)/shard_map/reduce_sum | solution.py:269
  (26 shorter events, 3.2 us)
Async XLA Ops:
  0.6 16.4 %collective-permute-start = (bf16[4,8192]{1,0:T(4,128)(2,1)}, bf16[4,8192]{1,0:T(4,128)(2,1)S(1)}, u32[]{:S(2)}, u32[]{:S(2)}) collective-permute-start(bf16[4,8192]{1,0:T(4,128)(2,1)} %param.8), channel_id=1, source_target_pairs={{16,0},{17,1},{18,2},{19,3},{20,4},{21,5},{22,6},{23,7},{24,8},{25... | collective-permute-start | bytes 196616 | tf_op jit(solution)/shard_map/ppermute | solution.py:238
  7.0 10.0 %collective-permute-start.1 = (bf16[4,8192]{1,0:T(4,128)(2,1)}, bf16[4,8192]{1,0:T(4,128)(2,1)S(1)}, u32[]{:S(2)}, u32[]{:S(2)}) collective-permute-start(bf16[4,8192]{1,0:T(4,128)(2,1)} %param.8), channel_id=1, source_target_pairs={{10,0},{11,1},{8,2},{9,3},{14,4},{15,5},{12,6},{13,7},{18,8},{19,9... | collective-permute-start | bytes 196616 | tf_op jit(solution)/shard_map/ppermute | solution.py:238
  10.2 9.0 %collective-permute-start.2 = (bf16[4,8192]{1,0:T(4,128)(2,1)}, bf16[4,8192]{1,0:T(4,128)(2,1)S(1)}, u32[]{:S(2)}, u32[]{:S(2)}) collective-permute-start(bf16[4,8192]{1,0:T(4,128)(2,1)} %param.8), channel_id=1, source_target_pairs={{26,0},{27,1},{24,2},{25,3},{30,4},{31,5},{28,6},{29,7},{2,8},{3,9... | collective-permute-start | bytes 196616 | tf_op jit(solution)/shard_map/ppermute | solution.py:238
  12.3 0.7 copy-start
  13.0 1.2 %copy-start.2 = (bf16[64,8192]{1,0:T(8,128)(2,1)S(1)}, bf16[64,8192]{1,0:T(8,128)(2,1)}, u32[]{:S(2)}) copy-start(bf16[64,8192]{1,0:T(8,128)(2,1)} %image_ref.3) | copy-start | bytes 3145732
  14.3 1.2 %copy-start.4 = (bf16[16,112,256]{2,1,0:T(8,128)(2,1)S(1)}, bf16[16,112,256]{2,1,0:T(8,128)(2,1)}, u32[]{:S(2)}) copy-start(bf16[16,112,256]{2,1,0:T(8,128)(2,1)} %constant.6.clone.table_ref) | copy-start | bytes 2752516
  15.4 3.7 %copy-start.5 = (bf16[4,8192]{1,0:T(4,128)(2,1)S(1)}, bf16[4,8192]{1,0:T(4,128)(2,1)}, u32[]{:S(2)}) copy-start(bf16[4,8192]{1,0:T(4,128)(2,1)} %param.8) | copy-start | bytes 196612
  15.4 15.5 %copy-start.3 = (bf16[48,112,256]{2,1,0:T(8,128)(2,1)S(1)}, bf16[48,112,256]{2,1,0:T(8,128)(2,1)}, u32[]{:S(2)}) copy-start(bf16[48,112,256]{2,1,0:T(8,128)(2,1)} %constant.7.clone.table_ref) | copy-start | bytes 8257540
  19.3 6.7 %collective-permute-start.5 = (bf16[16,8192]{1,0:T(8,128)(2,1)S(1)}, bf16[16,8192]{1,0:T(8,128)(2,1)S(1)}, u32[]{:S(2)}, u32[]{:S(2)}) collective-permute-start(bf16[16,8192]{1,0:T(8,128)(2,1)S(1)} %pad_maximum_fusion.refs_2_), channel_id=1, source_target_pairs={{1,0},{2,1},{3,2},{0,3},{5,4},{6,5},{7,6},{4,7},{9,8},{10,9},{11,1... | collective-permute-start | bytes 786440 | tf_op jit(solution)/shard_map/ppermute | solution.py:241
  20.8 8.4 %collective-permute-start.3 = (bf16[16,8192]{1,0:T(8,128)(2,1)S(1)}, bf16[16,8192]{1,0:T(8,128)(2,1)S(1)}, u32[]{:S(2)}, u32[]{:S(2)}) collective-permute-start(bf16[16,8192]{1,0:T(8,128)(2,1)S(1)} %pad_maximum_fusion.refs_2_), channel_id=1, source_target_pairs={{4,0},{5,1},{6,2},{7,3},{8,4},{9,5},{10,6},{11,7},{12,8},{13,9},{1... | collective-permute-start | bytes 786440 | tf_op jit(solution)/shard_map/ppermute | solution.py:241
  21.3 13.7 %collective-permute-start.4 = (bf16[16,8192]{1,0:T(8,128)(2,1)S(1)}, bf16[16,8192]{1,0:T(8,128)(2,1)S(1)}, u32[]{:S(2)}, u32[]{:S(2)}) collective-permute-start(bf16[16,8192]{1,0:T(8,128)(2,1)S(1)} %pad_maximum_fusion.refs_2_), channel_id=1, source_target_pairs={{28,0},{29,1},{30,2},{31,3},{0,4},{1,5},{2,6},{3,7},{4,8},{5,9},{6... | collective-permute-start | bytes 786440 | tf_op jit(solution)/shard_map/ppermute | solution.py:241
  22.9 12.2 %collective-permute-start.6 = (bf16[16,8192]{1,0:T(8,128)(2,1)S(1)}, bf16[16,8192]{1,0:T(8,128)(2,1)S(1)}, u32[]{:S(2)}, u32[]{:S(2)}) collective-permute-start(bf16[16,8192]{1,0:T(8,128)(2,1)S(1)} %pad_maximum_fusion.refs_2_), channel_id=1, source_target_pairs={{3,0},{0,1},{1,2},{2,3},{7,4},{4,5},{5,6},{6,7},{11,8},{8,9},{9,10... | collective-permute-start | bytes 786440 | tf_op jit(solution)/shard_map/ppermute | solution.py:241
  26.0 9.0 %collective-permute-start.7 = (bf16[16,8192]{1,0:T(8,128)(2,1)S(1)}, bf16[16,8192]{1,0:T(8,128)(2,1)S(1)}, u32[]{:S(2)}, u32[]{:S(2)}) collective-permute-start(bf16[16,8192]{1,0:T(8,128)(2,1)S(1)} %collective-permute-done.5.refs_5_), channel_id=1, source_target_pairs={{4,0},{5,1},{6,2},{7,3},{8,4},{9,5},{10,6},{11,7},{12,8},{13,9},{1... | collective-permute-start | bytes 786440 | tf_op jit(solution)/shard_map/ppermute | solution.py:243
  27.1 8.0 %collective-permute-start.8 = (bf16[16,8192]{1,0:T(8,128)(2,1)S(1)}, bf16[16,8192]{1,0:T(8,128)(2,1)S(1)}, u32[]{:S(2)}, u32[]{:S(2)}) collective-permute-start(bf16[16,8192]{1,0:T(8,128)(2,1)S(1)} %collective-permute-done.5.refs_5_), channel_id=1, source_target_pairs={{28,0},{29,1},{30,2},{31,3},{0,4},{1,5},{2,6},{3,7},{4,8},{5,9},{6... | collective-permute-start | bytes 786440 | tf_op jit(solution)/shard_map/ppermute | solution.py:243
  29.2 6.4 %collective-permute-start.9 = (bf16[16,8192]{1,0:T(8,128)(2,1)S(1)}, bf16[16,8192]{1,0:T(8,128)(2,1)S(1)}, u32[]{:S(2)}, u32[]{:S(2)}) collective-permute-start(bf16[16,8192]{1,0:T(8,128)(2,1)S(1)} %collective-permute-done.5.refs_5_), channel_id=1, source_target_pairs={{1,0},{2,1},{3,2},{0,3},{5,4},{6,5},{7,6},{4,7},{9,8},{10,9},{11,1... | collective-permute-start | bytes 786440 | tf_op jit(solution)/shard_map/ppermute | solution.py:243
  35.0 7.0 %copy-start.1 = (s32[128,8]{0,1:T(8,128)S(1)}, s32[128,8]{0,1:T(8,128)}, u32[]{:S(2)}) copy-start(s32[128,8]{0,1:T(8,128)} %param.9) | copy-start | bytes 12292
  38.6 4.5 %collective-permute-start.10 = (f32[2,64]{1,0:T(2,128)S(1)}, f32[2,64]{1,0:T(2,128)S(1)}, u32[]{:S(2)}, u32[]{:S(2)}) collective-permute-start(f32[2,64]{1,0:T(2,128)S(1)} %get-tuple-element.16.s0), channel_id=1, source_target_pairs={{0,96},{32,64},{64,32},{96,0},{1,97},{33,65},{65,33},{97,1},{2,98}... | collective-permute-start | bytes 1544 | tf_op jit(solution)/shard_map/ppermute | solution.py:261
  38.7 5.2 %collective-permute-start.11 = (f32[2,64]{1,0:T(2,128)S(1)}, f32[2,64]{1,0:T(2,128)S(1)}, u32[]{:S(2)}, u32[]{:S(2)}) collective-permute-start(f32[2,64]{1,0:T(2,128)S(1)} %get-tuple-element.16.s0), channel_id=1, source_target_pairs={{0,64},{64,0},{1,65},{65,1},{2,66},{66,2},{3,67},{67,3},{4,68},{68... | collective-permute-start | bytes 1544 | tf_op jit(solution)/shard_map/ppermute | solution.py:262
  41.8 2.1 %collective-permute-start.12 = (f32[2,64]{1,0:T(2,128)S(1)}, f32[2,64]{1,0:T(2,128)S(1)}, u32[]{:S(2)}, u32[]{:S(2)}) collective-permute-start(f32[2,64]{1,0:T(2,128)S(1)} %get-tuple-element.16.s0), channel_id=1, source_target_pairs={{0,32},{32,0},{1,33},{33,1},{2,34},{34,2},{3,35},{35,3},{4,36},{36... | collective-permute-start | bytes 1544 | tf_op jit(solution)/shard_map/ppermute | solution.py:263
  47.6 3.0 %collective-permute-start.13 = (bf16[128,1024]{1,0:T(8,128)(2,1)S(1)}, bf16[128,1024]{1,0:T(8,128)(2,1)S(1)}, u32[]{:S(2)}, u32[]{:S(2)}) collective-permute-start(bf16[128,1024]{1,0:T(8,128)(2,1)S(1)} %get-tuple-element.18), channel_id=1, source_target_pairs={{0,32},{32,0},{1,33},{33,1},{2,34},{34,2},{3,35},{35,3},{4,36},{36... | collective-permute-start | bytes 786440 | tf_op jit(solution)/shard_map/ppermute | solution.py:266

commit v5 on v4

--- a/solution.py
+++ b/solution.py
@@ -30,7 +30,7 @@
 
 
 FAR = ((0, 0), (4, 0), (2, 2), (-2, 2))
-NEAR = ((0, 0), (1, 0), (-1, 0), (0, 1), (0, -1), (1, 1), (-1, 1), (0, 2))
+NEAR = ((0, 0), (1, 0), (-1, 0), (0, 1), (0, -1), (-2, 0), (-1, 1), (-1, -1))
 
 
 def receive_from(dz, dy):
@@ -239,8 +239,8 @@
     far, early = lax.optimization_barrier((far, early()))
     own = jnp.concatenate([references, *far], axis=0)
     first = [lax.ppermute(own, "dom", receive_from(*d)) for d in NEAR[1:5]]
-    up = first[2]
-    second = [lax.ppermute(up, "dom", receive_from(*d)) for d in ((1, 0), (-1, 0), (0, 1))]
+    up = first[1]
+    second = [lax.ppermute(up, "dom", receive_from(*d)) for d in ((-1, 0), (0, 1), (0, -1))]
     return [own, *first, *second], (early, late())
 
 

time: 76.2 us -> 75.6 us (level)
  blocking collectives: 24.3 us -> 22 us
  waiting for transfers between devices: 9.09 us -> 10.9 us
    ppermute x3, waiting for transfers between devices: 0.53 us -> 3.49 us  [gather(): lax.ppermute(up, 'dom', receive_from(*d))]
    all_to_all x1, blocking collectives: 24.3 us -> 22 us  [shards(): arrived = lax.all_to_all(sent, ('dom', 'px'), 0, 0, tiled=True)]
    ppermute x4, waiting for transfers between devices: 3.69 us -> 2.56 us  [gather(): first = [lax.ppermute(own, 'dom', receive_from(*d)) for d in NEAR[1:5]]]
  transfers between devices with their start and end apart: 14 -> 14, of which waited for: 7 -> 6; matrix products, arithmetic and copies ran while one was open for 0% -> 0% of each run, Pallas kernels for 8% -> 8%
where the time goes in v5:
time: 75.6 us; the launch traced here: 75.4 us
  starting transfers between devices  24.8 us (33%)
  blocking collectives  22 us (29%)
  Pallas kernels  12.7 us (17%)
  waiting for transfers between devices  10.9 us (14%)
  local copies, waits for them, and re-layouts  3.21 us (4%)
  other arithmetic  1.05 us (1%)
    all_to_all x1, blocking collectives, shards(): arrived = lax.all_to_all(sent, ('dom', 'px'), 0, 0, tiled=True)  22 us
    ppermute x3, starting transfers between devices, gather(): far = [lax.ppermute(references, 'dom', receive_from(*d)) for d in FAR[1:]]  11.7 us
    pallas_call x2, Pallas kernels, shift_images(): pl.pallas_call(functools.partial(shift_kernel, start), in_specs=[VMEM] *...  5.58 us
    ppermute x4, starting transfers between devices, gather(): first = [lax.ppermute(own, 'dom', receive_from(*d)) for d in NEAR[1:5]]  4.13 us
    pallas_call x1, Pallas kernels, insert(): pl.pallas_call(functools.partial(insert_kernel, scale), in_specs=[VMEM] *...  3.79 us
    ppermute x3, starting transfers between devices, gather(): lax.ppermute(up, 'dom', receive_from(*d))  3.72 us
    ppermute x3, waiting for transfers between devices, gather(): lax.ppermute(up, 'dom', receive_from(*d))  3.49 us
    unnamed x12, local copies, waits for them, and re-layouts  3.11 us
  transfers between devices with their start and end apart: 14, of which 6 were waited for; matrix products, arithmetic and copies ran while one was open for 0% of the time, Pallas kernels for 8%

profile of v5, /device:TPU:32, one launch (start us, length us, event | category | flops | bytes accessed | tf_op | source)
XLA Modules:
  0.0 75.4 jit_solution(2391645543941289310)
XLA Ops:
  0.6 6.4 %collective-permute-start = (bf16[4,8192]{1,0:T(4,128)(2,1)}, bf16[4,8192]{1,0:T(4,128)(2,1)S(1)}, u32[]{:S(2)}, u32[]{:S(2)}) collective-permute-start(bf16[4,8192]{1,0:T(4,128)(2,1)} %param.8), channel_id=1, source_target_pairs={{16,0},{17,1},{18,2},{19,3},{20,4},{21,5},{22,6},{23,7},{24,8},{25... | collective-permute-start | bytes 196616 | tf_op jit(solution)/shard_map/ppermute | solution.py:238
  7.0 3.2 %collective-permute-start.1 = (bf16[4,8192]{1,0:T(4,128)(2,1)}, bf16[4,8192]{1,0:T(4,128)(2,1)S(1)}, u32[]{:S(2)}, u32[]{:S(2)}) collective-permute-start(bf16[4,8192]{1,0:T(4,128)(2,1)} %param.8), channel_id=1, source_target_pairs={{10,0},{11,1},{8,2},{9,3},{14,4},{15,5},{12,6},{13,7},{18,8},{19,9... | collective-permute-start | bytes 196616 | tf_op jit(solution)/shard_map/ppermute | solution.py:238
  10.2 2.1 %collective-permute-start.2 = (bf16[4,8192]{1,0:T(4,128)(2,1)}, bf16[4,8192]{1,0:T(4,128)(2,1)S(1)}, u32[]{:S(2)}, u32[]{:S(2)}) collective-permute-start(bf16[4,8192]{1,0:T(4,128)(2,1)} %param.8), channel_id=1, source_target_pairs={{26,0},{27,1},{24,2},{25,3},{30,4},{31,5},{28,6},{29,7},{2,8},{3,9... | collective-permute-start | bytes 196616 | tf_op jit(solution)/shard_map/ppermute | solution.py:238
  12.3 0.7 copy-done
  13.0 1.2 %copy-done.2 = bf16[64,8192]{1,0:T(8,128)(2,1)S(1)} copy-done((bf16[64,8192]{1,0:T(8,128)(2,1)S(1)}, bf16[64,8192]{1,0:T(8,128)(2,1)}, u32[]{:S(2)}) %copy-start.2) | copy-done | bytes 1048600
  14.3 1.2 %copy-done.4 = bf16[16,112,256]{2,1,0:T(8,128)(2,1)S(1)} copy-done((bf16[16,112,256]{2,1,0:T(8,128)(2,1)S(1)}, bf16[16,112,256]{2,1,0:T(8,128)(2,1)}, u32[]{:S(2)}) %copy-start.4) | copy-done | bytes 917528
  15.4 1.6 %shift.2.refs_0_.rest_0_ = bf16[576,2048]{1,0:T(8,128)(2,1)S(1)} custom-call(s32[9,64]{1,0:T(8,128)S(1)} %bitcast.3, bf16[64,8192]{1,0:T(8,128)(2,1)S(1)} %copy-done.2, bf16[16,112,256]{2,1,0:T(8,128)(2,1)S(1)} %copy-done.4), custom_call_target="tpu_custom_call" | custom-call | flops 1600000000 | bytes 4194304 | tf_op jit(solution)/shard_map/shift/pallas_call | solution.py:89
  17.0 2.2 %collective-permute-done.2 = bf16[4,8192]{1,0:T(4,128)(2,1)S(1)} collective-permute-done((bf16[4,8192]{1,0:T(4,128)(2,1)}, bf16[4,8192]{1,0:T(4,128)(2,1)S(1)}, u32[]{:S(2)}, u32[]{:S(2)}) %collective-permute-start.2) | collective-permute-done | bytes 65568 | tf_op jit(solution)/shard_map/ppermute | solution.py:238
  19.3 0.9 %collective-permute-start.4 = (bf16[16,8192]{1,0:T(8,128)(2,1)S(1)}, bf16[16,8192]{1,0:T(8,128)(2,1)S(1)}, u32[]{:S(2)}, u32[]{:S(2)}) collective-permute-start(bf16[16,8192]{1,0:T(8,128)(2,1)S(1)} %pad_maximum_fusion.refs_2_), channel_id=1, source_target_pairs={{28,0},{29,1},{30,2},{31,3},{0,4},{1,5},{2,6},{3,7},{4,8},{5,9},{6... | collective-permute-start | bytes 786440 | tf_op jit(solution)/shard_map/ppermute | solution.py:241
  20.3 1.2 %collective-permute-start.3 = (bf16[16,8192]{1,0:T(8,128)(2,1)S(1)}, bf16[16,8192]{1,0:T(8,128)(2,1)S(1)}, u32[]{:S(2)}, u32[]{:S(2)}) collective-permute-start(bf16[16,8192]{1,0:T(8,128)(2,1)S(1)} %pad_maximum_fusion.refs_2_), channel_id=1, source_target_pairs={{4,0},{5,1},{6,2},{7,3},{8,4},{9,5},{10,6},{11,7},{12,8},{13,9},{1... | collective-permute-start | bytes 786440 | tf_op jit(solution)/shard_map/ppermute | solution.py:241
  21.4 1.4 %collective-permute-start.5 = (bf16[16,8192]{1,0:T(8,128)(2,1)S(1)}, bf16[16,8192]{1,0:T(8,128)(2,1)S(1)}, u32[]{:S(2)}, u32[]{:S(2)}) collective-permute-start(bf16[16,8192]{1,0:T(8,128)(2,1)S(1)} %pad_maximum_fusion.refs_2_), channel_id=1, source_target_pairs={{1,0},{2,1},{3,2},{0,3},{5,4},{6,5},{7,6},{4,7},{9,8},{10,9},{11,1... | collective-permute-start | bytes 786440 | tf_op jit(solution)/shard_map/ppermute | solution.py:241
  23.5 2.5 %collective-permute-done.4.refs_4_ = bf16[16,8192]{1,0:T(8,128)(2,1)S(1)} collective-permute-done((bf16[16,8192]{1,0:T(8,128)(2,1)S(1)}, bf16[16,8192]{1,0:T(8,128)(2,1)S(1)}, u32[]{:S(2)}, u32[]{:S(2)}) %collective-permute-start.4) | collective-permute-done | bytes 262176 | tf_op jit(solution)/shard_map/ppermute | solution.py:241
  26.0 1.0 %collective-permute-start.7 = (bf16[16,8192]{1,0:T(8,128)(2,1)S(1)}, bf16[16,8192]{1,0:T(8,128)(2,1)S(1)}, u32[]{:S(2)}, u32[]{:S(2)}) collective-permute-start(bf16[16,8192]{1,0:T(8,128)(2,1)S(1)} %collective-permute-done.4.refs_4_), channel_id=1, source_target_pairs={{28,0},{29,1},{30,2},{31,3},{0,4},{1,5},{2,6},{3,7},{4,8},{5,9},{6... | collective-permute-start | bytes 786440 | tf_op jit(solution)/shard_map/ppermute | solution.py:243
  27.0 2.7 %collective-permute-start.8 = (bf16[16,8192]{1,0:T(8,128)(2,1)S(1)}, bf16[16,8192]{1,0:T(8,128)(2,1)S(1)}, u32[]{:S(2)}, u32[]{:S(2)}) collective-permute-start(bf16[16,8192]{1,0:T(8,128)(2,1)S(1)} %collective-permute-done.4.refs_4_), channel_id=1, source_target_pairs={{1,0},{2,1},{3,2},{0,3},{5,4},{6,5},{7,6},{4,7},{9,8},{10,9},{11,1... | collective-permute-start | bytes 786440 | tf_op jit(solution)/shard_map/ppermute | solution.py:243
  29.8 4.0 %shift.3.refs_1_.rest_1_ = bf16[576,6144]{1,0:T(8,128)(2,1)S(1)} custom-call(s32[9,64]{1,0:T(8,128)S(1)} %bitcast.4, bf16[64,8192]{1,0:T(8,128)(2,1)S(1)} %copy-done.2, bf16[48,112,256]{2,1,0:T(8,128)(2,1)S(1)} %copy-done.3), custom_call_target="tpu_custom_call" | custom-call | flops 4800000000 | bytes 12582912 | tf_op jit(solution)/shard_map/shift/pallas_call | solution.py:89
  33.8 3.5 %collective-permute-done.9.refs_9_ = bf16[16,8192]{1,0:T(8,128)(2,1)S(1)} collective-permute-done((bf16[16,8192]{1,0:T(8,128)(2,1)S(1)}, bf16[16,8192]{1,0:T(8,128)(2,1)S(1)}, u32[]{:S(2)}, u32[]{:S(2)}) %collective-permute-start.9) | collective-permute-done | bytes 262176 | tf_op jit(solution)/shard_map/ppermute | solution.py:243
  37.3 3.1 %score.1 = (f32[128,576]{1,0:T(8,128)S(1)}, f32[2,64]{1,0:T(2,128)S(1)}) custom-call(bf16[576,2048]{1,0:T(8,128)(2,1)S(1)} %shift.2.refs_0_.rest_0_, bf16[576,6144]{1,0:T(8,128)(2,1)S(1)} %shift.3.refs_1_.rest_1_, bf16[16,8192]{1,0:T(8,128)(2,1)S(1)} %pad_maximum_fusion.refs_2_, bf16[16,8192]{1,0:T(8,128)(2,1)S(1)} %collective-permute-done.3.refs_3_, ...), custom_call_target="tpu_custom_call" | custom-call | flops 2000000000 | bytes 12582912 | tf_op jit(solution)/shard_map/score/pallas_call | solution.py:185
  40.4 3.1 %collective-permute-start.11 = (f32[2,64]{1,0:T(2,128)S(1)}, f32[2,64]{1,0:T(2,128)S(1)}, u32[]{:S(2)}, u32[]{:S(2)}) collective-permute-start(f32[2,64]{1,0:T(2,128)S(1)} %get-tuple-element.16.s0), channel_id=1, source_target_pairs={{0,64},{64,0},{1,65},{65,1},{2,66},{66,2},{3,67},{67,3},{4,68},{68... | collective-permute-start | bytes 1544 | tf_op jit(solution)/shard_map/ppermute | solution.py:262
  44.0 0.9 %collective-permute-done.10.s1 = f32[2,64]{1,0:T(2,128)S(1)} collective-permute-done((f32[2,64]{1,0:T(2,128)S(1)}, f32[2,64]{1,0:T(2,128)S(1)}, u32[]{:S(2)}, u32[]{:S(2)}) %collective-permute-start.10) | collective-permute-done | bytes 544 | tf_op jit(solution)/shard_map/ppermute | solution.py:261
  45.6 3.8 %insert.1 = (f32[128,1024]{1,0:T(8,128)S(1)}, bf16[128,1024]{1,0:T(8,128)(2,1)S(1)}, f32[1,64]{1,0:T(1,128)}) custom-call(f32[128,576]{1,0:T(8,128)S(1)} %get-tuple-element.15.raised, f32[2,64]{1,0:T(2,128)S(1)} %get-tuple-element.16.s0, f32[2,64]{1,0:T(2,128)S(1)} %collective-permute-done.10.s1, f32[2,64]{1,0:T(2,128)S(1)} %collective-permute-done.11.s2, ...), custom_call_target="tpu_custom_call" | custom-call | flops 3000000000 | bytes 12582912 | tf_op jit(solution)/shard_map/insert/pallas_call | solution.py:221
  49.4 1.9 %collective-permute-start.13 = (bf16[128,1024]{1,0:T(8,128)(2,1)S(1)}, bf16[128,1024]{1,0:T(8,128)(2,1)S(1)}, u32[]{:S(2)}, u32[]{:S(2)}) collective-permute-start(bf16[128,1024]{1,0:T(8,128)(2,1)S(1)} %get-tuple-element.18), channel_id=1, source_target_pairs={{0,32},{32,0},{1,33},{33,1},{2,34},{34,2},{3,35},{35,3},{4,36},{36... | collective-permute-start | bytes 786440 | tf_op jit(solution)/shard_map/ppermute | solution.py:266
  51.3 1.2 %collective-permute-done.13 = bf16[128,1024]{1,0:T(8,128)(2,1)S(1)} collective-permute-done((bf16[128,1024]{1,0:T(8,128)(2,1)S(1)}, bf16[128,1024]{1,0:T(8,128)(2,1)S(1)}, u32[]{:S(2)}, u32[]{:S(2)}) %collective-permute-start.13) | collective-permute-done | bytes 262176 | tf_op jit(solution)/shard_map/ppermute | solution.py:266
  52.6 22.0 %all_to_all.5 = bf16[64,2,1024]{2,1,0:T(2,128)(2,1)S(1)} all-to-all(bf16[64,2,1024]{2,1,0:T(2,128)(2,1)S(1)} %reshape.10), channel_id=1, replica_groups=mesh['half'=2,'px'=2,'core'=2,'dom'=32] {'dom','px'}, dimensions={0} | all-to-all | bytes 524288 | tf_op jit(solution)/shard_map/all_to_all | solution.py:268
  74.5 0.8 %convert_reduce_fusion = f32[2,1024]{1,0:T(2,128)} fusion(bf16[64,2,1024]{2,1,0:T(2,128)(2,1)S(1)} %all_to_all.5), kind=kLoop, calls=%fused_computation | loop fusion | flops 260096 | bytes 270336 | tf_op jit(solution)/shard_map/reduce_sum | solution.py:269
  (26 shorter events, 2.2 us)
Async XLA Ops:
  0.6 16.4 %collective-permute-start = (bf16[4,8192]{1,0:T(4,128)(2,1)}, bf16[4,8192]{1,0:T(4,128)(2,1)S(1)}, u32[]{:S(2)}, u32[]{:S(2)}) collective-permute-start(bf16[4,8192]{1,0:T(4,128)(2,1)} %param.8), channel_id=1, source_target_pairs={{16,0},{17,1},{18,2},{19,3},{20,4},{21,5},{22,6},{23,7},{24,8},{25... | collective-permute-start | bytes 196616 | tf_op jit(solution)/shard_map/ppermute | solution.py:238
  7.0 10.0 %collective-permute-start.1 = (bf16[4,8192]{1,0:T(4,128)(2,1)}, bf16[4,8192]{1,0:T(4,128)(2,1)S(1)}, u32[]{:S(2)}, u32[]{:S(2)}) collective-permute-start(bf16[4,8192]{1,0:T(4,128)(2,1)} %param.8), channel_id=1, source_target_pairs={{10,0},{11,1},{8,2},{9,3},{14,4},{15,5},{12,6},{13,7},{18,8},{19,9... | collective-permute-start | bytes 196616 | tf_op jit(solution)/shard_map/ppermute | solution.py:238
  10.2 9.0 %collective-permute-start.2 = (bf16[4,8192]{1,0:T(4,128)(2,1)}, bf16[4,8192]{1,0:T(4,128)(2,1)S(1)}, u32[]{:S(2)}, u32[]{:S(2)}) collective-permute-start(bf16[4,8192]{1,0:T(4,128)(2,1)} %param.8), channel_id=1, source_target_pairs={{26,0},{27,1},{24,2},{25,3},{30,4},{31,5},{28,6},{29,7},{2,8},{3,9... | collective-permute-start | bytes 196616 | tf_op jit(solution)/shard_map/ppermute | solution.py:238
  12.3 0.7 copy-start
  13.0 1.2 %copy-start.2 = (bf16[64,8192]{1,0:T(8,128)(2,1)S(1)}, bf16[64,8192]{1,0:T(8,128)(2,1)}, u32[]{:S(2)}) copy-start(bf16[64,8192]{1,0:T(8,128)(2,1)} %image_ref.3) | copy-start | bytes 3145732
  14.3 1.2 %copy-start.4 = (bf16[16,112,256]{2,1,0:T(8,128)(2,1)S(1)}, bf16[16,112,256]{2,1,0:T(8,128)(2,1)}, u32[]{:S(2)}) copy-start(bf16[16,112,256]{2,1,0:T(8,128)(2,1)} %constant.6.clone.table_ref) | copy-start | bytes 2752516
  15.4 3.7 %copy-start.5 = (bf16[4,8192]{1,0:T(4,128)(2,1)S(1)}, bf16[4,8192]{1,0:T(4,128)(2,1)}, u32[]{:S(2)}) copy-start(bf16[4,8192]{1,0:T(4,128)(2,1)} %param.8) | copy-start | bytes 196612
  15.4 14.3 %copy-start.3 = (bf16[48,112,256]{2,1,0:T(8,128)(2,1)S(1)}, bf16[48,112,256]{2,1,0:T(8,128)(2,1)}, u32[]{:S(2)}) copy-start(bf16[48,112,256]{2,1,0:T(8,128)(2,1)} %constant.7.clone.table_ref) | copy-start | bytes 8257540
  19.3 6.7 %collective-permute-start.4 = (bf16[16,8192]{1,0:T(8,128)(2,1)S(1)}, bf16[16,8192]{1,0:T(8,128)(2,1)S(1)}, u32[]{:S(2)}, u32[]{:S(2)}) collective-permute-start(bf16[16,8192]{1,0:T(8,128)(2,1)S(1)} %pad_maximum_fusion.refs_2_), channel_id=1, source_target_pairs={{28,0},{29,1},{30,2},{31,3},{0,4},{1,5},{2,6},{3,7},{4,8},{5,9},{6... | collective-permute-start | bytes 786440 | tf_op jit(solution)/shard_map/ppermute | solution.py:241
  20.3 9.5 %collective-permute-start.3 = (bf16[16,8192]{1,0:T(8,128)(2,1)S(1)}, bf16[16,8192]{1,0:T(8,128)(2,1)S(1)}, u32[]{:S(2)}, u32[]{:S(2)}) collective-permute-start(bf16[16,8192]{1,0:T(8,128)(2,1)S(1)} %pad_maximum_fusion.refs_2_), channel_id=1, source_target_pairs={{4,0},{5,1},{6,2},{7,3},{8,4},{9,5},{10,6},{11,7},{12,8},{13,9},{1... | collective-permute-start | bytes 786440 | tf_op jit(solution)/shard_map/ppermute | solution.py:241
  21.4 12.4 %collective-permute-start.5 = (bf16[16,8192]{1,0:T(8,128)(2,1)S(1)}, bf16[16,8192]{1,0:T(8,128)(2,1)S(1)}, u32[]{:S(2)}, u32[]{:S(2)}) collective-permute-start(bf16[16,8192]{1,0:T(8,128)(2,1)S(1)} %pad_maximum_fusion.refs_2_), channel_id=1, source_target_pairs={{1,0},{2,1},{3,2},{0,3},{5,4},{6,5},{7,6},{4,7},{9,8},{10,9},{11,1... | collective-permute-start | bytes 786440 | tf_op jit(solution)/shard_map/ppermute | solution.py:241
  22.9 11.0 %collective-permute-start.6 = (bf16[16,8192]{1,0:T(8,128)(2,1)S(1)}, bf16[16,8192]{1,0:T(8,128)(2,1)S(1)}, u32[]{:S(2)}, u32[]{:S(2)}) collective-permute-start(bf16[16,8192]{1,0:T(8,128)(2,1)S(1)} %pad_maximum_fusion.refs_2_), channel_id=1, source_target_pairs={{3,0},{0,1},{1,2},{2,3},{7,4},{4,5},{5,6},{6,7},{11,8},{8,9},{9,10... | collective-permute-start | bytes 786440 | tf_op jit(solution)/shard_map/ppermute | solution.py:241
  26.0 7.8 %collective-permute-start.7 = (bf16[16,8192]{1,0:T(8,128)(2,1)S(1)}, bf16[16,8192]{1,0:T(8,128)(2,1)S(1)}, u32[]{:S(2)}, u32[]{:S(2)}) collective-permute-start(bf16[16,8192]{1,0:T(8,128)(2,1)S(1)} %collective-permute-done.4.refs_4_), channel_id=1, source_target_pairs={{28,0},{29,1},{30,2},{31,3},{0,4},{1,5},{2,6},{3,7},{4,8},{5,9},{6... | collective-permute-start | bytes 786440 | tf_op jit(solution)/shard_map/ppermute | solution.py:243
  27.0 6.8 %collective-permute-start.8 = (bf16[16,8192]{1,0:T(8,128)(2,1)S(1)}, bf16[16,8192]{1,0:T(8,128)(2,1)S(1)}, u32[]{:S(2)}, u32[]{:S(2)}) collective-permute-start(bf16[16,8192]{1,0:T(8,128)(2,1)S(1)} %collective-permute-done.4.refs_4_), channel_id=1, source_target_pairs={{1,0},{2,1},{3,2},{0,3},{5,4},{6,5},{7,6},{4,7},{9,8},{10,9},{11,1... | collective-permute-start | bytes 786440 | tf_op jit(solution)/shard_map/ppermute | solution.py:243
  29.7 7.6 %collective-permute-start.9 = (bf16[16,8192]{1,0:T(8,128)(2,1)S(1)}, bf16[16,8192]{1,0:T(8,128)(2,1)S(1)}, u32[]{:S(2)}, u32[]{:S(2)}) collective-permute-start(bf16[16,8192]{1,0:T(8,128)(2,1)S(1)} %collective-permute-done.4.refs_4_), channel_id=1, source_target_pairs={{3,0},{0,1},{1,2},{2,3},{7,4},{4,5},{5,6},{6,7},{11,8},{8,9},{9,10... | collective-permute-start | bytes 786440 | tf_op jit(solution)/shard_map/ppermute | solution.py:243
  33.8 10.0 %copy-start.1 = (s32[128,8]{0,1:T(8,128)S(1)}, s32[128,8]{0,1:T(8,128)}, u32[]{:S(2)}) copy-start(s32[128,8]{0,1:T(8,128)} %param.9) | copy-start | bytes 12292
  40.4 4.5 %collective-permute-start.10 = (f32[2,64]{1,0:T(2,128)S(1)}, f32[2,64]{1,0:T(2,128)S(1)}, u32[]{:S(2)}, u32[]{:S(2)}) collective-permute-start(f32[2,64]{1,0:T(2,128)S(1)} %get-tuple-element.16.s0), channel_id=1, source_target_pairs={{0,96},{32,64},{64,32},{96,0},{1,97},{33,65},{65,33},{97,1},{2,98}... | collective-permute-start | bytes 1544 | tf_op jit(solution)/shard_map/ppermute | solution.py:261
  40.4 5.2 %collective-permute-start.11 = (f32[2,64]{1,0:T(2,128)S(1)}, f32[2,64]{1,0:T(2,128)S(1)}, u32[]{:S(2)}, u32[]{:S(2)}) collective-permute-start(f32[2,64]{1,0:T(2,128)S(1)} %get-tuple-element.16.s0), channel_id=1, source_target_pairs={{0,64},{64,0},{1,65},{65,1},{2,66},{66,2},{3,67},{67,3},{4,68},{68... | collective-permute-start | bytes 1544 | tf_op jit(solution)/shard_map/ppermute | solution.py:262
  43.5 2.1 %collective-permute-start.12 = (f32[2,64]{1,0:T(2,128)S(1)}, f32[2,64]{1,0:T(2,128)S(1)}, u32[]{:S(2)}, u32[]{:S(2)}) collective-permute-start(f32[2,64]{1,0:T(2,128)S(1)} %get-tuple-element.16.s0), channel_id=1, source_target_pairs={{0,32},{32,0},{1,33},{33,1},{2,34},{34,2},{3,35},{35,3},{4,36},{36... | collective-permute-start | bytes 1544 | tf_op jit(solution)/shard_map/ppermute | solution.py:263
  49.4 3.0 %collective-permute-start.13 = (bf16[128,1024]{1,0:T(8,128)(2,1)S(1)}, bf16[128,1024]{1,0:T(8,128)(2,1)S(1)}, u32[]{:S(2)}, u32[]{:S(2)}) collective-permute-start(bf16[128,1024]{1,0:T(8,128)(2,1)S(1)} %get-tuple-element.18), channel_id=1, source_target_pairs={{0,32},{32,0},{1,33},{33,1},{2,34},{34,2},{3,35},{35,3},{4,36},{36... | collective-permute-start | bytes 786440 | tf_op jit(solution)/shard_map/ppermute | solution.py:266

commit v6 on v5

--- a/solution.py
+++ b/solution.py
@@ -30,7 +30,7 @@
 
 
 FAR = ((0, 0), (4, 0), (2, 2), (-2, 2))
-NEAR = ((0, 0), (1, 0), (-1, 0), (0, 1), (0, -1), (-2, 0), (-1, 1), (-1, -1))
+NEAR = ((0, 0), (-1, 0), (0, 1), (0, -1), (1, 0), (-2, 0), (-1, 1), (-1, -1))
 
 
 def receive_from(dz, dy):
@@ -239,7 +239,7 @@
     far, early = lax.optimization_barrier((far, early()))
     own = jnp.concatenate([references, *far], axis=0)
     first = [lax.ppermute(own, "dom", receive_from(*d)) for d in NEAR[1:5]]
-    up = first[1]
+    up = first[0]
     second = [lax.ppermute(up, "dom", receive_from(*d)) for d in ((-1, 0), (0, 1), (0, -1))]
     return [own, *first, *second], (early, late())
 

time: 75.6 us -> 75.1 us (level)
  no operation moved by 1% of the time
where the time goes in v6:
time: 75.1 us; the launch traced here: 74.8 us
  starting transfers between devices  24.8 us (33%)
  blocking collectives  21.4 us (28%)
  Pallas kernels  12.7 us (17%)
  waiting for transfers between devices  10.9 us (15%)
  local copies, waits for them, and re-layouts  3.21 us (4%)
  other arithmetic  1.06 us (1%)
    all_to_all x1, blocking collectives, shards(): arrived = lax.all_to_all(sent, ('dom', 'px'), 0, 0, tiled=True)  21.4 us
    ppermute x3, starting transfers between devices, gather(): far = [lax.ppermute(references, 'dom', receive_from(*d)) for d in FAR[1:]]  11.7 us
    pallas_call x2, Pallas kernels, shift_images(): pl.pallas_call(functools.partial(shift_kernel, start), in_specs=[VMEM] *...  5.58 us
    ppermute x4, starting transfers between devices, gather(): first = [lax.ppermute(own, 'dom', receive_from(*d)) for d in NEAR[1:5]]  4.13 us
    pallas_call x1, Pallas kernels, insert(): pl.pallas_call(functools.partial(insert_kernel, scale), in_specs=[VMEM] *...  3.79 us
    ppermute x3, starting transfers between devices, gather(): lax.ppermute(up, 'dom', receive_from(*d))  3.72 us
    ppermute x3, waiting for transfers between devices, gather(): lax.ppermute(up, 'dom', receive_from(*d))  3.49 us
    unnamed x12, local copies, waits for them, and re-layouts  3.11 us
  transfers between devices with their start and end apart: 14, of which 6 were waited for; matrix products, arithmetic and copies ran while one was open for 0% of the time, Pallas kernels for 8%

profile of v6, /device:TPU:32, one launch (start us, length us, event | category | flops | bytes accessed | tf_op | source)
XLA Modules:
  0.0 74.8 jit_solution(12376979801918029697)
XLA Ops:
  0.6 6.4 %collective-permute-start = (bf16[4,8192]{1,0:T(4,128)(2,1)}, bf16[4,8192]{1,0:T(4,128)(2,1)S(1)}, u32[]{:S(2)}, u32[]{:S(2)}) collective-permute-start(bf16[4,8192]{1,0:T(4,128)(2,1)} %param.8), channel_id=1, source_target_pairs={{16,0},{17,1},{18,2},{19,3},{20,4},{21,5},{22,6},{23,7},{24,8},{25... | collective-permute-start | bytes 196616 | tf_op jit(solution)/shard_map/ppermute | solution.py:238
  7.0 3.2 %collective-permute-start.1 = (bf16[4,8192]{1,0:T(4,128)(2,1)}, bf16[4,8192]{1,0:T(4,128)(2,1)S(1)}, u32[]{:S(2)}, u32[]{:S(2)}) collective-permute-start(bf16[4,8192]{1,0:T(4,128)(2,1)} %param.8), channel_id=1, source_target_pairs={{10,0},{11,1},{8,2},{9,3},{14,4},{15,5},{12,6},{13,7},{18,8},{19,9... | collective-permute-start | bytes 196616 | tf_op jit(solution)/shard_map/ppermute | solution.py:238
  10.2 2.1 %collective-permute-start.2 = (bf16[4,8192]{1,0:T(4,128)(2,1)}, bf16[4,8192]{1,0:T(4,128)(2,1)S(1)}, u32[]{:S(2)}, u32[]{:S(2)}) collective-permute-start(bf16[4,8192]{1,0:T(4,128)(2,1)} %param.8), channel_id=1, source_target_pairs={{26,0},{27,1},{24,2},{25,3},{30,4},{31,5},{28,6},{29,7},{2,8},{3,9... | collective-permute-start | bytes 196616 | tf_op jit(solution)/shard_map/ppermute | solution.py:238
  12.3 0.7 copy-done
  13.0 1.2 %copy-done.2 = bf16[64,8192]{1,0:T(8,128)(2,1)S(1)} copy-done((bf16[64,8192]{1,0:T(8,128)(2,1)S(1)}, bf16[64,8192]{1,0:T(8,128)(2,1)}, u32[]{:S(2)}) %copy-start.2) | copy-done | bytes 1048600
  14.3 1.2 %copy-done.4 = bf16[16,112,256]{2,1,0:T(8,128)(2,1)S(1)} copy-done((bf16[16,112,256]{2,1,0:T(8,128)(2,1)S(1)}, bf16[16,112,256]{2,1,0:T(8,128)(2,1)}, u32[]{:S(2)}) %copy-start.4) | copy-done | bytes 917528
  15.4 1.6 %shift.2.refs_0_.rest_0_ = bf16[576,2048]{1,0:T(8,128)(2,1)S(1)} custom-call(s32[9,64]{1,0:T(8,128)S(1)} %bitcast.3, bf16[64,8192]{1,0:T(8,128)(2,1)S(1)} %copy-done.2, bf16[16,112,256]{2,1,0:T(8,128)(2,1)S(1)} %copy-done.4), custom_call_target="tpu_custom_call" | custom-call | flops 1600000000 | bytes 4194304 | tf_op jit(solution)/shard_map/shift/pallas_call | solution.py:89
  17.0 2.2 %collective-permute-done.2 = bf16[4,8192]{1,0:T(4,128)(2,1)S(1)} collective-permute-done((bf16[4,8192]{1,0:T(4,128)(2,1)}, bf16[4,8192]{1,0:T(4,128)(2,1)S(1)}, u32[]{:S(2)}, u32[]{:S(2)}) %collective-permute-start.2) | collective-permute-done | bytes 65568 | tf_op jit(solution)/shard_map/ppermute | solution.py:238
  19.3 0.9 %collective-permute-start.3 = (bf16[16,8192]{1,0:T(8,128)(2,1)S(1)}, bf16[16,8192]{1,0:T(8,128)(2,1)S(1)}, u32[]{:S(2)}, u32[]{:S(2)}) collective-permute-start(bf16[16,8192]{1,0:T(8,128)(2,1)S(1)} %pad_maximum_fusion.refs_2_), channel_id=1, source_target_pairs={{28,0},{29,1},{30,2},{31,3},{0,4},{1,5},{2,6},{3,7},{4,8},{5,9},{6... | collective-permute-start | bytes 786440 | tf_op jit(solution)/shard_map/ppermute | solution.py:241
  20.3 2.3 %collective-permute-start.4 = (bf16[16,8192]{1,0:T(8,128)(2,1)S(1)}, bf16[16,8192]{1,0:T(8,128)(2,1)S(1)}, u32[]{:S(2)}, u32[]{:S(2)}) collective-permute-start(bf16[16,8192]{1,0:T(8,128)(2,1)S(1)} %pad_maximum_fusion.refs_2_), channel_id=1, source_target_pairs={{1,0},{2,1},{3,2},{0,3},{5,4},{6,5},{7,6},{4,7},{9,8},{10,9},{11,1... | collective-permute-start | bytes 786440 | tf_op jit(solution)/shard_map/ppermute | solution.py:241
  22.5 0.9 %collective-permute-start.6 = (bf16[16,8192]{1,0:T(8,128)(2,1)S(1)}, bf16[16,8192]{1,0:T(8,128)(2,1)S(1)}, u32[]{:S(2)}, u32[]{:S(2)}) collective-permute-start(bf16[16,8192]{1,0:T(8,128)(2,1)S(1)} %pad_maximum_fusion.refs_2_), channel_id=1, source_target_pairs={{4,0},{5,1},{6,2},{7,3},{8,4},{9,5},{10,6},{11,7},{12,8},{13,9},{1... | collective-permute-start | bytes 786440 | tf_op jit(solution)/shard_map/ppermute | solution.py:241
  23.5 2.5 %collective-permute-done.3.refs_3_ = bf16[16,8192]{1,0:T(8,128)(2,1)S(1)} collective-permute-done((bf16[16,8192]{1,0:T(8,128)(2,1)S(1)}, bf16[16,8192]{1,0:T(8,128)(2,1)S(1)}, u32[]{:S(2)}, u32[]{:S(2)}) %collective-permute-start.3) | collective-permute-done | bytes 262176 | tf_op jit(solution)/shard_map/ppermute | solution.py:241
  26.0 1.0 %collective-permute-start.7 = (bf16[16,8192]{1,0:T(8,128)(2,1)S(1)}, bf16[16,8192]{1,0:T(8,128)(2,1)S(1)}, u32[]{:S(2)}, u32[]{:S(2)}) collective-permute-start(bf16[16,8192]{1,0:T(8,128)(2,1)S(1)} %collective-permute-done.3.refs_3_), channel_id=1, source_target_pairs={{28,0},{29,1},{30,2},{31,3},{0,4},{1,5},{2,6},{3,7},{4,8},{5,9},{6... | collective-permute-start | bytes 786440 | tf_op jit(solution)/shard_map/ppermute | solution.py:243
  27.0 2.7 %collective-permute-start.8 = (bf16[16,8192]{1,0:T(8,128)(2,1)S(1)}, bf16[16,8192]{1,0:T(8,128)(2,1)S(1)}, u32[]{:S(2)}, u32[]{:S(2)}) collective-permute-start(bf16[16,8192]{1,0:T(8,128)(2,1)S(1)} %collective-permute-done.3.refs_3_), channel_id=1, source_target_pairs={{1,0},{2,1},{3,2},{0,3},{5,4},{6,5},{7,6},{4,7},{9,8},{10,9},{11,1... | collective-permute-start | bytes 786440 | tf_op jit(solution)/shard_map/ppermute | solution.py:243
  29.8 4.0 %shift.3.refs_1_.rest_1_ = bf16[576,6144]{1,0:T(8,128)(2,1)S(1)} custom-call(s32[9,64]{1,0:T(8,128)S(1)} %bitcast.4, bf16[64,8192]{1,0:T(8,128)(2,1)S(1)} %copy-done.2, bf16[48,112,256]{2,1,0:T(8,128)(2,1)S(1)} %copy-done.3), custom_call_target="tpu_custom_call" | custom-call | flops 4800000000 | bytes 12582912 | tf_op jit(solution)/shard_map/shift/pallas_call | solution.py:89
  33.8 3.5 %collective-permute-done.9.refs_9_ = bf16[16,8192]{1,0:T(8,128)(2,1)S(1)} collective-permute-done((bf16[16,8192]{1,0:T(8,128)(2,1)S(1)}, bf16[16,8192]{1,0:T(8,128)(2,1)S(1)}, u32[]{:S(2)}, u32[]{:S(2)}) %collective-permute-start.9) | collective-permute-done | bytes 262176 | tf_op jit(solution)/shard_map/ppermute | solution.py:243
  37.3 3.1 %score.1 = (f32[128,576]{1,0:T(8,128)S(1)}, f32[2,64]{1,0:T(2,128)S(1)}) custom-call(bf16[576,2048]{1,0:T(8,128)(2,1)S(1)} %shift.2.refs_0_.rest_0_, bf16[576,6144]{1,0:T(8,128)(2,1)S(1)} %shift.3.refs_1_.rest_1_, bf16[16,8192]{1,0:T(8,128)(2,1)S(1)} %pad_maximum_fusion.refs_2_, bf16[16,8192]{1,0:T(8,128)(2,1)S(1)} %collective-permute-done.3.refs_3_, ...), custom_call_target="tpu_custom_call" | custom-call | flops 2000000000 | bytes 12582912 | tf_op jit(solution)/shard_map/score/pallas_call | solution.py:185
  40.4 3.1 %collective-permute-start.11 = (f32[2,64]{1,0:T(2,128)S(1)}, f32[2,64]{1,0:T(2,128)S(1)}, u32[]{:S(2)}, u32[]{:S(2)}) collective-permute-start(f32[2,64]{1,0:T(2,128)S(1)} %get-tuple-element.16.s0), channel_id=1, source_target_pairs={{0,64},{64,0},{1,65},{65,1},{2,66},{66,2},{3,67},{67,3},{4,68},{68... | collective-permute-start | bytes 1544 | tf_op jit(solution)/shard_map/ppermute | solution.py:262
  44.0 0.9 %collective-permute-done.10.s1 = f32[2,64]{1,0:T(2,128)S(1)} collective-permute-done((f32[2,64]{1,0:T(2,128)S(1)}, f32[2,64]{1,0:T(2,128)S(1)}, u32[]{:S(2)}, u32[]{:S(2)}) %collective-permute-start.10) | collective-permute-done | bytes 544 | tf_op jit(solution)/shard_map/ppermute | solution.py:261
  45.6 3.8 %insert.1 = (f32[128,1024]{1,0:T(8,128)S(1)}, bf16[128,1024]{1,0:T(8,128)(2,1)S(1)}, f32[1,64]{1,0:T(1,128)}) custom-call(f32[128,576]{1,0:T(8,128)S(1)} %get-tuple-element.15.raised, f32[2,64]{1,0:T(2,128)S(1)} %get-tuple-element.16.s0, f32[2,64]{1,0:T(2,128)S(1)} %collective-permute-done.10.s1, f32[2,64]{1,0:T(2,128)S(1)} %collective-permute-done.11.s2, ...), custom_call_target="tpu_custom_call" | custom-call | flops 3000000000 | bytes 12582912 | tf_op jit(solution)/shard_map/insert/pallas_call | solution.py:221
  49.4 1.9 %collective-permute-start.13 = (bf16[128,1024]{1,0:T(8,128)(2,1)S(1)}, bf16[128,1024]{1,0:T(8,128)(2,1)S(1)}, u32[]{:S(2)}, u32[]{:S(2)}) collective-permute-start(bf16[128,1024]{1,0:T(8,128)(2,1)S(1)} %get-tuple-element.18), channel_id=1, source_target_pairs={{0,32},{32,0},{1,33},{33,1},{2,34},{34,2},{3,35},{35,3},{4,36},{36... | collective-permute-start | bytes 786440 | tf_op jit(solution)/shard_map/ppermute | solution.py:266
  51.3 1.2 %collective-permute-done.13 = bf16[128,1024]{1,0:T(8,128)(2,1)S(1)} collective-permute-done((bf16[128,1024]{1,0:T(8,128)(2,1)S(1)}, bf16[128,1024]{1,0:T(8,128)(2,1)S(1)}, u32[]{:S(2)}, u32[]{:S(2)}) %collective-permute-start.13) | collective-permute-done | bytes 262176 | tf_op jit(solution)/shard_map/ppermute | solution.py:266
  52.6 21.4 %all_to_all.5 = bf16[64,2,1024]{2,1,0:T(2,128)(2,1)S(1)} all-to-all(bf16[64,2,1024]{2,1,0:T(2,128)(2,1)S(1)} %reshape.10), channel_id=1, replica_groups=mesh['half'=2,'px'=2,'core'=2,'dom'=32] {'dom','px'}, dimensions={0} | all-to-all | bytes 524288 | tf_op jit(solution)/shard_map/all_to_all | solution.py:268
  74.0 0.8 %convert_reduce_fusion = f32[2,1024]{1,0:T(2,128)} fusion(bf16[64,2,1024]{2,1,0:T(2,128)(2,1)S(1)} %all_to_all.5), kind=kLoop, calls=%fused_computation | loop fusion | flops 260096 | bytes 270336 | tf_op jit(solution)/shard_map/reduce_sum | solution.py:269
  (26 shorter events, 1.6 us)
Async XLA Ops:
  0.6 16.4 %collective-permute-start = (bf16[4,8192]{1,0:T(4,128)(2,1)}, bf16[4,8192]{1,0:T(4,128)(2,1)S(1)}, u32[]{:S(2)}, u32[]{:S(2)}) collective-permute-start(bf16[4,8192]{1,0:T(4,128)(2,1)} %param.8), channel_id=1, source_target_pairs={{16,0},{17,1},{18,2},{19,3},{20,4},{21,5},{22,6},{23,7},{24,8},{25... | collective-permute-start | bytes 196616 | tf_op jit(solution)/shard_map/ppermute | solution.py:238
  7.0 10.0 %collective-permute-start.1 = (bf16[4,8192]{1,0:T(4,128)(2,1)}, bf16[4,8192]{1,0:T(4,128)(2,1)S(1)}, u32[]{:S(2)}, u32[]{:S(2)}) collective-permute-start(bf16[4,8192]{1,0:T(4,128)(2,1)} %param.8), channel_id=1, source_target_pairs={{10,0},{11,1},{8,2},{9,3},{14,4},{15,5},{12,6},{13,7},{18,8},{19,9... | collective-permute-start | bytes 196616 | tf_op jit(solution)/shard_map/ppermute | solution.py:238
  10.2 9.0 %collective-permute-start.2 = (bf16[4,8192]{1,0:T(4,128)(2,1)}, bf16[4,8192]{1,0:T(4,128)(2,1)S(1)}, u32[]{:S(2)}, u32[]{:S(2)}) collective-permute-start(bf16[4,8192]{1,0:T(4,128)(2,1)} %param.8), channel_id=1, source_target_pairs={{26,0},{27,1},{24,2},{25,3},{30,4},{31,5},{28,6},{29,7},{2,8},{3,9... | collective-permute-start | bytes 196616 | tf_op jit(solution)/shard_map/ppermute | solution.py:238
  12.3 0.7 copy-start
  13.0 1.2 %copy-start.2 = (bf16[64,8192]{1,0:T(8,128)(2,1)S(1)}, bf16[64,8192]{1,0:T(8,128)(2,1)}, u32[]{:S(2)}) copy-start(bf16[64,8192]{1,0:T(8,128)(2,1)} %image_ref.3) | copy-start | bytes 3145732
  14.3 1.2 %copy-start.4 = (bf16[16,112,256]{2,1,0:T(8,128)(2,1)S(1)}, bf16[16,112,256]{2,1,0:T(8,128)(2,1)}, u32[]{:S(2)}) copy-start(bf16[16,112,256]{2,1,0:T(8,128)(2,1)} %constant.6.clone.table_ref) | copy-start | bytes 2752516
  15.4 3.7 %copy-start.5 = (bf16[4,8192]{1,0:T(4,128)(2,1)S(1)}, bf16[4,8192]{1,0:T(4,128)(2,1)}, u32[]{:S(2)}) copy-start(bf16[4,8192]{1,0:T(4,128)(2,1)} %param.8) | copy-start | bytes 196612
  15.4 14.3 %copy-start.3 = (bf16[48,112,256]{2,1,0:T(8,128)(2,1)S(1)}, bf16[48,112,256]{2,1,0:T(8,128)(2,1)}, u32[]{:S(2)}) copy-start(bf16[48,112,256]{2,1,0:T(8,128)(2,1)} %constant.7.clone.table_ref) | copy-start | bytes 8257540
  19.3 6.7 %collective-permute-start.3 = (bf16[16,8192]{1,0:T(8,128)(2,1)S(1)}, bf16[16,8192]{1,0:T(8,128)(2,1)S(1)}, u32[]{:S(2)}, u32[]{:S(2)}) collective-permute-start(bf16[16,8192]{1,0:T(8,128)(2,1)S(1)} %pad_maximum_fusion.refs_2_), channel_id=1, source_target_pairs={{28,0},{29,1},{30,2},{31,3},{0,4},{1,5},{2,6},{3,7},{4,8},{5,9},{6... | collective-permute-start | bytes 786440 | tf_op jit(solution)/shard_map/ppermute | solution.py:241
  20.3 9.5 %collective-permute-start.4 = (bf16[16,8192]{1,0:T(8,128)(2,1)S(1)}, bf16[16,8192]{1,0:T(8,128)(2,1)S(1)}, u32[]{:S(2)}, u32[]{:S(2)}) collective-permute-start(bf16[16,8192]{1,0:T(8,128)(2,1)S(1)} %pad_maximum_fusion.refs_2_), channel_id=1, source_target_pairs={{1,0},{2,1},{3,2},{0,3},{5,4},{6,5},{7,6},{4,7},{9,8},{10,9},{11,1... | collective-permute-start | bytes 786440 | tf_op jit(solution)/shard_map/ppermute | solution.py:241
  22.5 11.3 %collective-permute-start.5 = (bf16[16,8192]{1,0:T(8,128)(2,1)S(1)}, bf16[16,8192]{1,0:T(8,128)(2,1)S(1)}, u32[]{:S(2)}, u32[]{:S(2)}) collective-permute-start(bf16[16,8192]{1,0:T(8,128)(2,1)S(1)} %pad_maximum_fusion.refs_2_), channel_id=1, source_target_pairs={{3,0},{0,1},{1,2},{2,3},{7,4},{4,5},{5,6},{6,7},{11,8},{8,9},{9,10... | collective-permute-start | bytes 786440 | tf_op jit(solution)/shard_map/ppermute | solution.py:241
  22.5 11.3 %collective-permute-start.6 = (bf16[16,8192]{1,0:T(8,128)(2,1)S(1)}, bf16[16,8192]{1,0:T(8,128)(2,1)S(1)}, u32[]{:S(2)}, u32[]{:S(2)}) collective-permute-start(bf16[16,8192]{1,0:T(8,128)(2,1)S(1)} %pad_maximum_fusion.refs_2_), channel_id=1, source_target_pairs={{4,0},{5,1},{6,2},{7,3},{8,4},{9,5},{10,6},{11,7},{12,8},{13,9},{1... | collective-permute-start | bytes 786440 | tf_op jit(solution)/shard_map/ppermute | solution.py:241
  26.0 7.8 %collective-permute-start.7 = (bf16[16,8192]{1,0:T(8,128)(2,1)S(1)}, bf16[16,8192]{1,0:T(8,128)(2,1)S(1)}, u32[]{:S(2)}, u32[]{:S(2)}) collective-permute-start(bf16[16,8192]{1,0:T(8,128)(2,1)S(1)} %collective-permute-done.3.refs_3_), channel_id=1, source_target_pairs={{28,0},{29,1},{30,2},{31,3},{0,4},{1,5},{2,6},{3,7},{4,8},{5,9},{6... | collective-permute-start | bytes 786440 | tf_op jit(solution)/shard_map/ppermute | solution.py:243
  27.0 6.8 %collective-permute-start.8 = (bf16[16,8192]{1,0:T(8,128)(2,1)S(1)}, bf16[16,8192]{1,0:T(8,128)(2,1)S(1)}, u32[]{:S(2)}, u32[]{:S(2)}) collective-permute-start(bf16[16,8192]{1,0:T(8,128)(2,1)S(1)} %collective-permute-done.3.refs_3_), channel_id=1, source_target_pairs={{1,0},{2,1},{3,2},{0,3},{5,4},{6,5},{7,6},{4,7},{9,8},{10,9},{11,1... | collective-permute-start | bytes 786440 | tf_op jit(solution)/shard_map/ppermute | solution.py:243
  29.7 7.6 %collective-permute-start.9 = (bf16[16,8192]{1,0:T(8,128)(2,1)S(1)}, bf16[16,8192]{1,0:T(8,128)(2,1)S(1)}, u32[]{:S(2)}, u32[]{:S(2)}) collective-permute-start(bf16[16,8192]{1,0:T(8,128)(2,1)S(1)} %collective-permute-done.3.refs_3_), channel_id=1, source_target_pairs={{3,0},{0,1},{1,2},{2,3},{7,4},{4,5},{5,6},{6,7},{11,8},{8,9},{9,10... | collective-permute-start | bytes 786440 | tf_op jit(solution)/shard_map/ppermute | solution.py:243
  33.8 10.0 %copy-start.1 = (s32[128,8]{0,1:T(8,128)S(1)}, s32[128,8]{0,1:T(8,128)}, u32[]{:S(2)}) copy-start(s32[128,8]{0,1:T(8,128)} %param.9) | copy-start | bytes 12292
  40.4 4.5 %collective-permute-start.10 = (f32[2,64]{1,0:T(2,128)S(1)}, f32[2,64]{1,0:T(2,128)S(1)}, u32[]{:S(2)}, u32[]{:S(2)}) collective-permute-start(f32[2,64]{1,0:T(2,128)S(1)} %get-tuple-element.16.s0), channel_id=1, source_target_pairs={{0,96},{32,64},{64,32},{96,0},{1,97},{33,65},{65,33},{97,1},{2,98}... | collective-permute-start | bytes 1544 | tf_op jit(solution)/shard_map/ppermute | solution.py:261
  40.4 5.2 %collective-permute-start.11 = (f32[2,64]{1,0:T(2,128)S(1)}, f32[2,64]{1,0:T(2,128)S(1)}, u32[]{:S(2)}, u32[]{:S(2)}) collective-permute-start(f32[2,64]{1,0:T(2,128)S(1)} %get-tuple-element.16.s0), channel_id=1, source_target_pairs={{0,64},{64,0},{1,65},{65,1},{2,66},{66,2},{3,67},{67,3},{4,68},{68... | collective-permute-start | bytes 1544 | tf_op jit(solution)/shard_map/ppermute | solution.py:262
  43.5 2.1 %collective-permute-start.12 = (f32[2,64]{1,0:T(2,128)S(1)}, f32[2,64]{1,0:T(2,128)S(1)}, u32[]{:S(2)}, u32[]{:S(2)}) collective-permute-start(f32[2,64]{1,0:T(2,128)S(1)} %get-tuple-element.16.s0), channel_id=1, source_target_pairs={{0,32},{32,0},{1,33},{33,1},{2,34},{34,2},{3,35},{35,3},{4,36},{36... | collective-permute-start | bytes 1544 | tf_op jit(solution)/shard_map/ppermute | solution.py:263
  49.4 3.0 %collective-permute-start.13 = (bf16[128,1024]{1,0:T(8,128)(2,1)S(1)}, bf16[128,1024]{1,0:T(8,128)(2,1)S(1)}, u32[]{:S(2)}, u32[]{:S(2)}) collective-permute-start(bf16[128,1024]{1,0:T(8,128)(2,1)S(1)} %get-tuple-element.18), channel_id=1, source_target_pairs={{0,32},{32,0},{1,33},{33,1},{2,34},{34,2},{3,35},{35,3},{4,36},{36... | collective-permute-start | bytes 786440 | tf_op jit(solution)/shard_map/ppermute | solution.py:266

commit v7 on v6

--- a/solution.py
+++ b/solution.py
@@ -29,7 +29,7 @@
     return (z % Z) * Y + y % Y
 
 
-FAR = ((0, 0), (4, 0), (2, 2), (-2, 2))
+FAR = ((0, 0), (2, 2), (-2, 2), (4, 0))
 NEAR = ((0, 0), (-1, 0), (0, 1), (0, -1), (1, 0), (-2, 0), (-1, 1), (-1, -1))
 
 

time: 75.1 us -> 74.3 us (0.989)
  waiting for transfers between devices: 10.9 us -> 13.8 us
  blocking collectives: 21.4 us -> 19.4 us
  starting transfers between devices: 24.8 us -> 23.1 us
    ppermute x3, waiting for transfers between devices: 2.16 us -> 4.23 us  [gather(): far = [lax.ppermute(references, 'dom', receive_from(*d)) for d in FAR[1:]]]
    all_to_all x1, blocking collectives: 21.4 us -> 19.4 us  [shards(): arrived = lax.all_to_all(sent, ('dom', 'px'), 0, 0, tiled=True)]
    ppermute x3, starting transfers between devices: 3.72 us -> 2.03 us  [gather(): lax.ppermute(up, 'dom', receive_from(*d))]
    ppermute x4, waiting for transfers between devices: 2.56 us -> 3.8 us  [gather(): first = [lax.ppermute(own, 'dom', receive_from(*d)) for d in NEAR[1:5]]]
  transfers between devices with their start and end apart: 14 -> 14, of which waited for: 6 -> 7; matrix products, arithmetic and copies ran while one was open for 0% -> 0% of each run, Pallas kernels for 8% -> 8%
where the time goes in v7:
time: 74.3 us; the launch traced here: 74 us
  starting transfers between devices  23.1 us (31%)
  blocking collectives  19.4 us (26%)
  waiting for transfers between devices  13.8 us (19%)
  Pallas kernels  12.7 us (17%)
  local copies, waits for them, and re-layouts  3.21 us (4%)
  other arithmetic  1.06 us (1%)
    all_to_all x1, blocking collectives, shards(): arrived = lax.all_to_all(sent, ('dom', 'px'), 0, 0, tiled=True)  19.4 us
    ppermute x3, starting transfers between devices, gather(): far = [lax.ppermute(references, 'dom', receive_from(*d)) for d in FAR[1:]]  11.7 us
    pallas_call x2, Pallas kernels, shift_images(): pl.pallas_call(functools.partial(shift_kernel, start), in_specs=[VMEM] *...  5.57 us
    ppermute x3, waiting for transfers between devices, gather(): far = [lax.ppermute(references, 'dom', receive_from(*d)) for d in FAR[1:]]  4.23 us
    ppermute x4, starting transfers between devices, gather(): first = [lax.ppermute(own, 'dom', receive_from(*d)) for d in NEAR[1:5]]  4.12 us
    ppermute x4, waiting for transfers between devices, gather(): first = [lax.ppermute(own, 'dom', receive_from(*d)) for d in NEAR[1:5]]  3.8 us
    pallas_call x1, Pallas kernels, insert(): pl.pallas_call(functools.partial(insert_kernel, scale), in_specs=[VMEM] *...  3.79 us
    unnamed x12, local copies, waits for them, and re-layouts  3.11 us
  transfers between devices with their start and end apart: 14, of which 7 were waited for; matrix products, arithmetic and copies ran while one was open for 0% of the time, Pallas kernels for 8%

profile of v7, /device:TPU:32, one launch (start us, length us, event | category | flops | bytes accessed | tf_op | source)
XLA Modules:
  0.0 74.0 jit_solution(17524508231125959833)
XLA Ops:
  0.6 8.1 %collective-permute-start = (bf16[4,8192]{1,0:T(4,128)(2,1)}, bf16[4,8192]{1,0:T(4,128)(2,1)S(1)}, u32[]{:S(2)}, u32[]{:S(2)}) collective-permute-start(bf16[4,8192]{1,0:T(4,128)(2,1)} %param.8), channel_id=1, source_target_pairs={{10,0},{11,1},{8,2},{9,3},{14,4},{15,5},{12,6},{13,7},{18,8},{19,9... | collective-permute-start | bytes 196616 | tf_op jit(solution)/shard_map/ppermute | solution.py:238
  8.7 3.6 %collective-permute-start.2 = (bf16[4,8192]{1,0:T(4,128)(2,1)}, bf16[4,8192]{1,0:T(4,128)(2,1)S(1)}, u32[]{:S(2)}, u32[]{:S(2)}) collective-permute-start(bf16[4,8192]{1,0:T(4,128)(2,1)} %param.8), channel_id=1, source_target_pairs={{16,0},{17,1},{18,2},{19,3},{20,4},{21,5},{22,6},{23,7},{24,8},{25... | collective-permute-start | bytes 196616 | tf_op jit(solution)/shard_map/ppermute | solution.py:238
  12.3 0.7 copy-done
  13.0 1.2 %copy-done.2 = bf16[64,8192]{1,0:T(8,128)(2,1)S(1)} copy-done((bf16[64,8192]{1,0:T(8,128)(2,1)S(1)}, bf16[64,8192]{1,0:T(8,128)(2,1)}, u32[]{:S(2)}) %copy-start.2) | copy-done | bytes 1048600
  14.3 1.2 %copy-done.4 = bf16[16,112,256]{2,1,0:T(8,128)(2,1)S(1)} copy-done((bf16[16,112,256]{2,1,0:T(8,128)(2,1)S(1)}, bf16[16,112,256]{2,1,0:T(8,128)(2,1)}, u32[]{:S(2)}) %copy-start.4) | copy-done | bytes 917528
  15.4 1.6 %shift.2.refs_0_.rest_0_ = bf16[576,2048]{1,0:T(8,128)(2,1)S(1)} custom-call(s32[9,64]{1,0:T(8,128)S(1)} %bitcast.3, bf16[64,8192]{1,0:T(8,128)(2,1)S(1)} %copy-done.2, bf16[16,112,256]{2,1,0:T(8,128)(2,1)S(1)} %copy-done.4), custom_call_target="tpu_custom_call" | custom-call | flops 1600000000 | bytes 4194304 | tf_op jit(solution)/shard_map/shift/pallas_call | solution.py:89
  17.0 4.2 %collective-permute-done.1 = bf16[4,8192]{1,0:T(4,128)(2,1)S(1)} collective-permute-done((bf16[4,8192]{1,0:T(4,128)(2,1)}, bf16[4,8192]{1,0:T(4,128)(2,1)S(1)}, u32[]{:S(2)}, u32[]{:S(2)}) %collective-permute-start.1) | collective-permute-done | bytes 65568 | tf_op jit(solution)/shard_map/ppermute | solution.py:238
  21.5 1.7 %collective-permute-start.4 = (bf16[16,8192]{1,0:T(8,128)(2,1)S(1)}, bf16[16,8192]{1,0:T(8,128)(2,1)S(1)}, u32[]{:S(2)}, u32[]{:S(2)}) collective-permute-start(bf16[16,8192]{1,0:T(8,128)(2,1)S(1)} %pad_maximum_fusion.refs_2_), channel_id=1, source_target_pairs={{1,0},{2,1},{3,2},{0,3},{5,4},{6,5},{7,6},{4,7},{9,8},{10,9},{11,1... | collective-permute-start | bytes 786440 | tf_op jit(solution)/shard_map/ppermute | solution.py:241
  23.2 0.4 collective-permute-start.5
  23.6 1.9 %collective-permute-start.6 = (bf16[16,8192]{1,0:T(8,128)(2,1)S(1)}, bf16[16,8192]{1,0:T(8,128)(2,1)S(1)}, u32[]{:S(2)}, u32[]{:S(2)}) collective-permute-start(bf16[16,8192]{1,0:T(8,128)(2,1)S(1)} %pad_maximum_fusion.refs_2_), channel_id=1, source_target_pairs={{4,0},{5,1},{6,2},{7,3},{8,4},{9,5},{10,6},{11,7},{12,8},{13,9},{1... | collective-permute-start | bytes 786440 | tf_op jit(solution)/shard_map/ppermute | solution.py:241
  25.5 3.8 %collective-permute-done.3.refs_3_ = bf16[16,8192]{1,0:T(8,128)(2,1)S(1)} collective-permute-done((bf16[16,8192]{1,0:T(8,128)(2,1)S(1)}, bf16[16,8192]{1,0:T(8,128)(2,1)S(1)}, u32[]{:S(2)}, u32[]{:S(2)}) %collective-permute-start.3) | collective-permute-done | bytes 262176 | tf_op jit(solution)/shard_map/ppermute | solution.py:241
  29.3 1.6 %collective-permute-start.8 = (bf16[16,8192]{1,0:T(8,128)(2,1)S(1)}, bf16[16,8192]{1,0:T(8,128)(2,1)S(1)}, u32[]{:S(2)}, u32[]{:S(2)}) collective-permute-start(bf16[16,8192]{1,0:T(8,128)(2,1)S(1)} %collective-permute-done.3.refs_3_), channel_id=1, source_target_pairs={{1,0},{2,1},{3,2},{0,3},{5,4},{6,5},{7,6},{4,7},{9,8},{10,9},{11,1... | collective-permute-start | bytes 786440 | tf_op jit(solution)/shard_map/ppermute | solution.py:243
  30.9 0.5 collective-permute-start.9
  31.4 4.0 %shift.3.refs_1_.rest_1_ = bf16[576,6144]{1,0:T(8,128)(2,1)S(1)} custom-call(s32[9,64]{1,0:T(8,128)S(1)} %bitcast.4, bf16[64,8192]{1,0:T(8,128)(2,1)S(1)} %copy-done.2, bf16[48,112,256]{2,1,0:T(8,128)(2,1)S(1)} %copy-done.3), custom_call_target="tpu_custom_call" | custom-call | flops 4800000000 | bytes 12582912 | tf_op jit(solution)/shard_map/shift/pallas_call | solution.py:89
  35.7 2.8 %collective-permute-done.9.refs_9_ = bf16[16,8192]{1,0:T(8,128)(2,1)S(1)} collective-permute-done((bf16[16,8192]{1,0:T(8,128)(2,1)S(1)}, bf16[16,8192]{1,0:T(8,128)(2,1)S(1)}, u32[]{:S(2)}, u32[]{:S(2)}) %collective-permute-start.9) | collective-permute-done | bytes 262176 | tf_op jit(solution)/shard_map/ppermute | solution.py:243
  38.5 3.0 %score.1 = (f32[128,576]{1,0:T(8,128)S(1)}, f32[2,64]{1,0:T(2,128)S(1)}) custom-call(bf16[576,2048]{1,0:T(8,128)(2,1)S(1)} %shift.2.refs_0_.rest_0_, bf16[576,6144]{1,0:T(8,128)(2,1)S(1)} %shift.3.refs_1_.rest_1_, bf16[16,8192]{1,0:T(8,128)(2,1)S(1)} %pad_maximum_fusion.refs_2_, bf16[16,8192]{1,0:T(8,128)(2,1)S(1)} %collective-permute-done.3.refs_3_, ...), custom_call_target="tpu_custom_call" | custom-call | flops 2000000000 | bytes 12582912 | tf_op jit(solution)/shard_map/score/pallas_call | solution.py:185
  41.6 3.1 %collective-permute-start.11 = (f32[2,64]{1,0:T(2,128)S(1)}, f32[2,64]{1,0:T(2,128)S(1)}, u32[]{:S(2)}, u32[]{:S(2)}) collective-permute-start(f32[2,64]{1,0:T(2,128)S(1)} %get-tuple-element.16.s0), channel_id=1, source_target_pairs={{0,64},{64,0},{1,65},{65,1},{2,66},{66,2},{3,67},{67,3},{4,68},{68... | collective-permute-start | bytes 1544 | tf_op jit(solution)/shard_map/ppermute | solution.py:262
  45.2 0.9 %collective-permute-done.10.s1 = f32[2,64]{1,0:T(2,128)S(1)} collective-permute-done((f32[2,64]{1,0:T(2,128)S(1)}, f32[2,64]{1,0:T(2,128)S(1)}, u32[]{:S(2)}, u32[]{:S(2)}) %collective-permute-start.10) | collective-permute-done | bytes 544 | tf_op jit(solution)/shard_map/ppermute | solution.py:261
  46.1 0.7 collective-permute-done.11.s2
  46.7 3.8 %insert.1 = (f32[128,1024]{1,0:T(8,128)S(1)}, bf16[128,1024]{1,0:T(8,128)(2,1)S(1)}, f32[1,64]{1,0:T(1,128)}) custom-call(f32[128,576]{1,0:T(8,128)S(1)} %get-tuple-element.15.raised, f32[2,64]{1,0:T(2,128)S(1)} %get-tuple-element.16.s0, f32[2,64]{1,0:T(2,128)S(1)} %collective-permute-done.10.s1, f32[2,64]{1,0:T(2,128)S(1)} %collective-permute-done.11.s2, ...), custom_call_target="tpu_custom_call" | custom-call | flops 3000000000 | bytes 12582912 | tf_op jit(solution)/shard_map/insert/pallas_call | solution.py:221
  50.5 1.9 %collective-permute-start.13 = (bf16[128,1024]{1,0:T(8,128)(2,1)S(1)}, bf16[128,1024]{1,0:T(8,128)(2,1)S(1)}, u32[]{:S(2)}, u32[]{:S(2)}) collective-permute-start(bf16[128,1024]{1,0:T(8,128)(2,1)S(1)} %get-tuple-element.18), channel_id=1, source_target_pairs={{0,32},{32,0},{1,33},{33,1},{2,34},{34,2},{3,35},{35,3},{4,36},{36... | collective-permute-start | bytes 786440 | tf_op jit(solution)/shard_map/ppermute | solution.py:266
  52.4 1.2 %collective-permute-done.13 = bf16[128,1024]{1,0:T(8,128)(2,1)S(1)} collective-permute-done((bf16[128,1024]{1,0:T(8,128)(2,1)S(1)}, bf16[128,1024]{1,0:T(8,128)(2,1)S(1)}, u32[]{:S(2)}, u32[]{:S(2)}) %collective-permute-start.13) | collective-permute-done | bytes 262176 | tf_op jit(solution)/shard_map/ppermute | solution.py:266
  53.8 19.4 %all_to_all.5 = bf16[64,2,1024]{2,1,0:T(2,128)(2,1)S(1)} all-to-all(bf16[64,2,1024]{2,1,0:T(2,128)(2,1)S(1)} %reshape.10), channel_id=1, replica_groups=mesh['half'=2,'px'=2,'core'=2,'dom'=32] {'dom','px'}, dimensions={0} | all-to-all | bytes 524288 | tf_op jit(solution)/shard_map/all_to_all | solution.py:268
  73.2 0.8 %convert_reduce_fusion = f32[2,1024]{1,0:T(2,128)} fusion(bf16[64,2,1024]{2,1,0:T(2,128)(2,1)S(1)} %all_to_all.5), kind=kLoop, calls=%fused_computation | loop fusion | flops 260096 | bytes 270336 | tf_op jit(solution)/shard_map/reduce_sum | solution.py:269
  (26 shorter events, 1.3 us)
Async XLA Ops:
  0.6 16.4 %collective-permute-start = (bf16[4,8192]{1,0:T(4,128)(2,1)}, bf16[4,8192]{1,0:T(4,128)(2,1)S(1)}, u32[]{:S(2)}, u32[]{:S(2)}) collective-permute-start(bf16[4,8192]{1,0:T(4,128)(2,1)} %param.8), channel_id=1, source_target_pairs={{10,0},{11,1},{8,2},{9,3},{14,4},{15,5},{12,6},{13,7},{18,8},{19,9... | collective-permute-start | bytes 196616 | tf_op jit(solution)/shard_map/ppermute | solution.py:238
  8.7 12.5 %collective-permute-start.1 = (bf16[4,8192]{1,0:T(4,128)(2,1)}, bf16[4,8192]{1,0:T(4,128)(2,1)S(1)}, u32[]{:S(2)}, u32[]{:S(2)}) collective-permute-start(bf16[4,8192]{1,0:T(4,128)(2,1)} %param.8), channel_id=1, source_target_pairs={{26,0},{27,1},{24,2},{25,3},{30,4},{31,5},{28,6},{29,7},{2,8},{3,9... | collective-permute-start | bytes 196616 | tf_op jit(solution)/shard_map/ppermute | solution.py:238
  8.7 12.5 %collective-permute-start.2 = (bf16[4,8192]{1,0:T(4,128)(2,1)}, bf16[4,8192]{1,0:T(4,128)(2,1)S(1)}, u32[]{:S(2)}, u32[]{:S(2)}) collective-permute-start(bf16[4,8192]{1,0:T(4,128)(2,1)} %param.8), channel_id=1, source_target_pairs={{16,0},{17,1},{18,2},{19,3},{20,4},{21,5},{22,6},{23,7},{24,8},{25... | collective-permute-start | bytes 196616 | tf_op jit(solution)/shard_map/ppermute | solution.py:238
  12.3 0.7 copy-start
  13.0 1.2 %copy-start.2 = (bf16[64,8192]{1,0:T(8,128)(2,1)S(1)}, bf16[64,8192]{1,0:T(8,128)(2,1)}, u32[]{:S(2)}) copy-start(bf16[64,8192]{1,0:T(8,128)(2,1)} %image_ref.3) | copy-start | bytes 3145732
  14.2 1.2 %copy-start.4 = (bf16[16,112,256]{2,1,0:T(8,128)(2,1)S(1)}, bf16[16,112,256]{2,1,0:T(8,128)(2,1)}, u32[]{:S(2)}) copy-start(bf16[16,112,256]{2,1,0:T(8,128)(2,1)} %constant.6.clone.table_ref) | copy-start | bytes 2752516
  15.4 5.8 %copy-start.5 = (bf16[4,8192]{1,0:T(4,128)(2,1)S(1)}, bf16[4,8192]{1,0:T(4,128)(2,1)}, u32[]{:S(2)}) copy-start(bf16[4,8192]{1,0:T(4,128)(2,1)} %param.8) | copy-start | bytes 196612
  15.4 15.9 %copy-start.3 = (bf16[48,112,256]{2,1,0:T(8,128)(2,1)S(1)}, bf16[48,112,256]{2,1,0:T(8,128)(2,1)}, u32[]{:S(2)}) copy-start(bf16[48,112,256]{2,1,0:T(8,128)(2,1)} %constant.7.clone.table_ref) | copy-start | bytes 8257540
  21.4 7.9 %collective-permute-start.3 = (bf16[16,8192]{1,0:T(8,128)(2,1)S(1)}, bf16[16,8192]{1,0:T(8,128)(2,1)S(1)}, u32[]{:S(2)}, u32[]{:S(2)}) collective-permute-start(bf16[16,8192]{1,0:T(8,128)(2,1)S(1)} %pad_maximum_fusion.refs_2_), channel_id=1, source_target_pairs={{28,0},{29,1},{30,2},{31,3},{0,4},{1,5},{2,6},{3,7},{4,8},{5,9},{6... | collective-permute-start | bytes 786440 | tf_op jit(solution)/shard_map/ppermute | solution.py:241
  21.5 9.4 %collective-permute-start.4 = (bf16[16,8192]{1,0:T(8,128)(2,1)S(1)}, bf16[16,8192]{1,0:T(8,128)(2,1)S(1)}, u32[]{:S(2)}, u32[]{:S(2)}) collective-permute-start(bf16[16,8192]{1,0:T(8,128)(2,1)S(1)} %pad_maximum_fusion.refs_2_), channel_id=1, source_target_pairs={{1,0},{2,1},{3,2},{0,3},{5,4},{6,5},{7,6},{4,7},{9,8},{10,9},{11,1... | collective-permute-start | bytes 786440 | tf_op jit(solution)/shard_map/ppermute | solution.py:241
  23.2 12.2 %collective-permute-start.5 = (bf16[16,8192]{1,0:T(8,128)(2,1)S(1)}, bf16[16,8192]{1,0:T(8,128)(2,1)S(1)}, u32[]{:S(2)}, u32[]{:S(2)}) collective-permute-start(bf16[16,8192]{1,0:T(8,128)(2,1)S(1)} %pad_maximum_fusion.refs_2_), channel_id=1, source_target_pairs={{3,0},{0,1},{1,2},{2,3},{7,4},{4,5},{5,6},{6,7},{11,8},{8,9},{9,10... | collective-permute-start | bytes 786440 | tf_op jit(solution)/shard_map/ppermute | solution.py:241
  23.6 11.8 %collective-permute-start.6 = (bf16[16,8192]{1,0:T(8,128)(2,1)S(1)}, bf16[16,8192]{1,0:T(8,128)(2,1)S(1)}, u32[]{:S(2)}, u32[]{:S(2)}) collective-permute-start(bf16[16,8192]{1,0:T(8,128)(2,1)S(1)} %pad_maximum_fusion.refs_2_), channel_id=1, source_target_pairs={{4,0},{5,1},{6,2},{7,3},{8,4},{9,5},{10,6},{11,7},{12,8},{13,9},{1... | collective-permute-start | bytes 786440 | tf_op jit(solution)/shard_map/ppermute | solution.py:241
  29.3 6.4 %collective-permute-start.7 = (bf16[16,8192]{1,0:T(8,128)(2,1)S(1)}, bf16[16,8192]{1,0:T(8,128)(2,1)S(1)}, u32[]{:S(2)}, u32[]{:S(2)}) collective-permute-start(bf16[16,8192]{1,0:T(8,128)(2,1)S(1)} %collective-permute-done.3.refs_3_), channel_id=1, source_target_pairs={{28,0},{29,1},{30,2},{31,3},{0,4},{1,5},{2,6},{3,7},{4,8},{5,9},{6... | collective-permute-start | bytes 786440 | tf_op jit(solution)/shard_map/ppermute | solution.py:243
  29.3 6.4 %collective-permute-start.8 = (bf16[16,8192]{1,0:T(8,128)(2,1)S(1)}, bf16[16,8192]{1,0:T(8,128)(2,1)S(1)}, u32[]{:S(2)}, u32[]{:S(2)}) collective-permute-start(bf16[16,8192]{1,0:T(8,128)(2,1)S(1)} %collective-permute-done.3.refs_3_), channel_id=1, source_target_pairs={{1,0},{2,1},{3,2},{0,3},{5,4},{6,5},{7,6},{4,7},{9,8},{10,9},{11,1... | collective-permute-start | bytes 786440 | tf_op jit(solution)/shard_map/ppermute | solution.py:243
  30.9 7.6 %collective-permute-start.9 = (bf16[16,8192]{1,0:T(8,128)(2,1)S(1)}, bf16[16,8192]{1,0:T(8,128)(2,1)S(1)}, u32[]{:S(2)}, u32[]{:S(2)}) collective-permute-start(bf16[16,8192]{1,0:T(8,128)(2,1)S(1)} %collective-permute-done.3.refs_3_), channel_id=1, source_target_pairs={{3,0},{0,1},{1,2},{2,3},{7,4},{4,5},{5,6},{6,7},{11,8},{8,9},{9,10... | collective-permute-start | bytes 786440 | tf_op jit(solution)/shard_map/ppermute | solution.py:243
  35.4 9.6 %copy-start.1 = (s32[128,8]{0,1:T(8,128)S(1)}, s32[128,8]{0,1:T(8,128)}, u32[]{:S(2)}) copy-start(s32[128,8]{0,1:T(8,128)} %param.9) | copy-start | bytes 12292
  41.5 4.5 %collective-permute-start.10 = (f32[2,64]{1,0:T(2,128)S(1)}, f32[2,64]{1,0:T(2,128)S(1)}, u32[]{:S(2)}, u32[]{:S(2)}) collective-permute-start(f32[2,64]{1,0:T(2,128)S(1)} %get-tuple-element.16.s0), channel_id=1, source_target_pairs={{0,96},{32,64},{64,32},{96,0},{1,97},{33,65},{65,33},{97,1},{2,98}... | collective-permute-start | bytes 1544 | tf_op jit(solution)/shard_map/ppermute | solution.py:261
  41.6 5.2 %collective-permute-start.11 = (f32[2,64]{1,0:T(2,128)S(1)}, f32[2,64]{1,0:T(2,128)S(1)}, u32[]{:S(2)}, u32[]{:S(2)}) collective-permute-start(f32[2,64]{1,0:T(2,128)S(1)} %get-tuple-element.16.s0), channel_id=1, source_target_pairs={{0,64},{64,0},{1,65},{65,1},{2,66},{66,2},{3,67},{67,3},{4,68},{68... | collective-permute-start | bytes 1544 | tf_op jit(solution)/shard_map/ppermute | solution.py:262
  44.7 2.1 %collective-permute-start.12 = (f32[2,64]{1,0:T(2,128)S(1)}, f32[2,64]{1,0:T(2,128)S(1)}, u32[]{:S(2)}, u32[]{:S(2)}) collective-permute-start(f32[2,64]{1,0:T(2,128)S(1)} %get-tuple-element.16.s0), channel_id=1, source_target_pairs={{0,32},{32,0},{1,33},{33,1},{2,34},{34,2},{3,35},{35,3},{4,36},{36... | collective-permute-start | bytes 1544 | tf_op jit(solution)/shard_map/ppermute | solution.py:263
  50.5 3.0 %collective-permute-start.13 = (bf16[128,1024]{1,0:T(8,128)(2,1)S(1)}, bf16[128,1024]{1,0:T(8,128)(2,1)S(1)}, u32[]{:S(2)}, u32[]{:S(2)}) collective-permute-start(bf16[128,1024]{1,0:T(8,128)(2,1)S(1)} %get-tuple-element.18), channel_id=1, source_target_pairs={{0,32},{32,0},{1,33},{33,1},{2,34},{34,2},{3,35},{35,3},{4,36},{36... | collective-permute-start | bytes 786440 | tf_op jit(solution)/shard_map/ppermute | solution.py:266

commit v8 on v7

--- a/solution.py
+++ b/solution.py
@@ -29,7 +29,7 @@
     return (z % Z) * Y + y % Y
 
 
-FAR = ((0, 0), (2, 2), (-2, 2), (4, 0))
+FAR = ((0, 0), (2, 2), (4, 0), (-2, 2))
 NEAR = ((0, 0), (-1, 0), (0, 1), (0, -1), (1, 0), (-2, 0), (-1, 1), (-1, -1))
 
 

time: 74.3 us -> 75.7 us (1.019)
  blocking collectives: 19.4 us -> 22 us
  waiting for transfers between devices: 13.8 us -> 12.3 us
    all_to_all x1, blocking collectives: 19.4 us -> 22 us  [shards(): arrived = lax.all_to_all(sent, ('dom', 'px'), 0, 0, tiled=True)]
    ppermute x3, waiting for transfers between devices: 4.23 us -> 2.83 us  [gather(): far = [lax.ppermute(references, 'dom', receive_from(*d)) for d in FAR[1:]]]
  transfers between devices with their start and end apart: 14 -> 14, of which waited for: 7 -> 9; matrix products, arithmetic and copies ran while one was open for 0% -> 0% of each run, Pallas kernels for 8% -> 8%
where the time goes in v8:
time: 75.7 us; the launch traced here: 75.4 us
  starting transfers between devices  23.4 us (31%)
  blocking collectives  22 us (29%)
  Pallas kernels  12.7 us (17%)
  waiting for transfers between devices  12.3 us (16%)
  local copies, waits for them, and re-layouts  3.21 us (4%)
  other arithmetic  1.06 us (1%)
    all_to_all x1, blocking collectives, shards(): arrived = lax.all_to_all(sent, ('dom', 'px'), 0, 0, tiled=True)  22 us
    ppermute x3, starting transfers between devices, gather(): far = [lax.ppermute(references, 'dom', receive_from(*d)) for d in FAR[1:]]  11.7 us
    pallas_call x2, Pallas kernels, shift_images(): pl.pallas_call(functools.partial(shift_kernel, start), in_specs=[VMEM] *...  5.59 us
    ppermute x4, starting transfers between devices, gather(): first = [lax.ppermute(own, 'dom', receive_from(*d)) for d in NEAR[1:5]]  4.13 us
    pallas_call x1, Pallas kernels, insert(): pl.pallas_call(functools.partial(insert_kernel, scale), in_specs=[VMEM] *...  3.78 us
    ppermute x4, waiting for transfers between devices, gather(): first = [lax.ppermute(own, 'dom', receive_from(*d)) for d in NEAR[1:5]]  3.76 us
    ppermute x1, starting transfers between devices, shards(): lax.ppermute(stats, 'px', swap)  3.12 us
    unnamed x12, local copies, waits for them, and re-layouts  3.11 us
  transfers between devices with their start and end apart: 14, of which 9 were waited for; matrix products, arithmetic and copies ran while one was open for 0% of the time, Pallas kernels for 8%

profile of v8, /device:TPU:32, one launch (start us, length us, event | category | flops | bytes accessed | tf_op | source)
XLA Modules:
  0.0 75.4 jit_solution(16122729907144215529)
XLA Ops:
  0.6 8.1 %collective-permute-start = (bf16[4,8192]{1,0:T(4,128)(2,1)}, bf16[4,8192]{1,0:T(4,128)(2,1)S(1)}, u32[]{:S(2)}, u32[]{:S(2)}) collective-permute-start(bf16[4,8192]{1,0:T(4,128)(2,1)} %param.8), channel_id=1, source_target_pairs={{10,0},{11,1},{8,2},{9,3},{14,4},{15,5},{12,6},{13,7},{18,8},{19,9... | collective-permute-start | bytes 196616 | tf_op jit(solution)/shard_map/ppermute | solution.py:238
  8.7 1.4 %collective-permute-start.1 = (bf16[4,8192]{1,0:T(4,128)(2,1)}, bf16[4,8192]{1,0:T(4,128)(2,1)S(1)}, u32[]{:S(2)}, u32[]{:S(2)}) collective-permute-start(bf16[4,8192]{1,0:T(4,128)(2,1)} %param.8), channel_id=1, source_target_pairs={{16,0},{17,1},{18,2},{19,3},{20,4},{21,5},{22,6},{23,7},{24,8},{25... | collective-permute-start | bytes 196616 | tf_op jit(solution)/shard_map/ppermute | solution.py:238
  10.2 2.1 %collective-permute-start.2 = (bf16[4,8192]{1,0:T(4,128)(2,1)}, bf16[4,8192]{1,0:T(4,128)(2,1)S(1)}, u32[]{:S(2)}, u32[]{:S(2)}) collective-permute-start(bf16[4,8192]{1,0:T(4,128)(2,1)} %param.8), channel_id=1, source_target_pairs={{26,0},{27,1},{24,2},{25,3},{30,4},{31,5},{28,6},{29,7},{2,8},{3,9... | collective-permute-start | bytes 196616 | tf_op jit(solution)/shard_map/ppermute | solution.py:238
  12.3 0.7 copy-done
  13.0 1.2 %copy-done.2 = bf16[64,8192]{1,0:T(8,128)(2,1)S(1)} copy-done((bf16[64,8192]{1,0:T(8,128)(2,1)S(1)}, bf16[64,8192]{1,0:T(8,128)(2,1)}, u32[]{:S(2)}) %copy-start.2) | copy-done | bytes 1048600
  14.3 1.2 %copy-done.4 = bf16[16,112,256]{2,1,0:T(8,128)(2,1)S(1)} copy-done((bf16[16,112,256]{2,1,0:T(8,128)(2,1)S(1)}, bf16[16,112,256]{2,1,0:T(8,128)(2,1)}, u32[]{:S(2)}) %copy-start.4) | copy-done | bytes 917528
  15.4 1.6 %shift.2.refs_0_.rest_0_ = bf16[576,2048]{1,0:T(8,128)(2,1)S(1)} custom-call(s32[9,64]{1,0:T(8,128)S(1)} %bitcast.3, bf16[64,8192]{1,0:T(8,128)(2,1)S(1)} %copy-done.2, bf16[16,112,256]{2,1,0:T(8,128)(2,1)S(1)} %copy-done.4), custom_call_target="tpu_custom_call" | custom-call | flops 1600000000 | bytes 4194304 | tf_op jit(solution)/shard_map/shift/pallas_call | solution.py:89
  17.4 2.4 %collective-permute-done.2 = bf16[4,8192]{1,0:T(4,128)(2,1)S(1)} collective-permute-done((bf16[4,8192]{1,0:T(4,128)(2,1)}, bf16[4,8192]{1,0:T(4,128)(2,1)S(1)}, u32[]{:S(2)}, u32[]{:S(2)}) %collective-permute-start.2) | collective-permute-done | bytes 65568 | tf_op jit(solution)/shard_map/ppermute | solution.py:238
  20.3 2.2 %collective-permute-start.4 = (bf16[16,8192]{1,0:T(8,128)(2,1)S(1)}, bf16[16,8192]{1,0:T(8,128)(2,1)S(1)}, u32[]{:S(2)}, u32[]{:S(2)}) collective-permute-start(bf16[16,8192]{1,0:T(8,128)(2,1)S(1)} %pad_maximum_fusion.refs_2_), channel_id=1, source_target_pairs={{1,0},{2,1},{3,2},{0,3},{5,4},{6,5},{7,6},{4,7},{9,8},{10,9},{11,1... | collective-permute-start | bytes 786440 | tf_op jit(solution)/shard_map/ppermute | solution.py:241
  22.5 1.6 %collective-permute-start.6 = (bf16[16,8192]{1,0:T(8,128)(2,1)S(1)}, bf16[16,8192]{1,0:T(8,128)(2,1)S(1)}, u32[]{:S(2)}, u32[]{:S(2)}) collective-permute-start(bf16[16,8192]{1,0:T(8,128)(2,1)S(1)} %pad_maximum_fusion.refs_2_), channel_id=1, source_target_pairs={{4,0},{5,1},{6,2},{7,3},{8,4},{9,5},{10,6},{11,7},{12,8},{13,9},{1... | collective-permute-start | bytes 786440 | tf_op jit(solution)/shard_map/ppermute | solution.py:241
  24.1 3.8 %collective-permute-done.3.refs_3_ = bf16[16,8192]{1,0:T(8,128)(2,1)S(1)} collective-permute-done((bf16[16,8192]{1,0:T(8,128)(2,1)S(1)}, bf16[16,8192]{1,0:T(8,128)(2,1)S(1)}, u32[]{:S(2)}, u32[]{:S(2)}) %collective-permute-start.3) | collective-permute-done | bytes 262176 | tf_op jit(solution)/shard_map/ppermute | solution.py:241
  28.2 1.6 %collective-permute-start.8 = (bf16[16,8192]{1,0:T(8,128)(2,1)S(1)}, bf16[16,8192]{1,0:T(8,128)(2,1)S(1)}, u32[]{:S(2)}, u32[]{:S(2)}) collective-permute-start(bf16[16,8192]{1,0:T(8,128)(2,1)S(1)} %collective-permute-done.3.refs_3_), channel_id=1, source_target_pairs={{1,0},{2,1},{3,2},{0,3},{5,4},{6,5},{7,6},{4,7},{9,8},{10,9},{11,1... | collective-permute-start | bytes 786440 | tf_op jit(solution)/shard_map/ppermute | solution.py:243
  30.2 4.0 %shift.3.refs_1_.rest_1_ = bf16[576,6144]{1,0:T(8,128)(2,1)S(1)} custom-call(s32[9,64]{1,0:T(8,128)S(1)} %bitcast.4, bf16[64,8192]{1,0:T(8,128)(2,1)S(1)} %copy-done.2, bf16[48,112,256]{2,1,0:T(8,128)(2,1)S(1)} %copy-done.3), custom_call_target="tpu_custom_call" | custom-call | flops 4800000000 | bytes 12582912 | tf_op jit(solution)/shard_map/shift/pallas_call | solution.py:89
  34.3 0.5 collective-permute-done.7.refs_7_
  35.0 2.3 %collective-permute-done.9.refs_9_ = bf16[16,8192]{1,0:T(8,128)(2,1)S(1)} collective-permute-done((bf16[16,8192]{1,0:T(8,128)(2,1)S(1)}, bf16[16,8192]{1,0:T(8,128)(2,1)S(1)}, u32[]{:S(2)}, u32[]{:S(2)}) %collective-permute-start.9) | collective-permute-done | bytes 262176 | tf_op jit(solution)/shard_map/ppermute | solution.py:243
  37.3 3.0 %score.1 = (f32[128,576]{1,0:T(8,128)S(1)}, f32[2,64]{1,0:T(2,128)S(1)}) custom-call(bf16[576,2048]{1,0:T(8,128)(2,1)S(1)} %shift.2.refs_0_.rest_0_, bf16[576,6144]{1,0:T(8,128)(2,1)S(1)} %shift.3.refs_1_.rest_1_, bf16[16,8192]{1,0:T(8,128)(2,1)S(1)} %pad_maximum_fusion.refs_2_, bf16[16,8192]{1,0:T(8,128)(2,1)S(1)} %collective-permute-done.3.refs_3_, ...), custom_call_target="tpu_custom_call" | custom-call | flops 2000000000 | bytes 12582912 | tf_op jit(solution)/shard_map/score/pallas_call | solution.py:185
  40.4 3.1 %collective-permute-start.11 = (f32[2,64]{1,0:T(2,128)S(1)}, f32[2,64]{1,0:T(2,128)S(1)}, u32[]{:S(2)}, u32[]{:S(2)}) collective-permute-start(f32[2,64]{1,0:T(2,128)S(1)} %get-tuple-element.16.s0), channel_id=1, source_target_pairs={{0,64},{64,0},{1,65},{65,1},{2,66},{66,2},{3,67},{67,3},{4,68},{68... | collective-permute-start | bytes 1544 | tf_op jit(solution)/shard_map/ppermute | solution.py:262
  44.0 0.9 %collective-permute-done.10.s1 = f32[2,64]{1,0:T(2,128)S(1)} collective-permute-done((f32[2,64]{1,0:T(2,128)S(1)}, f32[2,64]{1,0:T(2,128)S(1)}, u32[]{:S(2)}, u32[]{:S(2)}) %collective-permute-start.10) | collective-permute-done | bytes 544 | tf_op jit(solution)/shard_map/ppermute | solution.py:261
  44.9 0.7 collective-permute-done.11.s2
  45.6 3.8 %insert.1 = (f32[128,1024]{1,0:T(8,128)S(1)}, bf16[128,1024]{1,0:T(8,128)(2,1)S(1)}, f32[1,64]{1,0:T(1,128)}) custom-call(f32[128,576]{1,0:T(8,128)S(1)} %get-tuple-element.15.raised, f32[2,64]{1,0:T(2,128)S(1)} %get-tuple-element.16.s0, f32[2,64]{1,0:T(2,128)S(1)} %collective-permute-done.10.s1, f32[2,64]{1,0:T(2,128)S(1)} %collective-permute-done.11.s2, ...), custom_call_target="tpu_custom_call" | custom-call | flops 3000000000 | bytes 12582912 | tf_op jit(solution)/shard_map/insert/pallas_call | solution.py:221
  49.3 1.9 %collective-permute-start.13 = (bf16[128,1024]{1,0:T(8,128)(2,1)S(1)}, bf16[128,1024]{1,0:T(8,128)(2,1)S(1)}, u32[]{:S(2)}, u32[]{:S(2)}) collective-permute-start(bf16[128,1024]{1,0:T(8,128)(2,1)S(1)} %get-tuple-element.18), channel_id=1, source_target_pairs={{0,32},{32,0},{1,33},{33,1},{2,34},{34,2},{3,35},{35,3},{4,36},{36... | collective-permute-start | bytes 786440 | tf_op jit(solution)/shard_map/ppermute | solution.py:266
  51.2 1.2 %collective-permute-done.13 = bf16[128,1024]{1,0:T(8,128)(2,1)S(1)} collective-permute-done((bf16[128,1024]{1,0:T(8,128)(2,1)S(1)}, bf16[128,1024]{1,0:T(8,128)(2,1)S(1)}, u32[]{:S(2)}, u32[]{:S(2)}) %collective-permute-start.13) | collective-permute-done | bytes 262176 | tf_op jit(solution)/shard_map/ppermute | solution.py:266
  52.6 22.0 %all_to_all.5 = bf16[64,2,1024]{2,1,0:T(2,128)(2,1)S(1)} all-to-all(bf16[64,2,1024]{2,1,0:T(2,128)(2,1)S(1)} %reshape.10), channel_id=1, replica_groups=mesh['half'=2,'px'=2,'core'=2,'dom'=32] {'dom','px'}, dimensions={0} | all-to-all | bytes 524288 | tf_op jit(solution)/shard_map/all_to_all | solution.py:268
  74.6 0.8 %convert_reduce_fusion = f32[2,1024]{1,0:T(2,128)} fusion(bf16[64,2,1024]{2,1,0:T(2,128)(2,1)S(1)} %all_to_all.5), kind=kLoop, calls=%fused_computation | loop fusion | flops 260096 | bytes 270336 | tf_op jit(solution)/shard_map/reduce_sum | solution.py:269
  (26 shorter events, 2.6 us)
Async XLA Ops:
  0.6 16.4 %collective-permute-start = (bf16[4,8192]{1,0:T(4,128)(2,1)}, bf16[4,8192]{1,0:T(4,128)(2,1)S(1)}, u32[]{:S(2)}, u32[]{:S(2)}) collective-permute-start(bf16[4,8192]{1,0:T(4,128)(2,1)} %param.8), channel_id=1, source_target_pairs={{10,0},{11,1},{8,2},{9,3},{14,4},{15,5},{12,6},{13,7},{18,8},{19,9... | collective-permute-start | bytes 196616 | tf_op jit(solution)/shard_map/ppermute | solution.py:238
  8.7 8.7 %collective-permute-start.1 = (bf16[4,8192]{1,0:T(4,128)(2,1)}, bf16[4,8192]{1,0:T(4,128)(2,1)S(1)}, u32[]{:S(2)}, u32[]{:S(2)}) collective-permute-start(bf16[4,8192]{1,0:T(4,128)(2,1)} %param.8), channel_id=1, source_target_pairs={{16,0},{17,1},{18,2},{19,3},{20,4},{21,5},{22,6},{23,7},{24,8},{25... | collective-permute-start | bytes 196616 | tf_op jit(solution)/shard_map/ppermute | solution.py:238
  10.2 9.6 %collective-permute-start.2 = (bf16[4,8192]{1,0:T(4,128)(2,1)}, bf16[4,8192]{1,0:T(4,128)(2,1)S(1)}, u32[]{:S(2)}, u32[]{:S(2)}) collective-permute-start(bf16[4,8192]{1,0:T(4,128)(2,1)} %param.8), channel_id=1, source_target_pairs={{26,0},{27,1},{24,2},{25,3},{30,4},{31,5},{28,6},{29,7},{2,8},{3,9... | collective-permute-start | bytes 196616 | tf_op jit(solution)/shard_map/ppermute | solution.py:238
  12.3 0.7 copy-start
  13.0 1.2 %copy-start.2 = (bf16[64,8192]{1,0:T(8,128)(2,1)S(1)}, bf16[64,8192]{1,0:T(8,128)(2,1)}, u32[]{:S(2)}) copy-start(bf16[64,8192]{1,0:T(8,128)(2,1)} %image_ref.3) | copy-start | bytes 3145732
  14.2 1.2 %copy-start.4 = (bf16[16,112,256]{2,1,0:T(8,128)(2,1)S(1)}, bf16[16,112,256]{2,1,0:T(8,128)(2,1)}, u32[]{:S(2)}) copy-start(bf16[16,112,256]{2,1,0:T(8,128)(2,1)} %constant.6.clone.table_ref) | copy-start | bytes 2752516
  15.4 4.4 %copy-start.5 = (bf16[4,8192]{1,0:T(4,128)(2,1)S(1)}, bf16[4,8192]{1,0:T(4,128)(2,1)}, u32[]{:S(2)}) copy-start(bf16[4,8192]{1,0:T(4,128)(2,1)} %param.8) | copy-start | bytes 196612
  15.4 14.8 %copy-start.3 = (bf16[48,112,256]{2,1,0:T(8,128)(2,1)S(1)}, bf16[48,112,256]{2,1,0:T(8,128)(2,1)}, u32[]{:S(2)}) copy-start(bf16[48,112,256]{2,1,0:T(8,128)(2,1)} %constant.7.clone.table_ref) | copy-start | bytes 8257540
  20.0 7.9 %collective-permute-start.3 = (bf16[16,8192]{1,0:T(8,128)(2,1)S(1)}, bf16[16,8192]{1,0:T(8,128)(2,1)S(1)}, u32[]{:S(2)}, u32[]{:S(2)}) collective-permute-start(bf16[16,8192]{1,0:T(8,128)(2,1)S(1)} %pad_maximum_fusion.refs_2_), channel_id=1, source_target_pairs={{28,0},{29,1},{30,2},{31,3},{0,4},{1,5},{2,6},{3,7},{4,8},{5,9},{6... | collective-permute-start | bytes 786440 | tf_op jit(solution)/shard_map/ppermute | solution.py:241
  20.3 9.4 %collective-permute-start.4 = (bf16[16,8192]{1,0:T(8,128)(2,1)S(1)}, bf16[16,8192]{1,0:T(8,128)(2,1)S(1)}, u32[]{:S(2)}, u32[]{:S(2)}) collective-permute-start(bf16[16,8192]{1,0:T(8,128)(2,1)S(1)} %pad_maximum_fusion.refs_2_), channel_id=1, source_target_pairs={{1,0},{2,1},{3,2},{0,3},{5,4},{6,5},{7,6},{4,7},{9,8},{10,9},{11,1... | collective-permute-start | bytes 786440 | tf_op jit(solution)/shard_map/ppermute | solution.py:241
  22.5 11.7 %collective-permute-start.5 = (bf16[16,8192]{1,0:T(8,128)(2,1)S(1)}, bf16[16,8192]{1,0:T(8,128)(2,1)S(1)}, u32[]{:S(2)}, u32[]{:S(2)}) collective-permute-start(bf16[16,8192]{1,0:T(8,128)(2,1)S(1)} %pad_maximum_fusion.refs_2_), channel_id=1, source_target_pairs={{3,0},{0,1},{1,2},{2,3},{7,4},{4,5},{5,6},{6,7},{11,8},{8,9},{9,10... | collective-permute-start | bytes 786440 | tf_op jit(solution)/shard_map/ppermute | solution.py:241
  22.5 11.7 %collective-permute-start.6 = (bf16[16,8192]{1,0:T(8,128)(2,1)S(1)}, bf16[16,8192]{1,0:T(8,128)(2,1)S(1)}, u32[]{:S(2)}, u32[]{:S(2)}) collective-permute-start(bf16[16,8192]{1,0:T(8,128)(2,1)S(1)} %pad_maximum_fusion.refs_2_), channel_id=1, source_target_pairs={{4,0},{5,1},{6,2},{7,3},{8,4},{9,5},{10,6},{11,7},{12,8},{13,9},{1... | collective-permute-start | bytes 786440 | tf_op jit(solution)/shard_map/ppermute | solution.py:241
  27.9 6.9 %collective-permute-start.7 = (bf16[16,8192]{1,0:T(8,128)(2,1)S(1)}, bf16[16,8192]{1,0:T(8,128)(2,1)S(1)}, u32[]{:S(2)}, u32[]{:S(2)}) collective-permute-start(bf16[16,8192]{1,0:T(8,128)(2,1)S(1)} %collective-permute-done.3.refs_3_), channel_id=1, source_target_pairs={{28,0},{29,1},{30,2},{31,3},{0,4},{1,5},{2,6},{3,7},{4,8},{5,9},{6... | collective-permute-start | bytes 786440 | tf_op jit(solution)/shard_map/ppermute | solution.py:243
  28.2 6.9 %collective-permute-start.8 = (bf16[16,8192]{1,0:T(8,128)(2,1)S(1)}, bf16[16,8192]{1,0:T(8,128)(2,1)S(1)}, u32[]{:S(2)}, u32[]{:S(2)}) collective-permute-start(bf16[16,8192]{1,0:T(8,128)(2,1)S(1)} %collective-permute-done.3.refs_3_), channel_id=1, source_target_pairs={{1,0},{2,1},{3,2},{0,3},{5,4},{6,5},{7,6},{4,7},{9,8},{10,9},{11,1... | collective-permute-start | bytes 786440 | tf_op jit(solution)/shard_map/ppermute | solution.py:243
  29.7 7.6 %collective-permute-start.9 = (bf16[16,8192]{1,0:T(8,128)(2,1)S(1)}, bf16[16,8192]{1,0:T(8,128)(2,1)S(1)}, u32[]{:S(2)}, u32[]{:S(2)}) collective-permute-start(bf16[16,8192]{1,0:T(8,128)(2,1)S(1)} %collective-permute-done.3.refs_3_), channel_id=1, source_target_pairs={{3,0},{0,1},{1,2},{2,3},{7,4},{4,5},{5,6},{6,7},{11,8},{8,9},{9,10... | collective-permute-start | bytes 786440 | tf_op jit(solution)/shard_map/ppermute | solution.py:243
  34.2 9.5 %copy-start.1 = (s32[128,8]{0,1:T(8,128)S(1)}, s32[128,8]{0,1:T(8,128)}, u32[]{:S(2)}) copy-start(s32[128,8]{0,1:T(8,128)} %param.9) | copy-start | bytes 12292
  40.4 4.5 %collective-permute-start.10 = (f32[2,64]{1,0:T(2,128)S(1)}, f32[2,64]{1,0:T(2,128)S(1)}, u32[]{:S(2)}, u32[]{:S(2)}) collective-permute-start(f32[2,64]{1,0:T(2,128)S(1)} %get-tuple-element.16.s0), channel_id=1, source_target_pairs={{0,96},{32,64},{64,32},{96,0},{1,97},{33,65},{65,33},{97,1},{2,98}... | collective-permute-start | bytes 1544 | tf_op jit(solution)/shard_map/ppermute | solution.py:261
  40.4 5.2 %collective-permute-start.11 = (f32[2,64]{1,0:T(2,128)S(1)}, f32[2,64]{1,0:T(2,128)S(1)}, u32[]{:S(2)}, u32[]{:S(2)}) collective-permute-start(f32[2,64]{1,0:T(2,128)S(1)} %get-tuple-element.16.s0), channel_id=1, source_target_pairs={{0,64},{64,0},{1,65},{65,1},{2,66},{66,2},{3,67},{67,3},{4,68},{68... | collective-permute-start | bytes 1544 | tf_op jit(solution)/shard_map/ppermute | solution.py:262
  43.5 2.0 %collective-permute-start.12 = (f32[2,64]{1,0:T(2,128)S(1)}, f32[2,64]{1,0:T(2,128)S(1)}, u32[]{:S(2)}, u32[]{:S(2)}) collective-permute-start(f32[2,64]{1,0:T(2,128)S(1)} %get-tuple-element.16.s0), channel_id=1, source_target_pairs={{0,32},{32,0},{1,33},{33,1},{2,34},{34,2},{3,35},{35,3},{4,36},{36... | collective-permute-start | bytes 1544 | tf_op jit(solution)/shard_map/ppermute | solution.py:263
  49.3 3.1 %collective-permute-start.13 = (bf16[128,1024]{1,0:T(8,128)(2,1)S(1)}, bf16[128,1024]{1,0:T(8,128)(2,1)S(1)}, u32[]{:S(2)}, u32[]{:S(2)}) collective-permute-start(bf16[128,1024]{1,0:T(8,128)(2,1)S(1)} %get-tuple-element.18), channel_id=1, source_target_pairs={{0,32},{32,0},{1,33},{33,1},{2,34},{34,2},{3,35},{35,3},{4,36},{36... | collective-permute-start | bytes 786440 | tf_op jit(solution)/shard_map/ppermute | solution.py:266
